TPU v7x, 512 devices: a whole 4x4x16 slice. The times are simulated.
512 devices in a mesh: seq: 8 (over x, core), owner: 64 (over y, z).
Axes of the slice: x: 4, y: 4, z: 16, core: 2. Of those that a mesh axis runs over, the one named last changes fastest.
Arguments:
- queries: bfloat16 [64, 512, 2048], P('owner', 'seq'), may hold values from -16 to 16
- keys: bfloat16 [64, 512, 2048], P('owner', 'seq'), may hold values from -16 to 16
- values: bfloat16 [64, 512, 2048], P('owner', 'seq'), may hold values from -6 to 6
- text_grad: bfloat16 [64, 512, 2048], P('owner', 'seq'), may hold values from -6 to 6
- active: int32 [64, 512], P('owner', 'seq'), may hold values from 0 to 1, as said below
- target: int32 [64, 512], P('owner', 'seq'), may hold values from 0 to 63, as said below
- codes: bfloat16 [64, 472, 8, 1024], P('owner', 'seq'), may hold values from -12 to 12
- depth_cot: bfloat16 [64, 472, 8, 1024], P('owner', 'seq'), may hold values from -6 to 6
- w_in: bfloat16 [2097152], P(('seq', 'owner')), may hold values from -0.125 to 0.125
- norm_gain: bfloat16 [1024], replicated, may hold values from 0.25 to 1.75
- w_qkv: bfloat16 [1572864], P(('seq', 'owner')), may hold values from -4 to 4
- w_out: bfloat16 [524288], P(('seq', 'owner')), may hold values from -0.25 to 0.25
Outputs:
- query_grad: bfloat16 [64, 512, 2048], P('owner', 'seq')
- key_grad: bfloat16 [64, 512, 2048], P('owner', 'seq')
- value_grad: bfloat16 [64, 512, 2048], P('owner', 'seq')
Inputs may be any that keep to these rules, and one draw needn't show every extreme that they name: In every block of 64 positions of a sequence exactly 59 frames are active. For each block of positions, every owner index is the target of exactly 59 active frames; one sequence's block sends at most 2 active frames to one owner, and exactly 2 to some owner. Targets of inactive frames are arbitrary.
All inputs are finite; a program needn't handle non-finite values.
Results may differ from a plain program's by a relative error of at most 0.035.
Values may be sent and summed in bfloat16 or wider, within the bound.
No kernel may reach another device: no remote copies, remote signals or barrier semaphores. Data moves between devices by JAX's collectives and lax.ppermute only.
A program may use at most 128 MiB of HBM per device.

v0:
```python
import jax
import jax.numpy as jnp
from jax import lax
from jax.sharding import PartitionSpec as P

HEADS = 16
HEAD = 128
D_DEP = 1024
DHEADS = 8
DHEAD = 64
CODES = 8
D_CTX = 2048


def attend(query_rows, key_rows, value_rows, offset):
    query_count = query_rows.shape[0]
    key_count = key_rows.shape[0]
    query_heads = query_rows.astype(jnp.float32).reshape(query_count, HEADS, HEAD)
    key_heads = key_rows.astype(jnp.float32).reshape(key_count, HEADS, HEAD)
    value_heads = value_rows.astype(jnp.float32).reshape(key_count, HEADS, HEAD)
    scores = jnp.einsum("qhd,khd->hqk", query_heads, key_heads) * HEAD ** (-0.5)
    query_pos = offset + jnp.arange(query_count, dtype=jnp.int32)
    key_pos = jnp.arange(key_count, dtype=jnp.int32)
    allowed = key_pos[None, None, :] <= query_pos[None, :, None]
    scores = jnp.where(allowed, scores, -1e30)
    weights = jax.nn.softmax(scores, axis=-1).astype(jnp.bfloat16)
    mixed = jnp.einsum("hqk,khd->qhd", weights.astype(jnp.float32), value_heads)
    return mixed.reshape(query_count, HEADS * HEAD)


def depth_layer(frame_rows, code_rows, w_in, norm_gain, w_qkv, w_out):
    hidden = jnp.dot(frame_rows.astype(jnp.float32), w_in.astype(jnp.float32))[
        :, None, :
    ] + code_rows.astype(jnp.float32)
    scale = lax.rsqrt(jnp.mean(hidden * hidden, axis=-1, keepdims=True) + 1e-05)
    normed = (hidden * scale * norm_gain.astype(jnp.float32)).astype(jnp.bfloat16)
    row_count = hidden.shape[0]
    flat = normed.reshape(row_count * CODES, D_DEP)
    projected = jnp.dot(flat.astype(jnp.float32), w_qkv.astype(jnp.float32)).astype(jnp.bfloat16)
    projected = projected.reshape(row_count, CODES, 3, DHEADS, DHEAD).astype(jnp.float32)
    dquery = projected[:, :, 0]
    dkey = projected[:, :, 1]
    dvalue = projected[:, :, 2]
    scores = jnp.einsum("rchd,rkhd->rhck", dquery, dkey) * DHEAD ** (-0.5)
    causal = jnp.arange(CODES)[None, :] <= jnp.arange(CODES)[:, None]
    scores = jnp.where(causal[None, None], scores, -1e30)
    weights = jax.nn.softmax(scores, axis=-1).astype(jnp.bfloat16)
    mixed = jnp.einsum("rhck,rkhd->rchd", weights.astype(jnp.float32), dvalue).astype(jnp.bfloat16)
    mixed = mixed.reshape(row_count * CODES, DHEADS * DHEAD)
    update = jnp.dot(mixed.astype(jnp.float32), w_out.astype(jnp.float32))
    return hidden + update.reshape(hidden.shape)


def depth_grad(frame_rows, code_rows, cot_rows, w_in, norm_gain, w_qkv, w_out):

    def depth_forward(rows_in):
        return depth_layer(rows_in, code_rows, w_in, norm_gain, w_qkv, w_out)

    unused, pull = jax.vjp(depth_forward, frame_rows)
    return pull(cot_rows.astype(jnp.float32))[0]


def shards(
    queries,
    keys,
    values,
    text_grad,
    active,
    target,
    codes,
    depth_cot,
    w_in,
    norm_gain,
    w_qkv,
    w_out,
):
    frame_count = queries.shape[1]
    seq_index = lax.axis_index("seq")
    offset = seq_index * frame_count
    key_rows, value_rows = (
        lax.all_gather(keys[0], "seq", axis=0, tiled=True),
        lax.all_gather(values[0], "seq", axis=0, tiled=True),
    )
    full_in, full_qkv, full_out = (
        lax.all_gather(w_in, ("seq", "owner"), axis=0, tiled=True),
        lax.all_gather(w_qkv, ("seq", "owner"), axis=0, tiled=True),
        lax.all_gather(w_out, ("seq", "owner"), axis=0, tiled=True),
    )
    matrix_in = full_in.reshape(D_CTX, D_DEP)
    matrix_qkv = full_qkv.reshape(D_DEP, 3 * DHEADS * DHEAD)
    matrix_out = full_out.reshape(DHEADS * DHEAD, D_DEP)

    def body_forward(first, second, third):
        return attend(first, second, third, offset)

    primal, pull_attend = jax.vjp(body_forward, queries[0], key_rows, value_rows)
    context = primal.astype(jnp.bfloat16)
    owner_count = lax.axis_size("owner")
    received = codes.shape[1]
    capacity = (received + owner_count - 1) // owner_count + 1
    owner_ids = jnp.arange(owner_count, dtype=jnp.int32)
    matches = ((target[0][:, None] == owner_ids[None, :]) & (active[0][:, None] == 1)).astype(
        jnp.float32
    )
    earlier = jnp.cumsum(matches, axis=0) - matches
    slot_ids = jnp.arange(capacity, dtype=jnp.float32)
    slot_map = matches[:, :, None] * (earlier[:, :, None] == slot_ids[None, None, :]).astype(
        jnp.float32
    )
    picker = slot_map.reshape(frame_count, owner_count * capacity).T.astype(jnp.bfloat16)
    outgoing = jnp.dot(picker, context, preferred_element_type=jnp.float32).astype(jnp.bfloat16)
    outgoing = outgoing.reshape(owner_count, capacity, D_CTX)
    live_flags = jnp.sum(slot_map, axis=0).astype(jnp.bfloat16)
    incoming, live_back = (
        lax.all_to_all(outgoing, "owner", split_axis=0, concat_axis=0, tiled=True),
        lax.all_to_all(live_flags, "owner", split_axis=0, concat_axis=0, tiled=True),
    )
    live_flat = live_back.reshape(-1).astype(jnp.float32)
    ranking = jnp.cumsum(live_flat) - live_flat
    row_ids = jnp.arange(received, dtype=jnp.float32)
    compactor = (
        live_flat[None, :] * (ranking[None, :] == row_ids[:, None]).astype(jnp.float32)
    ).astype(jnp.bfloat16)
    slot_rows = incoming.reshape(owner_count * capacity, D_CTX)
    frame_rows = jnp.dot(compactor, slot_rows, preferred_element_type=jnp.float32).astype(
        jnp.bfloat16
    )
    row_grads = depth_grad(
        frame_rows, codes[0], depth_cot[0], matrix_in, norm_gain, matrix_qkv, matrix_out
    )
    outgrad = jnp.dot(compactor.T, row_grads, preferred_element_type=jnp.float32).astype(
        jnp.bfloat16
    )
    outgrad = outgrad.reshape(owner_count, capacity, D_CTX)
    returned = lax.all_to_all(outgrad, "owner", split_axis=0, concat_axis=0, tiled=True)
    carried = jnp.dot(
        picker.T,
        returned.reshape(owner_count * capacity, D_CTX),
        preferred_element_type=jnp.float32,
    )
    out_grad = (text_grad[0].astype(jnp.float32) + carried).astype(jnp.bfloat16)
    query_grad, key_part, value_part = pull_attend(out_grad.astype(jnp.float32))
    key_sum, value_sum = (
        lax.psum_scatter(
            key_part.astype(jnp.float32).astype(jnp.bfloat16),
            "seq",
            scatter_dimension=0,
            tiled=True,
        ).astype(jnp.float32),
        lax.psum_scatter(
            value_part.astype(jnp.float32).astype(jnp.bfloat16),
            "seq",
            scatter_dimension=0,
            tiled=True,
        ).astype(jnp.float32),
    )
    return (
        query_grad[None],
        key_sum.astype(jnp.bfloat16)[None],
        value_sum.astype(jnp.bfloat16)[None],
    )


def solution(mesh):
    in_specs = (
        P("owner", "seq", None),
        P("owner", "seq", None),
        P("owner", "seq", None),
        P("owner", "seq", None),
        P("owner", "seq"),
        P("owner", "seq"),
        P("owner", "seq", None, None),
        P("owner", "seq", None, None),
        P(("seq", "owner")),
        P(),
        P(("seq", "owner")),
        P(("seq", "owner")),
    )
    out_specs = (P("owner", "seq", None), P("owner", "seq", None), P("owner", "seq", None))
    return jax.shard_map(shards, mesh=mesh, in_specs=in_specs, out_specs=out_specs, check_vma=False)
```

profile of v0, /device:TPU:1, one launch (start us, length us, event | category | flops | bytes accessed | tf_op | source)
XLA Modules:
  0.0 835.4 jit_solution(4414323445456166710)
XLA Ops:
  14.0 19.3 %all-to-all-start = ((bf16[64,1,2]{2,1,0:T(2,128)(2,1)}), bf16[64,1,2]{2,1,0:T(2,128)(2,1)S(1)}, u32[]{:S(2)}, u32[]{:S(2)}) async-start(bf16[64,1,2]{2,1,0:T(2,128)(2,1)} %copy.105), calls=%async_computation | async-start | bytes 65536 | tf_op jit(solution)/shard_map/all_to_all | solution.py:116
  34.7 14.0 %all-gather.14.cloned.1.call-done = bf16[1,512,2048]{2,1,0:T(8,128)(2,1)} async-done(((bf16[1,64,2048]{2,1,0:T(8,128)(2,1)}), bf16[1,512,2048]{2,1,0:T(8,128)(2,1)}) %all-gather.14.cloned.1.call-update) | async-done | bytes 2097168 | tf_op jit(solution)/shard_map/all_gather | solution.py:81
  51.6 32.5 %all-gather.16.cloned.1.call-done = bf16[1,512,2048]{2,1,0:T(8,128)(2,1)} async-done(((bf16[1,64,2048]{2,1,0:T(8,128)(2,1)}), bf16[1,512,2048]{2,1,0:T(8,128)(2,1)}) %all-gather.16.cloned.1.call-update) | async-done | bytes 2097168 | tf_op jit(solution)/shard_map/all_gather | solution.py:82
  84.1 3.9 copy.111
  91.6 3.5 fusion.31
  96.5 15.5 %all-to-all-start.1 = ((bf16[64,2,2048]{2,1,0:T(2,128)(2,1)}), bf16[64,2,2048]{2,1,0:T(2,128)(2,1)S(1)}, u32[]{:S(2)}, u32[]{:S(2)}) async-start(bf16[64,2,2048]{2,1,0:T(2,128)(2,1)} %reshape.419), calls=%async_computation.1 | async-start | bytes 1048576 | tf_op jit(solution)/shard_map/all_to_all | solution.py:115
  112.8 143.9 %all-gather.8.cloned.1.call-done = bf16[524288]{0:T(1024)(128)(2,1)} async-done(((bf16[1024]{0:T(1024)(128)(2,1)}), bf16[524288]{0:T(1024)(128)(2,1)}) %all-gather.8.cloned.1.call-update) | async-done | bytes 1048592 | tf_op jit(solution)/shard_map/all_gather | solution.py:87
  260.6 191.1 %all-gather.12.cloned.1.call-done = bf16[1572864]{0:T(1024)(128)(2,1)} async-done(((bf16[3072]{0:T(1024)(128)(2,1)}), bf16[1572864]{0:T(1024)(128)(2,1)}) %all-gather.12.cloned.1.call-update) | async-done | bytes 3145744 | tf_op jit(solution)/shard_map/all_gather | solution.py:86
  451.7 6.8 reshape.422
  458.5 191.4 %all-gather.10.cloned.1.call-done = bf16[2097152]{0:T(1024)(128)(2,1)} async-done(((bf16[4096]{0:T(1024)(128)(2,1)}), bf16[2097152]{0:T(1024)(128)(2,1)}) %all-gather.10.cloned.1.call-update) | async-done | bytes 4194320 | tf_op jit(solution)/shard_map/all_gather | solution.py:85
  649.9 7.3 reshape.421
  657.2 3.2 fusion.29
  661.6 4.9 convolution_convert_fusion
  666.5 3.6 reshape.423
  672.1 4.4 fusion.86
  687.0 4.5 fusion.19
  694.3 3.8 convolution_convert_fusion.1
  699.5 9.9 %all-to-all-start.2 = ((bf16[64,2,2048]{2,1,0:T(2,128)(2,1)}), bf16[64,2,2048]{2,1,0:T(2,128)(2,1)S(1)}, u32[]{:S(2)}, u32[]{:S(2)}) async-start(bf16[64,2,2048]{2,1,0:T(2,128)(2,1)} %reshape.425), calls=%async_computation.2 | async-start | bytes 1048576 | tf_op jit(solution)/shard_map/all_to_all | solution.py:135
  709.5 30.0 %all-to-all-done.2 = bf16[64,2,2048]{2,1,0:T(2,128)(2,1)S(1)} async-done(((bf16[64,2,2048]{2,1,0:T(2,128)(2,1)}), bf16[64,2,2048]{2,1,0:T(2,128)(2,1)S(1)}, u32[]{:S(2)}, u32[]{:S(2)}) %all-to-all-start.2) | async-done | bytes 524320 | tf_op jit(solution)/shard_map/all_to_all | solution.py:135
  743.2 5.3 convolution_convert_fusion.6
  751.9 3.8 convolution_convert_fusion.5
  759.8 5.2 fusion.32
  766.0 19.1 %reduce-scatter.3.cloned.1.call-done = bf16[64,2048]{1,0:T(8,128)(2,1)} async-done(((bf16[512,2048]{1,0:T(8,128)(2,1)}), bf16[64,2048]{1,0:T(8,128)(2,1)}) %reduce-scatter.3.cloned.1.call-update) | async-done | bytes 262160 | tf_op jit(solution)/shard_map/reduce_scatter | solution.py:144
  785.1 43.5 %reduce-scatter.5.cloned.1.call-done = bf16[64,2048]{1,0:T(8,128)(2,1)} async-done(((bf16[512,2048]{1,0:T(8,128)(2,1)}), bf16[64,2048]{1,0:T(8,128)(2,1)}) %reduce-scatter.5.cloned.1.call-update) | async-done | bytes 262160 | tf_op jit(solution)/shard_map/reduce_scatter | solution.py:150
  (137 shorter events, 50.3 us)
Async XLA Ops:
  7.2 41.5 %all-gather.14.cloned.1.call-start = ((), (), s32[]{:S(2)}) async-start(), calls=%async_computation.10 | async-start | bytes 2359296 | tf_op jit(solution)/shard_map/all_gather | solution.py:81
  7.9 76.2 %all-gather.16.cloned.1.call-start = ((), (), s32[]{:S(2)}) async-start(), calls=%async_computation.11 | async-start | bytes 2359296 | tf_op jit(solution)/shard_map/all_gather | solution.py:82
  8.6 248.1 %all-gather.8.cloned.1.call-start = ((), (), s32[]{:S(2)}) async-start(), calls=%async_computation.5 | async-start | bytes 1050624 | tf_op jit(solution)/shard_map/all_gather | solution.py:87
  9.4 442.4 %all-gather.12.cloned.1.call-start = ((), (), s32[]{:S(2)}) async-start(), calls=%async_computation.7 | async-start | bytes 3151872 | tf_op jit(solution)/shard_map/all_gather | solution.py:86
  10.0 639.9 %all-gather.10.cloned.1.call-start = ((), (), s32[]{:S(2)}) async-start(), calls=%async_computation.6 | async-start | bytes 4202496 | tf_op jit(solution)/shard_map/all_gather | solution.py:85
  14.0 82.6 %all-to-all-start = ((bf16[64,1,2]{2,1,0:T(2,128)(2,1)}), bf16[64,1,2]{2,1,0:T(2,128)(2,1)S(1)}, u32[]{:S(2)}, u32[]{:S(2)}) async-start(bf16[64,1,2]{2,1,0:T(2,128)(2,1)} %copy.105), calls=%async_computation | async-start | bytes 65536 | tf_op jit(solution)/shard_map/all_to_all | solution.py:116
  34.5 56.1 %copy-start.20 = (pred[64,512]{1,0:T(8,128)(4,1)}, pred[64,512]{1,0:T(8,128)(4,1)S(1)}, u32[]{:S(2)}) copy-start(pred[64,512]{1,0:T(8,128)(4,1)S(1)} %iota_compare_fusion) | copy-start | bytes 98308
  34.7 60.4 %copy-start.16 = (bf16[64,128]{0,1:T(8,128)(2,1)}, bf16[64,128]{0,1:T(8,128)(2,1)S(1)}, u32[]{:S(2)}) copy-start(bf16[64,128]{0,1:T(8,128)(2,1)S(1)} %select_convert_fusion) | copy-start | bytes 49156
  51.6 36.4 %copy-start = (bf16[1,512,2048]{1,2,0:T(8,128)(2,1)}, bf16[1,512,2048]{1,2,0:T(8,128)(2,1)S(1)}, u32[]{:S(2)}) copy-start(bf16[1,512,2048]{1,2,0:T(8,128)(2,1)S(1)} %copy.108) | copy-start | bytes 6291460
  90.6 4.5 copy-start.22
  95.1 17.0 %copy-start.27 = (bf16[1024]{0:T(1024)(128)(2,1)S(1)}, bf16[1024]{0:T(1024)(128)(2,1)}, u32[]{:S(2)}) copy-start(bf16[1024]{0:T(1024)(128)(2,1)} %param.21) | copy-start | bytes 6148
  95.4 162.9 %copy-start.12 = (bf16[1,59,8,1024]{3,2,1,0:T(8,128)(2,1)S(1)}, bf16[1,59,8,1024]{3,2,1,0:T(8,128)(2,1)}, u32[]{:S(2)}) copy-start(bf16[1,59,8,1024]{3,2,1,0:T(8,128)(2,1)} %param.19) | copy-start | bytes 2899972
  96.5 163.9 %all-to-all-start.1 = ((bf16[64,2,2048]{2,1,0:T(2,128)(2,1)}), bf16[64,2,2048]{2,1,0:T(2,128)(2,1)S(1)}, u32[]{:S(2)}, u32[]{:S(2)}) async-start(bf16[64,2,2048]{2,1,0:T(2,128)(2,1)} %reshape.419), calls=%async_computation.1 | async-start | bytes 1048576 | tf_op jit(solution)/shard_map/all_to_all | solution.py:115
  112.1 574.9 %copy-start.25 = (f32[1024]{0:T(1024)}, f32[1024]{0:T(1024)S(1)}, u32[]{:S(2)}) copy-start(f32[1024]{0:T(1024)S(1)} %convert_element_type.243) | copy-start | bytes 12292
  112.3 544.9 %copy-start.26 = (f32[128]{0:T(128)}, f32[128]{0:T(128)S(1)}, u32[]{:S(2)}) copy-start(f32[128]{0:T(128)S(1)} %reshape.430) | copy-start | bytes 1540
  112.8 544.4 %copy-start.28 = (f32[128]{0:T(128)}, f32[128]{0:T(128)S(1)}, u32[]{:S(2)}) copy-start(f32[128]{0:T(128)S(1)} %sub.31) | copy-start | bytes 1540
  687.0 5.3 copy-start.6
  687.0 5.3 copy-start.13
  694.3 15.2 %copy-start.23 = (f32[16,64]{1,0:T(8,128)S(1)}, f32[16,64]{1,0:T(8,128)}, u32[]{:S(2)}) copy-start(f32[16,64]{1,0:T(8,128)} %copy-done.22) | copy-start | bytes 12292
  698.1 41.6 %copy-start.17 = (bf16[64,128]{0,1:T(8,128)(2,1)S(1)}, bf16[64,128]{0,1:T(8,128)(2,1)}, u32[]{:S(2)}) copy-start(bf16[64,128]{0,1:T(8,128)(2,1)} %copy-done.16) | copy-start | bytes 49156
  698.1 42.8 %copy-start.4 = (bf16[1,512,2048]{1,2,0:T(8,128)(2,1)S(1)}, bf16[1,512,2048]{1,2,0:T(8,128)(2,1)}, u32[]{:S(2)}) copy-start(bf16[1,512,2048]{1,2,0:T(8,128)(2,1)} %copy.111) | copy-start | bytes 6291460
  699.5 40.0 %all-to-all-start.2 = ((bf16[64,2,2048]{2,1,0:T(2,128)(2,1)}), bf16[64,2,2048]{2,1,0:T(2,128)(2,1)S(1)}, u32[]{:S(2)}, u32[]{:S(2)}) async-start(bf16[64,2,2048]{2,1,0:T(2,128)(2,1)} %reshape.425), calls=%async_computation.2 | async-start | bytes 1048576 | tf_op jit(solution)/shard_map/all_to_all | solution.py:135
  709.4 75.6 %reduce-scatter.3.cloned.1.call-start = ((), (), s32[]{:S(2)}) async-start(), calls=%async_computation.8 | async-start | bytes 2359296 | tf_op jit(solution)/shard_map/reduce_scatter | solution.py:144
  751.0 77.6 %reduce-scatter.5.cloned.1.call-start = ((), (), s32[]{:S(2)}) async-start(), calls=%async_computation.9 | async-start | bytes 2359296 | tf_op jit(solution)/shard_map/reduce_scatter | solution.py:150
  (15 other events, 35.8 us)
Sparse Core Ops, SparseCore 0:
  10.2 38.5 all-gather.13
  50.9 33.1 all-gather.15
  88.7 167.9 all-gather.7
  261.0 190.7 all-gather.11
  456.2 193.6 all-gather.9
  751.1 33.8 reduce-scatter.2
  788.5 40.0 reduce-scatter.4
where the time goes:
time: 838 us; the launch traced here: 835 us
  waiting for transfers between devices  669 us (80%)
  local copies, waits for them, and re-layouts  49.7 us (6%)
  matrix products  49.3 us (6%)
  starting transfers between devices  45 us (5%)
  between operations  14.7 us (2%)
    all_gather x1, waiting for transfers between devices, shards(): lax.all_gather(w_in, ('seq', 'owner'), axis=0, tiled=True)  191 us
    all_gather x1, waiting for transfers between devices, shards(): lax.all_gather(w_qkv, ('seq', 'owner'), axis=0, tiled=True)  191 us
    all_gather x1, waiting for transfers between devices, shards(): lax.all_gather(w_out, ('seq', 'owner'), axis=0, tiled=True)  144 us
    reduce_scatter x1, waiting for transfers between devices, shards(): lax.psum_scatter(value_part.astype(jnp.float32).astype(jnp.bfloat16), 'se...  43.5 us
    all_gather x1, waiting for transfers between devices, shards(): lax.all_gather(values[0], 'seq', axis=0, tiled=True)  32.5 us
    all_to_all x1, waiting for transfers between devices, shards(): lax.all_to_all(outgrad, 'owner', split_axis=0, concat_axis=0, tiled=True)  30 us
    all_to_all x1, starting transfers between devices, shards(): lax.all_to_all(live_flags, 'owner', split_axis=0, concat_axis=0, tiled=True)  19.3 us
    reduce_scatter x1, waiting for transfers between devices, shards(): lax.psum_scatter(key_part.astype(jnp.float32).astype(jnp.bfloat16), 'seq'...  19.1 us
  transfers between devices with their start and end apart: 10, of which 8 were waited for; matrix products, arithmetic and copies ran while one was open for 5% of the time, Pallas kernels for 0%

commit v1 on v0

v1 whole, which is shorter than its diff:
```python
import jax
import jax.numpy as jnp
from jax import lax
from jax.experimental import pallas as pl
from jax.experimental.pallas import tpu as pltpu
from jax.sharding import Mesh
from jax.sharding import PartitionSpec as P

HEADS = 16
HEAD = 128
D_DEP = 1024
DHEADS = 8
DHEAD = 64
CODES = 8
D_CTX = 2048
FRAMES = 64
SEQ = 8
OWNERS = 64
CAP = 2
SLOTS = OWNERS * CAP
RECEIVED = 59
LENGTH = SEQ * FRAMES
COLS = D_CTX // SEQ
ROWS = RECEIVED * CODES
PADDED = 512
CHUNK = 256
GROUP = 128
EMPTY = 2.0**100
BF = jnp.bfloat16
F32 = jnp.float32


def dot(a, b):
    return jnp.dot(a, b, preferred_element_type=F32)


def dot_nt(a, b):
    return lax.dot_general(a, b, (((1,), (1,)), ((), ())), preferred_element_type=F32)


def dot_tn(a, b):
    return lax.dot_general(a, b, (((0,), (0,)), ((), ())), preferred_element_type=F32)


def iota(shape, axis):
    return lax.broadcasted_iota(jnp.int32, shape, axis)


def call(kernel, out_shape, name, **options):
    limit = options.pop("vmem", 32)
    return pl.pallas_call(
        kernel,
        out_shape=out_shape,
        name=name,
        compiler_params=pltpu.CompilerParams(vmem_limit_bytes=limit * 2**20),
        **options,
    )


def weight_kernel(gathered_ref, out_ref):
    row = iota((512, 512), 0)
    col = iota((512, 512), 1)
    none = jnp.full((512, 512), -1, jnp.int32)

    def pick(first, second, third, fourth):
        source = jnp.where(
            row < 256, first, jnp.where(row < 384, second, jnp.where(row < 448, third, fourth))
        )
        return (col == source).astype(F32).astype(BF)

    in_row = ((row >> 2) << 3) + (row & 3)
    wide = row - 256
    wide_base = (wide >> 1) << 3
    wide_odd = (wide & 1) == 1
    tail = row - 384
    tail_base = (tail >> 1) << 3
    tail_odd = (tail & 1) == 1
    out_row = ((row - 448) << 3) + 7
    left_left = pick(
        in_row,
        jnp.where(wide_odd, none, wide_base + 4),
        jnp.where(tail_odd, none, tail_base + 5),
        out_row,
    )
    left_right = pick(
        none, jnp.where(wide_odd, wide_base + 5, none), jnp.where(tail_odd, tail_base + 6, none), none
    )
    right_left = pick(
        none,
        jnp.where(wide_odd, wide_base + 6, none),
        jnp.where(tail_odd, none, tail_base + 256 + 5),
        none,
    )
    right_right = pick(
        in_row,
        jnp.where(wide_odd, none, wide_base + 4),
        jnp.where(tail_odd, tail_base + 256 + 6, none),
        out_row,
    )
    left = gathered_ref[:, :512]
    right = gathered_ref[:, 512:]
    out_ref[:, :512] = (dot(left_left, left) + dot(left_right, right)).astype(BF)
    out_ref[:, 512:] = (dot(right_left, left) + dot(right_right, right)).astype(BF)


def pack_kernel(first_ref, second_ref, third_ref, out_ref):
    for part in range(SEQ):
        for place, ref in enumerate((first_ref, second_ref, third_ref)):
            out_ref[part, :, place * COLS : (place + 1) * COLS] = ref[
                :, part * COLS : (part + 1) * COLS
            ]


def unpack_kernel(packed_ref, first_ref, second_ref, third_ref):
    for part in range(SEQ):
        for place, ref in enumerate((first_ref, second_ref, third_ref)):
            ref[:, part * COLS : (part + 1) * COLS] = packed_ref[
                part, :, place * COLS : (place + 1) * COLS
            ]


def head_weights(packed_ref, head):
    base = head * HEAD
    query = packed_ref[:, base : base + HEAD]
    key = packed_ref[:, COLS + base : COLS + base + HEAD]
    value = packed_ref[:, 2 * COLS + base : 2 * COLS + base + HEAD]
    scores = dot_nt(query, key) * HEAD ** (-0.5)
    allowed = iota((LENGTH, LENGTH), 1) <= iota((LENGTH, LENGTH), 0)
    scores = jnp.where(allowed, scores, -1e30)
    raised = jnp.exp(scores - jnp.max(scores, axis=1, keepdims=True))
    weights = raised * (1.0 / jnp.sum(raised, axis=1, keepdims=True))
    return query, key, value, weights


def forward_kernel(packed_ref, w_in_ref, out_ref):
    total = None
    for head in range(2):
        unused_q, unused_k, value, weights = head_weights(packed_ref, head)
        context = dot(weights.astype(BF), value).astype(BF)
        part = dot(context, w_in_ref[head * HEAD : (head + 1) * HEAD, :])
        total = part if total is None else total + part
    out_ref[...] = total.astype(BF)


def backward_kernel(packed_ref, grad_ref, out_ref):
    for head in range(2):
        base = head * HEAD
        query, key, value, weights = head_weights(packed_ref, head)
        grad = grad_ref[:, base : base + HEAD]
        weight_grad = dot_nt(grad, value).astype(BF).astype(F32)
        inner = jnp.sum(weight_grad * weights, axis=1, keepdims=True)
        score_grad = (weights * (weight_grad - inner) * HEAD ** (-0.5)).astype(BF)
        out_ref[:, base : base + HEAD] = dot(score_grad, key).astype(BF)
        out_ref[:, COLS + base : COLS + base + HEAD] = dot_tn(score_grad, query).astype(BF)
        out_ref[:, 2 * COLS + base : 2 * COLS + base + HEAD] = dot_tn(
            weights.astype(BF), grad
        ).astype(BF)


def routing(target_ref, active_ref):
    down = iota((FRAMES, FRAMES), 0)
    across = iota((FRAMES, FRAMES), 1)
    target_row = target_ref[...].astype(F32)
    live_row = (active_ref[...] == 1).astype(F32)
    target_col = jnp.sum(jnp.where(down == across, target_row, 0.0), axis=1, keepdims=True)
    live_col = jnp.sum(jnp.where(down == across, live_row, 0.0), axis=1, keepdims=True)
    same = target_col == target_row
    earlier_row = jnp.sum(jnp.where(same & (down < across), live_col, 0.0), axis=0, keepdims=True)
    earlier_col = jnp.sum(jnp.where(same & (across < down), live_row, 0.0), axis=1, keepdims=True)
    return (target_row, live_row, earlier_row), (target_col, live_col, earlier_col)


def send_kernel(parts_ref, target_ref, active_ref, out_ref):
    rows = parts_ref[0].astype(F32)
    for part in range(1, SEQ):
        rows = rows + parts_ref[part].astype(F32)
    (target, live, earlier), unused = routing(target_ref, active_ref)
    slot = iota((SLOTS, FRAMES), 0)
    chosen = (
        (target == (slot >> 1).astype(F32)) & (live > 0.5) & (earlier == (slot & 1).astype(F32))
    ).astype(F32)
    sent = dot(chosen.astype(BF), rows.astype(BF))
    filled = jnp.sum(chosen, axis=1, keepdims=True) > 0.5
    out_ref[...] = jnp.where(filled, sent, EMPTY).astype(BF)


def return_kernel(returned_ref, target_ref, active_ref, text_ref, w_in_ref, out_ref, rows_ref):
    @pl.when(pl.program_id(0) == 0)
    def _():
        unused, (target, live, earlier) = routing(target_ref, active_ref)
        slot = iota((FRAMES, SLOTS), 1)
        chosen = (
            (target == (slot >> 1).astype(F32)) & (live > 0.5) & (earlier == (slot & 1).astype(F32))
        ).astype(F32)
        rows_ref[...] = dot(chosen.astype(BF), returned_ref[...]).astype(BF)

    carried = dot_nt(rows_ref[...], w_in_ref[0]).astype(BF).astype(F32)
    out_ref[0] = (text_ref[...].astype(F32) + carried).astype(BF)


def depth_kernel(
    slots_ref,
    codes_ref,
    cot_ref,
    gain_ref,
    weights_ref,
    out_ref,
    w_qkv,
    w_out,
    hidden_s,
    cot_s,
    grads_s,
    frames_s,
    sems,
):
    copies = []
    for part in range(SEQ):
        low = part * 128
        pairs = (
            (weights_ref.at[part, 256:384, :], w_qkv.at[low : low + 128, :1024]),
            (weights_ref.at[part, 384:448, :512], w_qkv.at[low : low + 64, 1024:]),
            (weights_ref.at[part, 384:448, 512:], w_qkv.at[low + 64 : low + 128, 1024:]),
            (weights_ref.at[part, 448:512, :], w_out.at[part * 64 : part * 64 + 64, :]),
        )
        for source, goal in pairs:
            copies.append(pltpu.make_async_copy(source, goal, sems.at[len(copies)]))
    for copy in copies:
        copy.start()

    slots = slots_ref[...]
    live_col = (slots[:, 0:1].astype(F32) < EMPTY * 0.5).astype(F32)
    down = iota((SLOTS, SLOTS), 0)
    across = iota((SLOTS, SLOTS), 1)
    live_row = jnp.sum(jnp.where(down == across, live_col, 0.0), axis=0, keepdims=True)
    rank_row = jnp.sum(jnp.where(down < across, live_col, 0.0), axis=0, keepdims=True)
    rank_col = jnp.sum(jnp.where(across < down, live_row, 0.0), axis=1, keepdims=True)

    spread = (
        (live_row > 0.5) & (rank_row == (iota((PADDED, SLOTS), 0) >> 3).astype(F32))
    ).astype(F32)
    spare = jnp.zeros((PADDED - ROWS, D_DEP), F32)
    hidden_s[...] = dot(spread.astype(BF), slots) + jnp.concatenate(
        [codes_ref[...].astype(F32), spare], axis=0
    )
    cot_s[...] = jnp.concatenate([cot_ref[...].astype(F32), spare], axis=0)
    gain = gain_ref[...].astype(F32)
    for copy in copies:
        copy.wait()

    row = iota((GROUP, GROUP), 0)
    col = iota((GROUP, GROUP), 1)
    allowed = ((row >> 3) == (col >> 3)) & (col <= row)
    first_half = iota((GROUP, GROUP), 1) < DHEAD
    nothing = jnp.zeros((GROUP, GROUP), BF)
    width = DHEADS * DHEAD
    for chunk in range(PADDED // CHUNK):
        low = chunk * CHUNK
        hidden = hidden_s[low : low + CHUNK, :]
        cot = cot_s[low : low + CHUNK, :]
        scale = lax.rsqrt(jnp.sum(hidden * hidden, axis=1, keepdims=True) * (1.0 / D_DEP) + 1e-05)
        normed = (hidden * scale * gain).astype(BF)
        projected = dot(normed, w_qkv[...]).astype(BF)
        mixed_grad = dot_nt(cot.astype(BF), w_out[...]).astype(BF)
        for group in range(CHUNK // GROUP):
            rows = slice(group * GROUP, (group + 1) * GROUP)
            for pair in range(DHEADS // 2):
                lanes = pair * 128
                query = projected[rows, lanes : lanes + 128]
                key = projected[rows, width + lanes : width + lanes + 128]
                value = projected[rows, 2 * width + lanes : 2 * width + lanes + 128]
                grad = mixed_grad[rows, lanes : lanes + 128]
                totals = [None, None, None]
                for half in range(2):
                    own = first_half if half == 0 else ~first_half
                    own_query = jnp.where(own, query, nothing)
                    own_key = jnp.where(own, key, nothing)
                    own_grad = jnp.where(own, grad, nothing)
                    scores = dot_nt(own_query, key) * DHEAD ** (-0.5)
                    scores = jnp.where(allowed, scores, -1e30)
                    raised = jnp.exp(scores - jnp.max(scores, axis=1, keepdims=True))
                    weights = raised * (1.0 / jnp.sum(raised, axis=1, keepdims=True))
                    weight_grad = dot_nt(own_grad, value).astype(BF).astype(F32)
                    inner = jnp.sum(weight_grad * weights, axis=1, keepdims=True)
                    score_grad = (weights * (weight_grad - inner) * DHEAD ** (-0.5)).astype(BF)
                    terms = (
                        dot(score_grad, own_key),
                        dot_tn(score_grad, own_query),
                        dot_tn(weights.astype(BF), own_grad),
                    )
                    totals = [t if s is None else s + t for s, t in zip(totals, terms)]
                for place, total in enumerate(totals):
                    start = place * width + lanes
                    grads_s[rows, start : start + 128] = total.astype(BF)
        normed_grad = dot_nt(grads_s[...], w_qkv[...]).astype(BF).astype(F32) * gain
        inner = jnp.sum(normed_grad * hidden, axis=1, keepdims=True) * (1.0 / D_DEP)
        hidden_grad = cot + scale * normed_grad - hidden * (scale * scale * scale * inner)
        frames = jnp.sum(hidden_grad.reshape(CHUNK // CODES, CODES, D_DEP), axis=1)
        frames_s[low // CODES : (low + CHUNK) // CODES, :] = frames

    back = ((live_col > 0.5) & (rank_col == iota((SLOTS, FRAMES), 1).astype(F32))).astype(F32)
    out_ref[...] = dot(back.astype(BF), frames_s[...].astype(BF)).astype(BF)


def exchange(array, axis):
    return lax.all_to_all(array, axis, split_axis=0, concat_axis=0, tiled=True)


def shards(
    queries,
    keys,
    values,
    text_grad,
    active,
    target,
    codes,
    depth_cot,
    w_in,
    norm_gain,
    w_qkv,
    w_out,
):
    owner = ("y", "z")
    mine = jnp.concatenate([w_in, w_qkv, w_out]).reshape(1, 8, D_DEP)
    along_z = exchange(jnp.broadcast_to(mine, (16, 8, D_DEP)), "z")
    along_y = exchange(jnp.broadcast_to(along_z.reshape(1, 128, D_DEP), (4, 128, D_DEP)), "y")
    own_weights = call(weight_kernel, jax.ShapeDtypeStruct((512, D_DEP), BF), "sort_weights")(
        along_y.reshape(512, D_DEP)
    )
    all_weights = lax.all_gather(own_weights, "seq", axis=0, tiled=True).reshape(SEQ, 512, D_DEP)

    packed = call(pack_kernel, jax.ShapeDtypeStruct((SEQ, FRAMES, 3 * COLS), BF), "pack_qkv")(
        queries[0], keys[0], values[0]
    )
    packed = exchange(packed, "seq").reshape(LENGTH, 3 * COLS)
    parts = call(
        forward_kernel,
        jax.ShapeDtypeStruct((LENGTH, D_DEP), BF),
        "attention_forward",
        grid=(1,),
        in_specs=[
            pl.BlockSpec((LENGTH, 3 * COLS), lambda i: (0, 0)),
            pl.BlockSpec((COLS, D_DEP), lambda i: (0, 0)),
        ],
        out_specs=pl.BlockSpec((LENGTH, D_DEP), lambda i: (0, 0)),
    )(packed, own_weights)
    parts = exchange(parts.reshape(SEQ, FRAMES, D_DEP), "seq")
    sent = call(send_kernel, jax.ShapeDtypeStruct((SLOTS, D_DEP), BF), "send_rows")(
        parts, target, active
    )
    slots = exchange(sent.reshape(OWNERS, CAP, D_DEP), owner).reshape(SLOTS, D_DEP)
    vmem = pl.BlockSpec(memory_space=pltpu.VMEM)
    grads = call(
        depth_kernel,
        jax.ShapeDtypeStruct((SLOTS, D_DEP), BF),
        "depth_layer",
        in_specs=[vmem, vmem, vmem, vmem, pl.BlockSpec(memory_space=pl.ANY)],
        out_specs=vmem,
        scratch_shapes=[
            pltpu.VMEM((D_DEP, 3 * DHEADS * DHEAD), BF),
            pltpu.VMEM((DHEADS * DHEAD, D_DEP), BF),
            pltpu.VMEM((PADDED, D_DEP), F32),
            pltpu.VMEM((PADDED, D_DEP), F32),
            pltpu.VMEM((CHUNK, 3 * DHEADS * DHEAD), BF),
            pltpu.VMEM((FRAMES, D_DEP), F32),
            pltpu.SemaphoreType.DMA((4 * SEQ,)),
        ],
        vmem=48,
    )(
        slots,
        codes.reshape(ROWS, D_DEP),
        depth_cot.reshape(ROWS, D_DEP),
        norm_gain.reshape(1, D_DEP),
        all_weights,
    )
    returned = exchange(grads.reshape(OWNERS, CAP, D_DEP), owner).reshape(SLOTS, D_DEP)
    out_grad = call(
        return_kernel,
        jax.ShapeDtypeStruct((SEQ, FRAMES, COLS), BF),
        "return_rows",
        grid=(SEQ,),
        in_specs=[
            pl.BlockSpec((SLOTS, D_DEP), lambda i: (0, 0)),
            pl.BlockSpec((1, FRAMES), lambda i: (0, 0)),
            pl.BlockSpec((1, FRAMES), lambda i: (0, 0)),
            pl.BlockSpec((FRAMES, COLS), lambda i: (0, i)),
            pl.BlockSpec((1, COLS, D_DEP), lambda i: (i, 0, 0)),
        ],
        out_specs=pl.BlockSpec((1, FRAMES, COLS), lambda i: (i, 0, 0)),
        scratch_shapes=[pltpu.VMEM((FRAMES, D_DEP), BF)],
    )(returned, target, active, text_grad[0], all_weights)
    out_grad = exchange(out_grad, "seq").reshape(LENGTH, COLS)
    grads = call(
        backward_kernel, jax.ShapeDtypeStruct((LENGTH, 3 * COLS), BF), "attention_backward"
    )(packed, out_grad)
    grads = exchange(grads.reshape(SEQ, FRAMES, 3 * COLS), "seq")
    shape = jax.ShapeDtypeStruct((FRAMES, D_CTX), BF)
    query_grad, key_grad, value_grad = call(unpack_kernel, (shape, shape, shape), "unpack_grads")(grads)
    return query_grad[None], key_grad[None], value_grad[None]


def solution(mesh):
    split = Mesh(mesh.devices.reshape(SEQ, 4, 16), ("seq", "y", "z"))
    rows = P(("y", "z"), "seq", None)
    frames = P(("y", "z"), "seq")
    code_rows = P(("y", "z"), "seq", None, None)
    flat = P(("seq", "y", "z"))
    in_specs = (
        rows,
        rows,
        rows,
        rows,
        frames,
        frames,
        code_rows,
        code_rows,
        flat,
        P(),
        flat,
        flat,
    )
    return jax.shard_map(
        shards, mesh=split, in_specs=in_specs, out_specs=(rows, rows, rows), check_vma=False
    )
```

time: 838 us -> 232 us (0.28)
  waiting for transfers between devices: 669 us -> 18.6 us
  blocking collectives: 0 us -> 152 us
  matrix products: 49.3 us -> 0 us
  local copies, waits for them, and re-layouts: 49.7 us -> 7.51 us
  starting transfers between devices: 45 us -> 11 us
  Pallas kernels: 0 us -> 27.3 us
    all_gather x5 -> x1, waiting for transfers between devices: 573 us -> 0.02 us  [shards(): lax.all_gather(own_weights, 'seq', axis=0, tiled=True)]
    all_to_all x0 -> x7, blocking collectives: none -> 152 us  [exchange(): return lax.all_to_all(array, axis, split_axis=0, concat_axis=0, tiled=True)]
    reduce_scatter x2 -> x0, waiting for transfers between devices: 62.6 us -> none  [the longest x1 43.5 us: shards(): lax.psum_scatter(value_part.astype(jnp.float32).astype(jnp.bfloat16), 'se...]
    dot_general x17 -> x0, matrix products: 44.9 us -> none  [the longest x3 10.9 us: attend(): scores = jnp.einsum('qhd,khd->hqk', query_heads, key_heads) * HEAD ** (-0.5)]
    all_to_all x3 -> x1, starting transfers between devices: 44.7 us -> 11 us  [exchange(): return lax.all_to_all(array, axis, split_axis=0, concat_axis=0, tiled=True)]
    pallas_call x0 -> x8, Pallas kernels: none -> 27.3 us  [the longest x1 15.4 us: shards(): call(depth_kernel, jax.ShapeDtypeStruct((SLOTS, D_DEP), BF), 'depth_layer...]
    reshape x10 -> x5, local copies, waits for them, and re-layouts: 26.5 us -> 1.11 us  [the longest x1 0.8 us: shards(): sent.reshape(OWNERS, CAP, D_DEP)]
    all_to_all x3 -> x1, waiting for transfers between devices: 30 us -> 18.5 us  [exchange(): return lax.all_to_all(array, axis, split_axis=0, concat_axis=0, tiled=True)]
  transfers between devices with their start and end apart: 10 -> 2, of which waited for: 8 -> 1; matrix products, arithmetic and copies ran while one was open for 5% -> 0% of each run, Pallas kernels for 0% -> 2%
where the time goes in v1:
time: 232 us
  blocking collectives  152 us (66%)
  Pallas kernels  27.3 us (12%)
  waiting for transfers between devices  18.6 us (8%)
  between operations  14.2 us (6%)
  starting transfers between devices  11 us (5%)
  local copies, waits for them, and re-layouts  7.51 us (3%)
    all_to_all x7, blocking collectives, exchange(): return lax.all_to_all(array, axis, split_axis=0, concat_axis=0, tiled=True)  152 us
    all_to_all x1, waiting for transfers between devices, exchange(): return lax.all_to_all(array, axis, split_axis=0, concat_axis=0, tiled=True)  18.5 us
    pallas_call x1, Pallas kernels, shards(): call(depth_kernel, jax.ShapeDtypeStruct((SLOTS, D_DEP), BF), 'depth_layer...  15.4 us
    all_to_all x1, starting transfers between devices, exchange(): return lax.all_to_all(array, axis, split_axis=0, concat_axis=0, tiled=True)  11 us
    unnamed x20, local copies, waits for them, and re-layouts  6.25 us
  transfers between devices with their start and end apart: 2, of which 1 were waited for; matrix products, arithmetic and copies ran while one was open for 0% of the time, Pallas kernels for 2%

profile of v1, /device:TPU:1, one launch (start us, length us, event | category | flops | bytes accessed | tf_op | source)
XLA Modules:
  0.0 231.5 jit_solution(17067252359219742)
XLA Ops:
  7.2 0.7 pad_maximum_fusion
  8.0 28.7 %all_to_all.40 = bf16[16,8,1024]{2,1,0:T(8,128)(2,1)S(1)} all-to-all(bf16[16,8,1024]{2,1,0:T(8,128)(2,1)S(1)} %broadcast_in_dim.24), channel_id=1, replica_groups=mesh['seq'=8,'y'=4,'z'=16] {'z'}, dimensions={0} | all-to-all | bytes 524288 | tf_op jit(solution)/shard_map/all_to_all | solution.py:305
  36.7 0.1 broadcast_in_dim.26
  36.8 13.9 %all_to_all.41 = bf16[4,128,1024]{2,1,0:T(8,128)(2,1)S(1)} all-to-all(bf16[4,128,1024]{2,1,0:T(8,128)(2,1)S(1)} %broadcast_in_dim.26), channel_id=1, replica_groups=mesh['seq'=8,'y'=4,'z'=16] {'y'}, dimensions={0} | all-to-all | bytes 2097152 | tf_op jit(solution)/shard_map/all_to_all | solution.py:305
  50.7 2.3 %sort_weights.1.w_in_ref = bf16[512,1024]{1,0:T(8,128)(2,1)} custom-call(bf16[512,1024]{1,0:T(8,128)(2,1)S(1)} %bitcast.20), custom_call_target="tpu_custom_call" | custom-call | tf_op jit(solution)/shard_map/sort_weights/pallas_call | solution.py:326
  53.1 0.9 copy-done.4
  54.0 0.9 copy-done.5
  54.9 0.9 copy-done.6
  56.0 24.4 %all_to_all.42 = bf16[8,64,768]{2,1,0:T(8,128)(2,1)S(1)} all-to-all(bf16[8,64,768]{2,1,0:T(8,128)(2,1)S(1)} %pack_qkv.1), channel_id=1, replica_groups=mesh['seq'=8,'y'=4,'z'=16] {'seq'}, dimensions={0} | all-to-all | bytes 1572864 | tf_op jit(solution)/shard_map/all_to_all | solution.py:305
  80.3 3.1 %attention_forward.1 = bf16[512,1024]{1,0:T(8,128)(2,1)S(1)} custom-call(bf16[512,768]{1,0:T(8,128)(2,1)S(1)} %bitcast.18, bf16[512,1024]{1,0:T(8,128)(2,1)} %sort_weights.1.w_in_ref), custom_call_target="tpu_custom_call" | custom-call | tf_op jit(solution)/shard_map/attention_forward/pallas_call | solution.py:335
  83.5 30.9 %all_to_all.43.parts_ref = bf16[8,64,1024]{2,1,0:T(8,128)(2,1)S(1)} all-to-all(bf16[8,64,1024]{2,1,0:T(8,128)(2,1)S(1)} %bitcast.21), channel_id=1, replica_groups=mesh['seq'=8,'y'=4,'z'=16] {'seq'}, dimensions={0} | all-to-all | bytes 2097152 | tf_op jit(solution)/shard_map/all_to_all | solution.py:305
  114.3 0.3 send_rows.1
  114.7 0.8 reshape.52
  115.5 11.0 %all-to-all-start.4 = ((bf16[64,2,1024]{2,1,0:T(2,128)(2,1)}), bf16[64,2,1024]{2,1,0:T(2,128)(2,1)S(1)}, u32[]{:S(2)}, u32[]{:S(2)}) async-start(bf16[64,2,1024]{2,1,0:T(2,128)(2,1)} %reshape.52), calls=%async_computation.4 | async-start | bytes 524288 | tf_op jit(solution)/shard_map/all_to_all | solution.py:305
  126.5 18.5 %all-to-all-done.4 = bf16[64,2,1024]{2,1,0:T(2,128)(2,1)S(1)} async-done(((bf16[64,2,1024]{2,1,0:T(2,128)(2,1)}), bf16[64,2,1024]{2,1,0:T(2,128)(2,1)S(1)}, u32[]{:S(2)}, u32[]{:S(2)}) %all-to-all-start.4) | async-done | bytes 262176 | tf_op jit(solution)/shard_map/all_to_all | solution.py:305
  145.2 15.4 %depth_layer.1 = bf16[128,1024]{1,0:T(8,128)(2,1)S(1)} custom-call(bf16[128,1024]{1,0:T(8,128)(2,1)S(1)} %reshape.53.slots_ref, bf16[472,1024]{1,0:T(8,128)(2,1)S(1)} %bitcast.24, bf16[472,1024]{1,0:T(8,128)(2,1)S(1)} %bitcast.25, bf16[1,1024]{1,0:T(2,128)(2,1)S(1)} %reshape.56.gain_ref, bf16[8,512,1024]{2,1,0:T(8,128)(2,1)} %bitcast.16), custom_call_target="tpu_custom_call" | custom-call | tf_op jit(solution)/shard_map/depth_layer/pallas_call | solution.py:352
  160.7 0.1 reshape.58
  160.8 26.0 %all_to_all.44 = bf16[64,2,1024]{2,1,0:T(2,128)(2,1)S(1)} all-to-all(bf16[64,2,1024]{2,1,0:T(2,128)(2,1)S(1)} %reshape.58), channel_id=1, replica_groups=mesh['seq'=8,'y'=4,'z'=16] {'y','z'}, dimensions={0} | all-to-all | bytes 524288 | tf_op jit(solution)/shard_map/all_to_all | solution.py:305
  187.0 3.4 %copy-done = bf16[4096,1024]{1,0:T(8,128)(2,1)S(1)} copy-done((bf16[4096,1024]{1,0:T(8,128)(2,1)S(1)}, bf16[4096,1024]{1,0:T(8,128)(2,1)}, u32[]{:S(2)}) %copy-start) | copy-done | bytes 8388632
  190.3 2.7 %return_rows.1 = bf16[8,64,256]{2,1,0:T(8,128)(2,1)S(1)} custom-call(bf16[128,1024]{1,0:T(8,128)(2,1)S(1)} %reshape.59.returned_ref, s32[1,64]{1,0:T(1,128)S(1)} %copy-done.7, s32[1,64]{1,0:T(1,128)S(1)} %copy-done.8, bf16[64,2048]{1,0:T(8,128)(2,1)S(1)} %bitcast.26, bf16[8,512,1024]{2,1,0:T(8,128)(2,1)S(1)} %bitcast.17), custom_call_target="tpu_custom_call" | custom-call | tf_op jit(solution)/shard_map/return_rows/pallas_call | solution.py:376
  193.1 12.6 %all_to_all.45 = bf16[8,64,256]{2,1,0:T(8,128)(2,1)S(1)} all-to-all(bf16[8,64,256]{2,1,0:T(8,128)(2,1)S(1)} %return_rows.1), channel_id=1, replica_groups=mesh['seq'=8,'y'=4,'z'=16] {'seq'}, dimensions={0} | all-to-all | bytes 524288 | tf_op jit(solution)/shard_map/all_to_all | solution.py:305
  205.7 2.4 %attention_backward.1 = bf16[512,768]{1,0:T(8,128)(2,1)S(1)} custom-call(bf16[512,768]{1,0:T(8,128)(2,1)S(1)} %bitcast.19, bf16[512,256]{1,0:T(8,128)(2,1)S(1)} %bitcast.23), custom_call_target="tpu_custom_call" | custom-call | tf_op jit(solution)/shard_map/attention_backward/pallas_call | solution.py:392
  208.1 15.7 %all_to_all.46.packed_ref = bf16[8,64,768]{2,1,0:T(8,128)(2,1)S(1)} all-to-all(bf16[8,64,768]{2,1,0:T(8,128)(2,1)S(1)} %bitcast.22), channel_id=1, replica_groups=mesh['seq'=8,'y'=4,'z'=16] {'seq'}, dimensions={0} | all-to-all | bytes 1572864 | tf_op jit(solution)/shard_map/all_to_all | solution.py:305
  223.7 0.9 unpack_grads.1
  (25 shorter events, 0.4 us)
Async XLA Ops:
  7.2 107.2 %copy-start.8 = (s32[1,64]{1,0:T(1,128)S(1)}, s32[1,64]{1,0:T(1,128)}, u32[]{:S(2)}) copy-start(s32[1,64]{1,0:T(1,128)} %active_ref.3) | copy-start | bytes 772
  7.2 107.2 %copy-start.7 = (s32[1,64]{1,0:T(1,128)S(1)}, s32[1,64]{1,0:T(1,128)}, u32[]{:S(2)}) copy-start(s32[1,64]{1,0:T(1,128)} %target_ref.3) | copy-start | bytes 772
  7.2 138.0 %all-gather.2.cloned.1.call-start = ((), (), s32[]{:S(2)}) async-start(), calls=%async_computation.8 | async-start | bytes 9437184 | tf_op jit(solution)/shard_map/all_gather | solution.py:329
  36.7 89.8 %copy-start.9 = (bf16[1024]{0:T(1024)(128)(2,1)S(1)}, bf16[1024]{0:T(1024)(128)(2,1)}, u32[]{:S(2)}) copy-start(bf16[1024]{0:T(1024)(128)(2,1)} %param.21) | copy-start | bytes 6148
  36.8 108.4 %copy-start.1 = (bf16[1,59,8,1024]{3,2,1,0:T(8,128)(2,1)S(1)}, bf16[1,59,8,1024]{3,2,1,0:T(8,128)(2,1)}, u32[]{:S(2)}) copy-start(bf16[1,59,8,1024]{3,2,1,0:T(8,128)(2,1)} %param.18) | copy-start | bytes 2899972
  36.8 108.4 %copy-start.2 = (bf16[1,59,8,1024]{3,2,1,0:T(8,128)(2,1)S(1)}, bf16[1,59,8,1024]{3,2,1,0:T(8,128)(2,1)}, u32[]{:S(2)}) copy-start(bf16[1,59,8,1024]{3,2,1,0:T(8,128)(2,1)} %param.19) | copy-start | bytes 2899972
  53.0 1.0 copy-start.4
  54.0 0.9 copy-start.5
  54.9 0.9 copy-start.6
  83.4 103.5 %copy-start.3 = (bf16[1,64,2048]{2,1,0:T(8,128)(2,1)S(1)}, bf16[1,64,2048]{2,1,0:T(8,128)(2,1)}, u32[]{:S(2)}) copy-start(bf16[1,64,2048]{2,1,0:T(8,128)(2,1)} %param.15) | copy-start | bytes 786436
  115.5 29.6 %all-to-all-start.4 = ((bf16[64,2,1024]{2,1,0:T(2,128)(2,1)}), bf16[64,2,1024]{2,1,0:T(2,128)(2,1)S(1)}, u32[]{:S(2)}, u32[]{:S(2)}) async-start(bf16[64,2,1024]{2,1,0:T(2,128)(2,1)} %reshape.52), calls=%async_computation.4 | async-start | bytes 524288 | tf_op jit(solution)/shard_map/all_to_all | solution.py:305
  187.0 3.4 %copy-start = (bf16[4096,1024]{1,0:T(8,128)(2,1)S(1)}, bf16[4096,1024]{1,0:T(8,128)(2,1)}, u32[]{:S(2)}) copy-start(bf16[4096,1024]{1,0:T(8,128)(2,1)} %all-gather.2.cloned.1.call-done) | copy-start | bytes 25165828
Sparse Core Ops, SparseCore 0:
  53.2 74.1 all-gather.1

commit v2 on v1

--- a/solution.py
+++ b/solution.py
@@ -26,6 +26,7 @@
 CHUNK = 256
 GROUP = 128
 EMPTY = 2.0**100
+SHIFTS = (0, 1, 3, 2)
 BF = jnp.bfloat16
 F32 = jnp.float32
 
@@ -57,7 +58,12 @@
     )
 
 
-def weight_kernel(gathered_ref, out_ref):
+def weight_kernel(*refs):
+    pieces, in_ref, rest_ref, gathered_ref = refs[:4], refs[4], refs[5], refs[6]
+    here = lax.axis_index("y")
+    for shift, piece in zip(SHIFTS, pieces):
+        start = pl.multiple_of(((here + 4 - shift) & 3) * 128, 128)
+        gathered_ref[pl.ds(start, 128), :] = piece[...]
     row = iota((512, 512), 0)
     col = iota((512, 512), 1)
     none = jnp.full((512, 512), -1, jnp.int32)
@@ -99,8 +105,11 @@
     )
     left = gathered_ref[:, :512]
     right = gathered_ref[:, 512:]
-    out_ref[:, :512] = (dot(left_left, left) + dot(left_right, right)).astype(BF)
-    out_ref[:, 512:] = (dot(right_left, left) + dot(right_right, right)).astype(BF)
+    new_left = (dot(left_left, left) + dot(left_right, right)).astype(BF)
+    new_right = (dot(right_left, left) + dot(right_right, right)).astype(BF)
+    for ref, rows in ((in_ref, slice(0, 256)), (rest_ref, slice(256, 512))):
+        ref[:, :512] = new_left[rows]
+        ref[:, 512:] = new_right[rows]
 
 
 def pack_kernel(first_ref, second_ref, third_ref, out_ref):
@@ -184,43 +193,37 @@
     out_ref[...] = jnp.where(filled, sent, EMPTY).astype(BF)
 
 
-def return_kernel(returned_ref, target_ref, active_ref, text_ref, w_in_ref, out_ref, rows_ref):
-    @pl.when(pl.program_id(0) == 0)
-    def _():
-        unused, (target, live, earlier) = routing(target_ref, active_ref)
-        slot = iota((FRAMES, SLOTS), 1)
-        chosen = (
-            (target == (slot >> 1).astype(F32)) & (live > 0.5) & (earlier == (slot & 1).astype(F32))
-        ).astype(F32)
-        rows_ref[...] = dot(chosen.astype(BF), returned_ref[...]).astype(BF)
-
-    carried = dot_nt(rows_ref[...], w_in_ref[0]).astype(BF).astype(F32)
-    out_ref[0] = (text_ref[...].astype(F32) + carried).astype(BF)
-
-
-def depth_kernel(
-    slots_ref,
-    codes_ref,
-    cot_ref,
-    gain_ref,
-    weights_ref,
-    out_ref,
-    w_qkv,
-    w_out,
-    hidden_s,
-    cot_s,
-    grads_s,
-    frames_s,
-    sems,
-):
+def parts_held():
+    x, core = lax.axis_index("x"), lax.axis_index("core")
+    return [((x + 4 - shift) & 3) * 2 + side for side in (core, 1 - core) for shift in SHIFTS]
+
+
+def return_kernel(returned_ref, target_ref, active_ref, text_ref, *refs):
+    pieces, out_ref = refs[:SEQ], refs[SEQ]
+    unused, (target, live, earlier) = routing(target_ref, active_ref)
+    slot = iota((FRAMES, SLOTS), 1)
+    chosen = (
+        (target == (slot >> 1).astype(F32)) & (live > 0.5) & (earlier == (slot & 1).astype(F32))
+    ).astype(F32)
+    rows = dot(chosen.astype(BF), returned_ref[...]).astype(BF)
+    for part, piece in zip(parts_held(), pieces):
+        carried = dot_nt(rows, piece[...]).astype(BF).astype(F32)
+        start = pl.multiple_of(part * COLS, COLS)
+        out_ref[part] = (text_ref[:, pl.ds(start, COLS)].astype(F32) + carried).astype(BF)
+
+
+def depth_kernel(slots_ref, codes_ref, cot_ref, gain_ref, *refs):
+    pieces, refs = refs[:SEQ], refs[SEQ:]
+    out_ref, w_qkv, w_out, hidden_s, cot_s, grads_s, frames_s, sems = refs
     copies = []
-    for part in range(SEQ):
-        low = part * 128
+    for part, piece in zip(parts_held(), pieces):
+        low = pl.multiple_of(part * 128, 128)
+        low_half = pl.multiple_of(part * 64, 64)
         pairs = (
-            (weights_ref.at[part, 256:384, :], w_qkv.at[low : low + 128, :1024]),
-            (weights_ref.at[part, 384:448, :512], w_qkv.at[low : low + 64, 1024:]),
-            (weights_ref.at[part, 384:448, 512:], w_qkv.at[low + 64 : low + 128, 1024:]),
-            (weights_ref.at[part, 448:512, :], w_out.at[part * 64 : part * 64 + 64, :]),
+            (piece.at[:128, :], w_qkv.at[pl.ds(low, 128), :1024]),
+            (piece.at[128:192, :512], w_qkv.at[pl.ds(low, 64), 1024:]),
+            (piece.at[128:192, 512:], w_qkv.at[pl.ds(low + 64, 64), 1024:]),
+            (piece.at[192:256, :], w_out.at[pl.ds(low_half, 64), :]),
         )
         for source, goal in pairs:
             copies.append(pltpu.make_async_copy(source, goal, sems.at[len(copies)]))
@@ -305,6 +308,15 @@
     return lax.all_to_all(array, axis, split_axis=0, concat_axis=0, tiled=True)
 
 
+def moved(array, axis, size, shift):
+    return lax.ppermute(array, axis, [(i, (i + shift) % size) for i in range(size)])
+
+
+def gathered(piece):
+    along = [piece] + [moved(piece, "x", 4, shift) for shift in SHIFTS[1:]]
+    return along + [moved(each, "core", 2, 1) for each in along]
+
+
 def shards(
     queries,
     keys,
@@ -319,31 +331,32 @@
     w_qkv,
     w_out,
 ):
+    seq = ("x", "core")
     owner = ("y", "z")
     mine = jnp.concatenate([w_in, w_qkv, w_out]).reshape(1, 8, D_DEP)
-    along_z = exchange(jnp.broadcast_to(mine, (16, 8, D_DEP)), "z")
-    along_y = exchange(jnp.broadcast_to(along_z.reshape(1, 128, D_DEP), (4, 128, D_DEP)), "y")
-    own_weights = call(weight_kernel, jax.ShapeDtypeStruct((512, D_DEP), BF), "sort_weights")(
-        along_y.reshape(512, D_DEP)
-    )
-    all_weights = lax.all_gather(own_weights, "seq", axis=0, tiled=True).reshape(SEQ, 512, D_DEP)
+    along_z = exchange(jnp.broadcast_to(mine, (16, 8, D_DEP)), "z").reshape(128, D_DEP)
+    along_y = [along_z] + [moved(along_z, "y", 4, shift) for shift in SHIFTS[1:]]
+    half = jax.ShapeDtypeStruct((256, D_DEP), BF)
+    own_in, own_rest = call(
+        weight_kernel,
+        (half, half),
+        "sort_weights",
+        scratch_shapes=[pltpu.VMEM((512, D_DEP), BF)],
+    )(*along_y)
+    rest = gathered(own_rest)
 
     packed = call(pack_kernel, jax.ShapeDtypeStruct((SEQ, FRAMES, 3 * COLS), BF), "pack_qkv")(
         queries[0], keys[0], values[0]
     )
-    packed = exchange(packed, "seq").reshape(LENGTH, 3 * COLS)
+    packed = exchange(packed, seq).reshape(LENGTH, 3 * COLS)
     parts = call(
         forward_kernel,
         jax.ShapeDtypeStruct((LENGTH, D_DEP), BF),
         "attention_forward",
-        grid=(1,),
-        in_specs=[
-            pl.BlockSpec((LENGTH, 3 * COLS), lambda i: (0, 0)),
-            pl.BlockSpec((COLS, D_DEP), lambda i: (0, 0)),
-        ],
-        out_specs=pl.BlockSpec((LENGTH, D_DEP), lambda i: (0, 0)),
-    )(packed, own_weights)
-    parts = exchange(parts.reshape(SEQ, FRAMES, D_DEP), "seq")
+    )(packed, own_in)
+    parts = exchange(parts.reshape(SEQ, FRAMES, D_DEP), seq)
+    late_in, unused = lax.optimization_barrier((own_in, parts))
+    all_in = gathered(late_in)
     sent = call(send_kernel, jax.ShapeDtypeStruct((SLOTS, D_DEP), BF), "send_rows")(
         parts, target, active
     )
@@ -353,7 +366,7 @@
         depth_kernel,
         jax.ShapeDtypeStruct((SLOTS, D_DEP), BF),
         "depth_layer",
-        in_specs=[vmem, vmem, vmem, vmem, pl.BlockSpec(memory_space=pl.ANY)],
+        in_specs=[vmem] * 4 + [pl.BlockSpec(memory_space=pl.ANY)] * SEQ,
         out_specs=vmem,
         scratch_shapes=[
             pltpu.VMEM((D_DEP, 3 * DHEADS * DHEAD), BF),
@@ -370,40 +383,30 @@
         codes.reshape(ROWS, D_DEP),
         depth_cot.reshape(ROWS, D_DEP),
         norm_gain.reshape(1, D_DEP),
-        all_weights,
+        *rest,
     )
     returned = exchange(grads.reshape(OWNERS, CAP, D_DEP), owner).reshape(SLOTS, D_DEP)
     out_grad = call(
         return_kernel,
         jax.ShapeDtypeStruct((SEQ, FRAMES, COLS), BF),
         "return_rows",
-        grid=(SEQ,),
-        in_specs=[
-            pl.BlockSpec((SLOTS, D_DEP), lambda i: (0, 0)),
-            pl.BlockSpec((1, FRAMES), lambda i: (0, 0)),
-            pl.BlockSpec((1, FRAMES), lambda i: (0, 0)),
-            pl.BlockSpec((FRAMES, COLS), lambda i: (0, i)),
-            pl.BlockSpec((1, COLS, D_DEP), lambda i: (i, 0, 0)),
-        ],
-        out_specs=pl.BlockSpec((1, FRAMES, COLS), lambda i: (i, 0, 0)),
-        scratch_shapes=[pltpu.VMEM((FRAMES, D_DEP), BF)],
-    )(returned, target, active, text_grad[0], all_weights)
-    out_grad = exchange(out_grad, "seq").reshape(LENGTH, COLS)
+    )(returned, target, active, text_grad[0], *all_in)
+    out_grad = exchange(out_grad, seq).reshape(LENGTH, COLS)
     grads = call(
         backward_kernel, jax.ShapeDtypeStruct((LENGTH, 3 * COLS), BF), "attention_backward"
     )(packed, out_grad)
-    grads = exchange(grads.reshape(SEQ, FRAMES, 3 * COLS), "seq")
+    grads = exchange(grads.reshape(SEQ, FRAMES, 3 * COLS), seq)
     shape = jax.ShapeDtypeStruct((FRAMES, D_CTX), BF)
     query_grad, key_grad, value_grad = call(unpack_kernel, (shape, shape, shape), "unpack_grads")(grads)
     return query_grad[None], key_grad[None], value_grad[None]
 
 
 def solution(mesh):
-    split = Mesh(mesh.devices.reshape(SEQ, 4, 16), ("seq", "y", "z"))
-    rows = P(("y", "z"), "seq", None)
-    frames = P(("y", "z"), "seq")
-    code_rows = P(("y", "z"), "seq", None, None)
-    flat = P(("seq", "y", "z"))
+    split = Mesh(mesh.devices.reshape(4, 2, 4, 16), ("x", "core", "y", "z"))
+    rows = P(("y", "z"), ("x", "core"), None)
+    frames = P(("y", "z"), ("x", "core"))
+    code_rows = P(("y", "z"), ("x", "core"), None, None)
+    flat = P(("x", "core", "y", "z"))
     in_specs = (
         rows,
         rows,

time: 232 us -> 207 us (0.89)
  blocking collectives: 152 us -> 29.8 us
  starting transfers between devices: 11 us -> 102 us
  waiting for transfers between devices: 18.6 us -> 36.4 us
  between operations: 14.2 us -> 1.05 us
    all_to_all x7 -> x2, blocking collectives: 152 us -> 29.8 us  [exchange(): return lax.all_to_all(array, axis, split_axis=0, concat_axis=0, tiled=True)]
    ppermute x0 -> x17, starting transfers between devices: none -> 49.4 us  [moved(): lax.ppermute(array, axis, [(i, (i + shift) % size) for i in range(size)])]
    all_to_all x1 -> x5, starting transfers between devices: 11 us -> 52.7 us  [exchange(): return lax.all_to_all(array, axis, split_axis=0, concat_axis=0, tiled=True)]
    ppermute x0 -> x17, waiting for transfers between devices: none -> 10.8 us  [moved(): lax.ppermute(array, axis, [(i, (i + shift) % size) for i in range(size)])]
    all_to_all x1 -> x5, waiting for transfers between devices: 18.5 us -> 25.6 us  [exchange(): return lax.all_to_all(array, axis, split_axis=0, concat_axis=0, tiled=True)]
    unnamed x20, local copies, waits for them, and re-layouts: 6.25 us -> 1.87 us
  transfers between devices with their start and end apart: 2 -> 22, of which waited for: 1 -> 7; matrix products, arithmetic and copies ran while one was open for 0% -> 2% of each run, Pallas kernels for 2% -> 10%
where the time goes in v2:
time: 207 us; the launch traced here: 206 us
  starting transfers between devices  102 us (49%)
  waiting for transfers between devices  36.4 us (18%)
  blocking collectives  29.8 us (14%)
  Pallas kernels  29.5 us (14%)
  local copies, waits for them, and re-layouts  6.32 us (3%)
    all_to_all x5, starting transfers between devices, exchange(): return lax.all_to_all(array, axis, split_axis=0, concat_axis=0, tiled=True)  52.7 us
    ppermute x17, starting transfers between devices, moved(): lax.ppermute(array, axis, [(i, (i + shift) % size) for i in range(size)])  49.4 us
    all_to_all x2, blocking collectives, exchange(): return lax.all_to_all(array, axis, split_axis=0, concat_axis=0, tiled=True)  29.8 us
    all_to_all x5, waiting for transfers between devices, exchange(): return lax.all_to_all(array, axis, split_axis=0, concat_axis=0, tiled=True)  25.6 us
    pallas_call x1, Pallas kernels, shards(): call(depth_kernel, jax.ShapeDtypeStruct((SLOTS, D_DEP), BF), 'depth_layer...  16.6 us
    ppermute x17, waiting for transfers between devices, moved(): lax.ppermute(array, axis, [(i, (i + shift) % size) for i in range(size)])  10.8 us
  transfers between devices with their start and end apart: 22, of which 7 were waited for; matrix products, arithmetic and copies ran while one was open for 2% of the time, Pallas kernels for 10%

profile of v2, /device:TPU:1, one launch (start us, length us, event | category | flops | bytes accessed | tf_op | source)
XLA Modules:
  0.0 205.9 jit_solution(16682538206881039758)
XLA Ops:
  2.1 15.9 %all-to-all-start.1 = ((bf16[16,8,1024]{2,1,0:T(8,128)(2,1)}), bf16[16,8,1024]{2,1,0:T(8,128)(2,1)S(1)}, u32[]{:S(2)}, u32[]{:S(2)}) async-start(bf16[16,8,1024]{2,1,0:T(8,128)(2,1)} %broadcast_in_dim.17), calls=%async_computation.1 | async-start | bytes 524288 | tf_op jit(solution)/shard_map/all_to_all | solution.py:308
  19.0 12.2 %all-to-all-done.1 = bf16[16,8,1024]{2,1,0:T(8,128)(2,1)S(1)} async-done(((bf16[16,8,1024]{2,1,0:T(8,128)(2,1)}), bf16[16,8,1024]{2,1,0:T(8,128)(2,1)S(1)}, u32[]{:S(2)}, u32[]{:S(2)}) %all-to-all-start.1) | async-done | bytes 262176 | tf_op jit(solution)/shard_map/all_to_all | solution.py:308
  31.1 10.5 %all-to-all-start = ((bf16[8,64,768]{2,1,0:T(8,128)(2,1)}), bf16[8,64,768]{2,1,0:T(8,128)(2,1)S(1)}, u32[]{:S(2)}, u32[]{:S(2)}) async-start(bf16[8,64,768]{2,1,0:T(8,128)(2,1)} %pack_qkv.1), calls=%async_computation | async-start | bytes 1572864 | tf_op jit(solution)/shard_map/all_to_all | solution.py:308
  41.6 3.2 %collective-permute-start = (bf16[128,1024]{1,0:T(8,128)(2,1)S(1)}, bf16[128,1024]{1,0:T(8,128)(2,1)S(1)}, u32[]{:S(2)}, u32[]{:S(2)}) collective-permute-start(bf16[128,1024]{1,0:T(8,128)(2,1)S(1)} %bitcast.18), channel_id=1, source_target_pairs={{0,16},{16,32},{32,48},{48,0},{1,17},{17,33},{33,49},{49,1},{2,18}... | collective-permute-start | bytes 786440 | tf_op jit(solution)/shard_map/ppermute | solution.py:312
  44.8 3.4 %collective-permute-start.1 = (bf16[128,1024]{1,0:T(8,128)(2,1)S(1)}, bf16[128,1024]{1,0:T(8,128)(2,1)S(1)}, u32[]{:S(2)}, u32[]{:S(2)}) collective-permute-start(bf16[128,1024]{1,0:T(8,128)(2,1)S(1)} %bitcast.19), channel_id=1, source_target_pairs={{0,48},{16,0},{32,16},{48,32},{1,49},{17,1},{33,17},{49,33},{2,50}... | collective-permute-start | bytes 786440 | tf_op jit(solution)/shard_map/ppermute | solution.py:312
  48.2 3.5 %collective-permute-start.2 = (bf16[128,1024]{1,0:T(8,128)(2,1)S(1)}, bf16[128,1024]{1,0:T(8,128)(2,1)S(1)}, u32[]{:S(2)}, u32[]{:S(2)}) collective-permute-start(bf16[128,1024]{1,0:T(8,128)(2,1)S(1)} %bitcast.20), channel_id=1, source_target_pairs={{0,32},{16,48},{32,0},{48,16},{1,33},{17,49},{33,1},{49,17},{2,34}... | collective-permute-start | bytes 786440 | tf_op jit(solution)/shard_map/ppermute | solution.py:312
  54.3 4.6 %collective-permute-done.2.refs_3_ = bf16[128,1024]{1,0:T(8,128)(2,1)S(1)} collective-permute-done((bf16[128,1024]{1,0:T(8,128)(2,1)S(1)}, bf16[128,1024]{1,0:T(8,128)(2,1)S(1)}, u32[]{:S(2)}, u32[]{:S(2)}) %collective-permute-start.2) | collective-permute-done | bytes 262176 | tf_op jit(solution)/shard_map/ppermute | solution.py:312
  61.1 3.0 %attention_forward.1 = bf16[512,1024]{1,0:T(8,128)(2,1)} custom-call(bf16[512,768]{1,0:T(8,128)(2,1)S(1)} %bitcast.14, bf16[256,1024]{1,0:T(8,128)(2,1)S(1)} %get-tuple-element.11.w_in_ref.refs_0_), custom_call_target="tpu_custom_call" | custom-call | tf_op jit(solution)/shard_map/attention_forward/pallas_call | solution.py:352
  64.1 5.8 %all-to-all-start.2 = ((bf16[8,64,1024]{2,1,0:T(8,128)(2,1)}), bf16[8,64,1024]{2,1,0:T(8,128)(2,1)S(1)}, u32[]{:S(2)}, u32[]{:S(2)}) async-start(bf16[8,64,1024]{2,1,0:T(8,128)(2,1)} %bitcast.5), calls=%async_computation.2 | async-start | bytes 2097152 | tf_op jit(solution)/shard_map/all_to_all | solution.py:308
  69.9 3.4 %collective-permute-start.3 = (bf16[256,1024]{1,0:T(8,128)(2,1)}, bf16[256,1024]{1,0:T(8,128)(2,1)}, u32[]{:S(2)}, u32[]{:S(2)}) collective-permute-start(bf16[256,1024]{1,0:T(8,128)(2,1)} %get-tuple-element.10.refs_0_), channel_id=1, source_target_pairs={{0,128},{128,256},{256,384},{384,0},{1,129},{129,257},{257,385},{3... | collective-permute-start | bytes 1572872 | tf_op jit(solution)/shard_map/ppermute | solution.py:312
  73.3 3.2 %collective-permute-start.4 = (bf16[256,1024]{1,0:T(8,128)(2,1)}, bf16[256,1024]{1,0:T(8,128)(2,1)}, u32[]{:S(2)}, u32[]{:S(2)}) collective-permute-start(bf16[256,1024]{1,0:T(8,128)(2,1)} %get-tuple-element.10.refs_0_), channel_id=1, source_target_pairs={{0,384},{128,0},{256,128},{384,256},{1,385},{129,1},{257,129},{385... | collective-permute-start | bytes 1572872 | tf_op jit(solution)/shard_map/ppermute | solution.py:312
  76.5 3.6 %collective-permute-start.5 = (bf16[256,1024]{1,0:T(8,128)(2,1)}, bf16[256,1024]{1,0:T(8,128)(2,1)}, u32[]{:S(2)}, u32[]{:S(2)}) collective-permute-start(bf16[256,1024]{1,0:T(8,128)(2,1)} %get-tuple-element.10.refs_0_), channel_id=1, source_target_pairs={{0,256},{128,384},{256,0},{384,128},{1,257},{129,385},{257,1},{385... | collective-permute-start | bytes 1572872 | tf_op jit(solution)/shard_map/ppermute | solution.py:312
  80.1 4.9 %all-to-all-done.2.parts_ref = bf16[8,64,1024]{2,1,0:T(8,128)(2,1)S(1)} async-done(((bf16[8,64,1024]{2,1,0:T(8,128)(2,1)}), bf16[8,64,1024]{2,1,0:T(8,128)(2,1)S(1)}, u32[]{:S(2)}, u32[]{:S(2)}) %all-to-all-start.2) | async-done | bytes 1048608 | tf_op jit(solution)/shard_map/all_to_all | solution.py:308
  86.2 9.9 %all-to-all-start.3 = ((bf16[64,2,1024]{2,1,0:T(2,128)(2,1)}), bf16[64,2,1024]{2,1,0:T(2,128)(2,1)}, u32[]{:S(2)}, u32[]{:S(2)}) async-start(bf16[64,2,1024]{2,1,0:T(2,128)(2,1)} %reshape.47), calls=%async_computation.3 | async-start | bytes 524288 | tf_op jit(solution)/shard_map/all_to_all | solution.py:308
  96.2 3.5 %collective-permute-start.6 = (bf16[256,1024]{1,0:T(8,128)(2,1)}, bf16[256,1024]{1,0:T(8,128)(2,1)S(1)}, u32[]{:S(2)}, u32[]{:S(2)}) collective-permute-start(bf16[256,1024]{1,0:T(8,128)(2,1)} %get-tuple-element.10.refs_0_), channel_id=1, source_target_pairs={{0,64},{64,0},{1,65},{65,1},{2,66},{66,2},{3,67},{67,3},{4,68},{68... | collective-permute-start | bytes 1572872 | tf_op jit(solution)/shard_map/ppermute | solution.py:312
  104.1 3.5 %collective-permute-done.5.refs_3_ = bf16[256,1024]{1,0:T(8,128)(2,1)} collective-permute-done((bf16[256,1024]{1,0:T(8,128)(2,1)}, bf16[256,1024]{1,0:T(8,128)(2,1)}, u32[]{:S(2)}, u32[]{:S(2)}) %collective-permute-start.5) | collective-permute-done | bytes 524320 | tf_op jit(solution)/shard_map/ppermute | solution.py:312
  112.6 4.3 %collective-permute-start.11 = (bf16[256,1024]{1,0:T(8,128)(2,1)S(1)}, bf16[256,1024]{1,0:T(8,128)(2,1)}, u32[]{:S(2)}, u32[]{:S(2)}) collective-permute-start(bf16[256,1024]{1,0:T(8,128)(2,1)S(1)} %get-tuple-element.11.w_in_ref.refs_0_), channel_id=1, source_target_pairs={{0,384},{128,0},{256,128},{384,256},{1,385},{129,1},{257,129},{385... | collective-permute-start | bytes 1572872 | tf_op jit(solution)/shard_map/ppermute | solution.py:312
  122.0 16.6 %depth_layer.1 = bf16[128,1024]{1,0:T(8,128)(2,1)S(1)} custom-call(bf16[128,1024]{1,0:T(8,128)(2,1)S(1)} %reshape.48.slots_ref, bf16[472,1024]{1,0:T(8,128)(2,1)S(1)} %bitcast.22, bf16[472,1024]{1,0:T(8,128)(2,1)} %bitcast.27, bf16[1,1024]{1,0:T(2,128)(2,1)S(1)} %reshape.51.gain_ref, bf16[256,1024]{1,0:T(8,128)(2,1)} %get-tuple-element.10.refs_0_, ...), custom_call_target="tpu_custom_call" | custom-call | tf_op jit(solution)/shard_map/depth_layer/pallas_call | solution.py:365
  139.4 10.7 %all-to-all-start.4 = ((bf16[64,2,1024]{2,1,0:T(2,128)(2,1)}), bf16[64,2,1024]{2,1,0:T(2,128)(2,1)}, u32[]{:S(2)}, u32[]{:S(2)}) async-start(bf16[64,2,1024]{2,1,0:T(2,128)(2,1)} %reshape.52), calls=%async_computation.4 | async-start | bytes 524288 | tf_op jit(solution)/shard_map/all_to_all | solution.py:308
  150.1 3.4 %collective-permute-start.13 = (bf16[256,1024]{1,0:T(8,128)(2,1)S(1)}, bf16[256,1024]{1,0:T(8,128)(2,1)S(1)}, u32[]{:S(2)}, u32[]{:S(2)}) collective-permute-start(bf16[256,1024]{1,0:T(8,128)(2,1)S(1)} %get-tuple-element.11.w_in_ref.refs_0_), channel_id=1, source_target_pairs={{0,64},{64,0},{1,65},{65,1},{2,66},{66,2},{3,67},{67,3},{4,68},{68... | collective-permute-start | bytes 1572872 | tf_op jit(solution)/shard_map/ppermute | solution.py:312
  160.0 8.5 %all-to-all-done.4 = bf16[64,2,1024]{2,1,0:T(2,128)(2,1)} async-done(((bf16[64,2,1024]{2,1,0:T(2,128)(2,1)}), bf16[64,2,1024]{2,1,0:T(2,128)(2,1)}, u32[]{:S(2)}, u32[]{:S(2)}) %all-to-all-start.4) | async-done | bytes 262176 | tf_op jit(solution)/shard_map/all_to_all | solution.py:308
  169.6 3.2 %return_rows.1 = bf16[8,64,256]{2,1,0:T(8,128)(2,1)S(1)} custom-call(bf16[128,1024]{1,0:T(8,128)(2,1)S(1)} %reshape.53.returned_ref, s32[1,64]{1,0:T(1,128)S(1)} %copy-done.7, s32[1,64]{1,0:T(1,128)S(1)} %copy-done.8, bf16[64,2048]{1,0:T(8,128)(2,1)S(1)} %bitcast.26, bf16[256,1024]{1,0:T(8,128)(2,1)S(1)} %get-tuple-element.11.w_in_ref.refs_0_, ...), custom_call_target="tpu_custom_call" | custom-call | tf_op jit(solution)/shard_map/return_rows/pallas_call | solution.py:389
  172.8 14.2 %all_to_all.35 = bf16[8,64,256]{2,1,0:T(8,128)(2,1)S(1)} all-to-all(bf16[8,64,256]{2,1,0:T(8,128)(2,1)S(1)} %return_rows.1), channel_id=1, replica_groups=mesh['x'=4,'core'=2,'y'=4,'z'=16] {'x','core'}, dimensions={0} | all-to-all | bytes 524288 | tf_op jit(solution)/shard_map/all_to_all | solution.py:308
  189.3 15.7 %all_to_all.36.packed_ref = bf16[8,64,768]{2,1,0:T(8,128)(2,1)S(1)} all-to-all(bf16[8,64,768]{2,1,0:T(8,128)(2,1)S(1)} %bitcast.16), channel_id=1, replica_groups=mesh['x'=4,'core'=2,'y'=4,'z'=16] {'x','core'}, dimensions={0} | all-to-all | bytes 1572864 | tf_op jit(solution)/shard_map/all_to_all | solution.py:308
  (58 shorter events, 34.2 us)
Async XLA Ops:
  2.1 29.0 %all-to-all-start.1 = ((bf16[16,8,1024]{2,1,0:T(8,128)(2,1)}), bf16[16,8,1024]{2,1,0:T(8,128)(2,1)S(1)}, u32[]{:S(2)}, u32[]{:S(2)}) async-start(bf16[16,8,1024]{2,1,0:T(8,128)(2,1)} %broadcast_in_dim.17), calls=%async_computation.1 | async-start | bytes 524288 | tf_op jit(solution)/shard_map/all_to_all | solution.py:308
  31.1 29.9 %all-to-all-start = ((bf16[8,64,768]{2,1,0:T(8,128)(2,1)}), bf16[8,64,768]{2,1,0:T(8,128)(2,1)S(1)}, u32[]{:S(2)}, u32[]{:S(2)}) async-start(bf16[8,64,768]{2,1,0:T(8,128)(2,1)} %pack_qkv.1), calls=%async_computation | async-start | bytes 1572864 | tf_op jit(solution)/shard_map/all_to_all | solution.py:308
  41.6 11.2 %collective-permute-start = (bf16[128,1024]{1,0:T(8,128)(2,1)S(1)}, bf16[128,1024]{1,0:T(8,128)(2,1)S(1)}, u32[]{:S(2)}, u32[]{:S(2)}) collective-permute-start(bf16[128,1024]{1,0:T(8,128)(2,1)S(1)} %bitcast.18), channel_id=1, source_target_pairs={{0,16},{16,32},{32,48},{48,0},{1,17},{17,33},{33,49},{49,1},{2,18}... | collective-permute-start | bytes 786440 | tf_op jit(solution)/shard_map/ppermute | solution.py:312
  44.8 9.5 %collective-permute-start.1 = (bf16[128,1024]{1,0:T(8,128)(2,1)S(1)}, bf16[128,1024]{1,0:T(8,128)(2,1)S(1)}, u32[]{:S(2)}, u32[]{:S(2)}) collective-permute-start(bf16[128,1024]{1,0:T(8,128)(2,1)S(1)} %bitcast.19), channel_id=1, source_target_pairs={{0,48},{16,0},{32,16},{48,32},{1,49},{17,1},{33,17},{49,33},{2,50}... | collective-permute-start | bytes 786440 | tf_op jit(solution)/shard_map/ppermute | solution.py:312
  48.2 10.8 %collective-permute-start.2 = (bf16[128,1024]{1,0:T(8,128)(2,1)S(1)}, bf16[128,1024]{1,0:T(8,128)(2,1)S(1)}, u32[]{:S(2)}, u32[]{:S(2)}) collective-permute-start(bf16[128,1024]{1,0:T(8,128)(2,1)S(1)} %bitcast.20), channel_id=1, source_target_pairs={{0,32},{16,48},{32,0},{48,16},{1,33},{17,49},{33,1},{49,17},{2,34}... | collective-permute-start | bytes 786440 | tf_op jit(solution)/shard_map/ppermute | solution.py:312
  64.1 20.9 %all-to-all-start.2 = ((bf16[8,64,1024]{2,1,0:T(8,128)(2,1)}), bf16[8,64,1024]{2,1,0:T(8,128)(2,1)S(1)}, u32[]{:S(2)}, u32[]{:S(2)}) async-start(bf16[8,64,1024]{2,1,0:T(8,128)(2,1)} %bitcast.5), calls=%async_computation.2 | async-start | bytes 2097152 | tf_op jit(solution)/shard_map/all_to_all | solution.py:308
  69.9 29.8 %collective-permute-start.3 = (bf16[256,1024]{1,0:T(8,128)(2,1)}, bf16[256,1024]{1,0:T(8,128)(2,1)}, u32[]{:S(2)}, u32[]{:S(2)}) collective-permute-start(bf16[256,1024]{1,0:T(8,128)(2,1)} %get-tuple-element.10.refs_0_), channel_id=1, source_target_pairs={{0,128},{128,256},{256,384},{384,0},{1,129},{129,257},{257,385},{3... | collective-permute-start | bytes 1572872 | tf_op jit(solution)/shard_map/ppermute | solution.py:312
  73.3 28.3 %collective-permute-start.4 = (bf16[256,1024]{1,0:T(8,128)(2,1)}, bf16[256,1024]{1,0:T(8,128)(2,1)}, u32[]{:S(2)}, u32[]{:S(2)}) collective-permute-start(bf16[256,1024]{1,0:T(8,128)(2,1)} %get-tuple-element.10.refs_0_), channel_id=1, source_target_pairs={{0,384},{128,0},{256,128},{384,256},{1,385},{129,1},{257,129},{385... | collective-permute-start | bytes 1572872 | tf_op jit(solution)/shard_map/ppermute | solution.py:312
  76.5 31.1 %collective-permute-start.5 = (bf16[256,1024]{1,0:T(8,128)(2,1)}, bf16[256,1024]{1,0:T(8,128)(2,1)}, u32[]{:S(2)}, u32[]{:S(2)}) collective-permute-start(bf16[256,1024]{1,0:T(8,128)(2,1)} %get-tuple-element.10.refs_0_), channel_id=1, source_target_pairs={{0,256},{128,384},{256,0},{384,128},{1,257},{129,385},{257,1},{385... | collective-permute-start | bytes 1572872 | tf_op jit(solution)/shard_map/ppermute | solution.py:312
  85.4 34.4 %copy-start.9 = (bf16[1024]{0:T(1024)(128)(2,1)S(1)}, bf16[1024]{0:T(1024)(128)(2,1)}, u32[]{:S(2)}) copy-start(bf16[1024]{0:T(1024)(128)(2,1)} %param.21) | copy-start | bytes 6148
  86.2 34.7 %copy-start = (bf16[1,59,8,1024]{3,2,1,0:T(8,128)(2,1)S(1)}, bf16[1,59,8,1024]{3,2,1,0:T(8,128)(2,1)}, u32[]{:S(2)}) copy-start(bf16[1,59,8,1024]{3,2,1,0:T(8,128)(2,1)} %param.18) | copy-start | bytes 2899972
  86.2 33.6 %all-to-all-start.3 = ((bf16[64,2,1024]{2,1,0:T(2,128)(2,1)}), bf16[64,2,1024]{2,1,0:T(2,128)(2,1)}, u32[]{:S(2)}, u32[]{:S(2)}) async-start(bf16[64,2,1024]{2,1,0:T(2,128)(2,1)} %reshape.47), calls=%async_computation.3 | async-start | bytes 524288 | tf_op jit(solution)/shard_map/all_to_all | solution.py:308
  96.2 16.4 %collective-permute-start.6 = (bf16[256,1024]{1,0:T(8,128)(2,1)}, bf16[256,1024]{1,0:T(8,128)(2,1)S(1)}, u32[]{:S(2)}, u32[]{:S(2)}) collective-permute-start(bf16[256,1024]{1,0:T(8,128)(2,1)} %get-tuple-element.10.refs_0_), channel_id=1, source_target_pairs={{0,64},{64,0},{1,65},{65,1},{2,66},{66,2},{3,67},{67,3},{4,68},{68... | collective-permute-start | bytes 1572872 | tf_op jit(solution)/shard_map/ppermute | solution.py:312
  99.7 17.2 %collective-permute-start.7 = (bf16[256,1024]{1,0:T(8,128)(2,1)}, bf16[256,1024]{1,0:T(8,128)(2,1)S(1)}, u32[]{:S(2)}, u32[]{:S(2)}) collective-permute-start(bf16[256,1024]{1,0:T(8,128)(2,1)} %collective-permute-done.3.refs_1_), channel_id=1, source_target_pairs={{0,64},{64,0},{1,65},{65,1},{2,66},{66,2},{3,67},{67,3},{4,68},{68... | collective-permute-start | bytes 1572872 | tf_op jit(solution)/shard_map/ppermute | solution.py:312
  101.7 19.3 %collective-permute-start.8 = (bf16[256,1024]{1,0:T(8,128)(2,1)}, bf16[256,1024]{1,0:T(8,128)(2,1)}, u32[]{:S(2)}, u32[]{:S(2)}) collective-permute-start(bf16[256,1024]{1,0:T(8,128)(2,1)} %collective-permute-done.4.refs_2_), channel_id=1, source_target_pairs={{0,64},{64,0},{1,65},{65,1},{2,66},{66,2},{3,67},{67,3},{4,68},{68... | collective-permute-start | bytes 1572872 | tf_op jit(solution)/shard_map/ppermute | solution.py:312
  107.6 13.3 %collective-permute-start.9 = (bf16[256,1024]{1,0:T(8,128)(2,1)}, bf16[256,1024]{1,0:T(8,128)(2,1)}, u32[]{:S(2)}, u32[]{:S(2)}) collective-permute-start(bf16[256,1024]{1,0:T(8,128)(2,1)} %collective-permute-done.5.refs_3_), channel_id=1, source_target_pairs={{0,64},{64,0},{1,65},{65,1},{2,66},{66,2},{3,67},{67,3},{4,68},{68... | collective-permute-start | bytes 1572872 | tf_op jit(solution)/shard_map/ppermute | solution.py:312
  110.4 43.1 %collective-permute-start.10 = (bf16[256,1024]{1,0:T(8,128)(2,1)S(1)}, bf16[256,1024]{1,0:T(8,128)(2,1)}, u32[]{:S(2)}, u32[]{:S(2)}) collective-permute-start(bf16[256,1024]{1,0:T(8,128)(2,1)S(1)} %get-tuple-element.11.w_in_ref.refs_0_), channel_id=1, source_target_pairs={{0,128},{128,256},{256,384},{384,0},{1,129},{129,257},{257,385},{3... | collective-permute-start | bytes 1572872 | tf_op jit(solution)/shard_map/ppermute | solution.py:312
  112.6 42.8 %collective-permute-start.11 = (bf16[256,1024]{1,0:T(8,128)(2,1)S(1)}, bf16[256,1024]{1,0:T(8,128)(2,1)}, u32[]{:S(2)}, u32[]{:S(2)}) collective-permute-start(bf16[256,1024]{1,0:T(8,128)(2,1)S(1)} %get-tuple-element.11.w_in_ref.refs_0_), channel_id=1, source_target_pairs={{0,384},{128,0},{256,128},{384,256},{1,385},{129,1},{257,129},{385... | collective-permute-start | bytes 1572872 | tf_op jit(solution)/shard_map/ppermute | solution.py:312
  117.7 40.1 %collective-permute-start.12 = (bf16[256,1024]{1,0:T(8,128)(2,1)S(1)}, bf16[256,1024]{1,0:T(8,128)(2,1)}, u32[]{:S(2)}, u32[]{:S(2)}) collective-permute-start(bf16[256,1024]{1,0:T(8,128)(2,1)S(1)} %get-tuple-element.11.w_in_ref.refs_0_), channel_id=1, source_target_pairs={{0,256},{128,384},{256,0},{384,128},{1,257},{129,385},{257,1},{385... | collective-permute-start | bytes 1572872 | tf_op jit(solution)/shard_map/ppermute | solution.py:312
  139.4 29.1 %all-to-all-start.4 = ((bf16[64,2,1024]{2,1,0:T(2,128)(2,1)}), bf16[64,2,1024]{2,1,0:T(2,128)(2,1)}, u32[]{:S(2)}, u32[]{:S(2)}) async-start(bf16[64,2,1024]{2,1,0:T(2,128)(2,1)} %reshape.52), calls=%async_computation.4 | async-start | bytes 524288 | tf_op jit(solution)/shard_map/all_to_all | solution.py:308
  150.1 19.5 %collective-permute-start.13 = (bf16[256,1024]{1,0:T(8,128)(2,1)S(1)}, bf16[256,1024]{1,0:T(8,128)(2,1)S(1)}, u32[]{:S(2)}, u32[]{:S(2)}) collective-permute-start(bf16[256,1024]{1,0:T(8,128)(2,1)S(1)} %get-tuple-element.11.w_in_ref.refs_0_), channel_id=1, source_target_pairs={{0,64},{64,0},{1,65},{65,1},{2,66},{66,2},{3,67},{67,3},{4,68},{68... | collective-permute-start | bytes 1572872 | tf_op jit(solution)/shard_map/ppermute | solution.py:312
  153.5 16.1 %collective-permute-start.14 = (bf16[256,1024]{1,0:T(8,128)(2,1)}, bf16[256,1024]{1,0:T(8,128)(2,1)S(1)}, u32[]{:S(2)}, u32[]{:S(2)}) collective-permute-start(bf16[256,1024]{1,0:T(8,128)(2,1)} %collective-permute-done.10.refs_1_), channel_id=1, source_target_pairs={{0,64},{64,0},{1,65},{65,1},{2,66},{66,2},{3,67},{67,3},{4,68},{68... | collective-permute-start | bytes 1572872 | tf_op jit(solution)/shard_map/ppermute | solution.py:312
  155.4 14.2 %collective-permute-start.15 = (bf16[256,1024]{1,0:T(8,128)(2,1)}, bf16[256,1024]{1,0:T(8,128)(2,1)S(1)}, u32[]{:S(2)}, u32[]{:S(2)}) collective-permute-start(bf16[256,1024]{1,0:T(8,128)(2,1)} %collective-permute-done.11.refs_2_), channel_id=1, source_target_pairs={{0,64},{64,0},{1,65},{65,1},{2,66},{66,2},{3,67},{67,3},{4,68},{68... | collective-permute-start | bytes 1572872 | tf_op jit(solution)/shard_map/ppermute | solution.py:312
  157.8 11.8 %collective-permute-start.16 = (bf16[256,1024]{1,0:T(8,128)(2,1)}, bf16[256,1024]{1,0:T(8,128)(2,1)}, u32[]{:S(2)}, u32[]{:S(2)}) collective-permute-start(bf16[256,1024]{1,0:T(8,128)(2,1)} %collective-permute-done.12.refs_3_), channel_id=1, source_target_pairs={{0,64},{64,0},{1,65},{65,1},{2,66},{66,2},{3,67},{67,3},{4,68},{68... | collective-permute-start | bytes 1572872 | tf_op jit(solution)/shard_map/ppermute | solution.py:312
  (8 other events, 100.1 us)

commit v3 on v2

v3 whole, which is shorter than its diff:
```python
import jax
import jax.numpy as jnp
from jax import lax
from jax.experimental import pallas as pl
from jax.experimental.pallas import tpu as pltpu
from jax.sharding import Mesh
from jax.sharding import PartitionSpec as P

HEADS = 16
HEAD = 128
D_DEP = 1024
DHEADS = 8
DHEAD = 64
CODES = 8
D_CTX = 2048
FRAMES = 64
SEQ = 8
OWNERS = 64
CAP = 2
SLOTS = OWNERS * CAP
RECEIVED = 59
LENGTH = SEQ * FRAMES
COLS = D_CTX // SEQ
ROWS = RECEIVED * CODES
PADDED = 512
GROUP = 128
EMPTY = 2.0**100
SHIFTS = (0, 1, 3, 2)
BF = jnp.bfloat16
F32 = jnp.float32


def dot(a, b):
    return jnp.dot(a, b, preferred_element_type=F32)


def dot_nt(a, b):
    return lax.dot_general(a, b, (((1,), (1,)), ((), ())), preferred_element_type=F32)


def dot_tn(a, b):
    return lax.dot_general(a, b, (((0,), (0,)), ((), ())), preferred_element_type=F32)


def iota(shape, axis):
    return lax.broadcasted_iota(jnp.int32, shape, axis)


def call(kernel, out_shape, name, **options):
    limit = options.pop("vmem", 32)
    return pl.pallas_call(
        kernel,
        out_shape=out_shape,
        name=name,
        compiler_params=pltpu.CompilerParams(vmem_limit_bytes=limit * 2**20),
        **options,
    )


def weight_kernel(*refs):
    pieces, in_ref, rest_ref, gathered_ref = refs[:4], refs[4], refs[5], refs[6]
    here = lax.axis_index("y")
    for shift, piece in zip(SHIFTS, pieces):
        start = pl.multiple_of(((here + 4 - shift) & 3) * 128, 128)
        gathered_ref[pl.ds(start, 128), :] = piece[...]

    def picked(rows, source):
        return (iota((rows, 512), 1) == source).astype(F32).astype(BF)

    row = iota((256, 512), 0)
    in_ref[...] = dot(picked(256, ((row >> 2) << 3) + (row & 3)), gathered_ref[...]).astype(BF)
    row = iota((128, 512), 0)
    base = (row >> 1) << 3
    even = (row & 1) == 0
    upper = row < 64
    wanted = (
        (jnp.where(even, base + 4, -1), jnp.where(even, -1, base + 5)),
        (jnp.where(even, -1, base + 6), jnp.where(even, base + 4, -1)),
        (jnp.where(even, base + 5, -1), jnp.where(even, -1, base + 6)),
        (jnp.where(upper, (row << 3) + 7, -1), jnp.where(upper, -1, ((row - 64) << 3) + 7)),
    )
    left = gathered_ref[:, :512]
    right = gathered_ref[:, 512:]
    for place, (from_left, from_right) in enumerate(wanted):
        new = dot(picked(128, from_left), left) + dot(picked(128, from_right), right)
        rest_ref[:, place * 512 : (place + 1) * 512] = new.astype(BF)


def pack_kernel(*refs):
    ins, out_ref = refs[:4], refs[4]
    for part in range(SEQ):
        for place, ref in enumerate(ins):
            out_ref[part, :, place * COLS : (place + 1) * COLS] = ref[
                :, part * COLS : (part + 1) * COLS
            ]


def unpack_kernel(packed_ref, first_ref, second_ref, third_ref):
    for part in range(SEQ):
        for place, ref in enumerate((first_ref, second_ref, third_ref)):
            ref[:, part * COLS : (part + 1) * COLS] = packed_ref[
                part, :, place * COLS : (place + 1) * COLS
            ]


def head_weights(packed_ref, head):
    base = head * HEAD
    query = packed_ref[:, base : base + HEAD]
    key = packed_ref[:, COLS + base : COLS + base + HEAD]
    value = packed_ref[:, 2 * COLS + base : 2 * COLS + base + HEAD]
    scores = dot_nt(query, key) * HEAD ** (-0.5)
    allowed = iota((LENGTH, LENGTH), 1) <= iota((LENGTH, LENGTH), 0)
    scores = jnp.where(allowed, scores, -1e30)
    raised = jnp.exp(scores - jnp.max(scores, axis=1, keepdims=True))
    weights = raised * (1.0 / jnp.sum(raised, axis=1, keepdims=True))
    return query, key, value, weights


def forward_kernel(packed_ref, w_in_ref, out_ref):
    total = None
    for head in range(2):
        unused_q, unused_k, value, weights = head_weights(packed_ref, head)
        context = dot(weights.astype(BF), value).astype(BF)
        part = dot(context, w_in_ref[head * HEAD : (head + 1) * HEAD, :])
        total = part if total is None else total + part
    out_ref[...] = total.astype(BF)


def backward_kernel(packed_ref, own_ref, near_ref, out_ref, grad_s):
    core = lax.axis_index("core")
    for x in range(4):
        for side, ref in ((core, own_ref), (1 - core, near_ref)):
            start = pl.multiple_of((2 * x + side) * FRAMES, FRAMES)
            carried = ref[x * FRAMES : (x + 1) * FRAMES, :].astype(F32)
            text = packed_ref[pl.ds(start, FRAMES), 3 * COLS :].astype(F32)
            grad_s[pl.ds(start, FRAMES), :] = (text + carried).astype(BF)
    for head in range(2):
        base = head * HEAD
        query, key, value, weights = head_weights(packed_ref, head)
        grad = grad_s[:, base : base + HEAD]
        weight_grad = dot_nt(grad, value).astype(BF).astype(F32)
        inner = jnp.sum(weight_grad * weights, axis=1, keepdims=True)
        score_grad = (weights * (weight_grad - inner) * HEAD ** (-0.5)).astype(BF)
        out_ref[:, base : base + HEAD] = dot(score_grad, key).astype(BF)
        out_ref[:, COLS + base : COLS + base + HEAD] = dot_tn(score_grad, query).astype(BF)
        out_ref[:, 2 * COLS + base : 2 * COLS + base + HEAD] = dot_tn(
            weights.astype(BF), grad
        ).astype(BF)


def routing(target_ref, active_ref):
    down = iota((FRAMES, FRAMES), 0)
    across = iota((FRAMES, FRAMES), 1)
    target_row = target_ref[...].astype(F32)
    live_row = (active_ref[...] == 1).astype(F32)
    target_col = jnp.sum(jnp.where(down == across, target_row, 0.0), axis=1, keepdims=True)
    live_col = jnp.sum(jnp.where(down == across, live_row, 0.0), axis=1, keepdims=True)
    same = target_col == target_row
    earlier_row = jnp.sum(jnp.where(same & (down < across), live_col, 0.0), axis=0, keepdims=True)
    earlier_col = jnp.sum(jnp.where(same & (across < down), live_row, 0.0), axis=1, keepdims=True)
    return (target_row, live_row, earlier_row), (target_col, live_col, earlier_col)


def narrow_to_wide(narrow_ref, scratch):
    scratch[...] = narrow_ref[...].astype(F32)
    return jnp.concatenate([scratch[pl.ds(c, SLOTS, stride=8), :] for c in range(8)], axis=1)


def wide_to_narrow(wide, narrow_ref, scratch):
    for c in range(8):
        scratch[pl.ds(c, SLOTS, stride=8), :] = wide[:, c * 128 : (c + 1) * 128]
    narrow_ref[...] = scratch[...].astype(BF)


def send_kernel(parts_ref, target_ref, active_ref, out_ref, narrow_s):
    rows = parts_ref[0].astype(F32)
    for part in range(1, SEQ):
        rows = rows + parts_ref[part].astype(F32)
    (target, live, earlier), unused = routing(target_ref, active_ref)
    slot = iota((SLOTS, FRAMES), 0)
    chosen = (
        (target == (slot >> 1).astype(F32)) & (live > 0.5) & (earlier == (slot & 1).astype(F32))
    ).astype(F32)
    sent = dot(chosen.astype(BF), rows.astype(BF))
    filled = jnp.sum(chosen, axis=1, keepdims=True) > 0.5
    wide_to_narrow(jnp.where(filled, sent, EMPTY), out_ref, narrow_s)


def parts_held():
    x, core = lax.axis_index("x"), lax.axis_index("core")
    return [((x + 4 - shift) & 3) * 2 + side for side in (core, 1 - core) for shift in SHIFTS]


def return_kernel(returned_ref, target_ref, active_ref, out_ref, narrow_s):
    unused, (target, live, earlier) = routing(target_ref, active_ref)
    slot = iota((FRAMES, SLOTS), 1)
    chosen = (
        (target == (slot >> 1).astype(F32)) & (live > 0.5) & (earlier == (slot & 1).astype(F32))
    ).astype(F32)
    returned = narrow_to_wide(returned_ref, narrow_s).astype(BF)
    rows = dot(chosen.astype(BF), returned).astype(BF)
    for x in range(4):
        out_ref[x] = rows


def carry_kernel(rows_ref, own_in_ref, near_in_ref, own_ref, near_ref):
    own_ref[...] = dot_nt(rows_ref[...], own_in_ref[...]).astype(BF)
    near_ref[...] = dot_nt(rows_ref[...], near_in_ref[...]).astype(BF)


def depth_kernel(slots_ref, codes_ref, cot_ref, gain_ref, *refs):
    pieces, refs = refs[:SEQ], refs[SEQ:]
    (
        out_ref,
        weights_s,
        hidden_s,
        cot_s,
        mixed_s,
        projected_s,
        grads_s,
        narrow_s,
        codes_s,
        given_s,
        sems,
    ) = refs
    copies = [
        pltpu.make_async_copy(codes_ref, codes_s, sems.at[0]),
        pltpu.make_async_copy(cot_ref, given_s, sems.at[1]),
    ]
    for part, piece in zip(parts_held(), pieces):
        goal = weights_s.at[pl.ds(pl.multiple_of(part * 128, 128), 128), :]
        copies.append(pltpu.make_async_copy(piece, goal, sems.at[len(copies)]))
    for copy in copies:
        copy.start()

    slots = narrow_to_wide(slots_ref, narrow_s).astype(BF)
    live_col = (slots[:, 0:1].astype(F32) < EMPTY * 0.5).astype(F32)
    down = iota((SLOTS, SLOTS), 0)
    across = iota((SLOTS, SLOTS), 1)
    live_row = jnp.sum(jnp.where(down == across, live_col, 0.0), axis=0, keepdims=True)
    rank_row = jnp.sum(jnp.where(down < across, live_col, 0.0), axis=0, keepdims=True)
    rank_col = jnp.sum(jnp.where(across < down, live_row, 0.0), axis=1, keepdims=True)

    spread = (
        (live_row > 0.5) & (rank_row == (iota((PADDED, SLOTS), 0) >> 3).astype(F32))
    ).astype(F32)
    spare = jnp.zeros((PADDED - ROWS, D_DEP), F32)
    copies[0].wait()
    hidden = dot(spread.astype(BF), slots) + jnp.concatenate(
        [codes_s[...].astype(F32), spare], axis=0
    )
    hidden_s[...] = hidden
    copies[1].wait()
    cot_s[...] = jnp.concatenate([given_s[...].astype(F32), spare], axis=0)
    gain = gain_ref[...].astype(F32)
    scale = lax.rsqrt(jnp.sum(hidden * hidden, axis=1, keepdims=True) * (1.0 / D_DEP) + 1e-05)
    normed = (hidden * scale * gain).astype(BF)
    for copy in copies[2:]:
        copy.wait()
    width = DHEADS * DHEAD
    w_out = weights_s[:, 3 * width :].reshape(SEQ, 2, DHEAD, width)
    mixed_grad = dot_nt(cot_s[:, :width].astype(BF), w_out[:, 0].reshape(width, width))
    mixed_grad += dot_nt(cot_s[:, width:].astype(BF), w_out[:, 1].reshape(width, width))
    mixed_s[...] = mixed_grad.astype(BF)
    projected_s[...] = dot(normed, weights_s[:, : 3 * width]).astype(BF)

    first_half = iota((GROUP, 128), 1) < DHEAD
    nothing = jnp.zeros((GROUP, 128), BF)
    frame = iota((GROUP // CODES, CODES, 2 * GROUP), 0)
    row = iota((GROUP // CODES, CODES, 2 * GROUP), 2) & (GROUP - 1)
    same_frame = frame == (row >> 3)

    def halves(array):
        return jnp.concatenate(
            [jnp.where(first_half, array, nothing), jnp.where(first_half, nothing, array)], axis=0
        )

    def own_frame(array):
        blocks = array.reshape(GROUP // CODES, CODES, 2 * GROUP)
        return jnp.sum(jnp.where(same_frame, blocks, 0.0), axis=0)

    def all_frames(array):
        blocks = jnp.where(same_frame, array[None], 0.0)
        return blocks.reshape(GROUP, 2 * GROUP).astype(BF)

    units = [
        (slice(group * GROUP, (group + 1) * GROUP), pair * 128)
        for group in range(PADDED // GROUP)
        for pair in range(DHEADS // 2)
    ]
    scores, weight_grad = [], []
    for rows, lanes in units:
        key = projected_s[rows, width + lanes : width + lanes + 128]
        value = projected_s[rows, 2 * width + lanes : 2 * width + lanes + 128]
        scores.append(own_frame(dot_nt(key, halves(projected_s[rows, lanes : lanes + 128]))))
        weight_grad.append(own_frame(dot_nt(value, halves(mixed_s[rows, lanes : lanes + 128]))))
    scores = jnp.concatenate(scores, axis=1) * DHEAD ** (-0.5)
    scores = jnp.where((iota(scores.shape, 0) <= (iota(scores.shape, 1) & 7)), scores, -1e30)
    raised = jnp.exp(scores - jnp.max(scores, axis=0, keepdims=True))
    weights = raised * (1.0 / jnp.sum(raised, axis=0, keepdims=True))
    weight_grad = jnp.concatenate(weight_grad, axis=1).astype(BF).astype(F32)
    inner = jnp.sum(weight_grad * weights, axis=0, keepdims=True)
    score_grad = weights * (weight_grad - inner) * DHEAD ** (-0.5)
    for place, (rows, lanes) in enumerate(units):
        own = slice(place * 2 * GROUP, (place + 1) * 2 * GROUP)
        back = all_frames(score_grad[:, own])
        query_grad = dot_tn(back, projected_s[rows, width + lanes : width + lanes + 128])
        grads_s[rows, lanes : lanes + 128] = jnp.where(
            first_half, query_grad[:GROUP], query_grad[GROUP:]
        ).astype(BF)
        grads_s[rows, width + lanes : width + lanes + 128] = dot(
            back, halves(projected_s[rows, lanes : lanes + 128])
        ).astype(BF)
        grads_s[rows, 2 * width + lanes : 2 * width + lanes + 128] = dot(
            all_frames(weights[:, own]), halves(mixed_s[rows, lanes : lanes + 128])
        ).astype(BF)
    normed_grad = dot_nt(grads_s[...], weights_s[:, : 3 * width]).astype(BF).astype(F32) * gain
    hidden = hidden_s[...]
    inner = jnp.sum(normed_grad * hidden, axis=1, keepdims=True) * (1.0 / D_DEP)
    hidden_grad = cot_s[...] + scale * normed_grad - hidden * (scale * scale * scale * inner)
    frames = jnp.sum(hidden_grad.reshape(FRAMES, CODES, D_DEP), axis=1)

    back = ((live_col > 0.5) & (rank_col == iota((SLOTS, FRAMES), 1).astype(F32))).astype(F32)
    wide_to_narrow(dot(back.astype(BF), frames.astype(BF)), out_ref, narrow_s)


def depth_scratch():
    width = DHEADS * DHEAD
    return [
        pltpu.VMEM((D_DEP, 4 * width), BF),
        pltpu.VMEM((PADDED, D_DEP), F32),
        pltpu.VMEM((PADDED, D_DEP), F32),
        pltpu.VMEM((PADDED, width), BF),
        pltpu.VMEM((PADDED, 3 * width), BF),
        pltpu.VMEM((PADDED, 3 * width), BF),
        pltpu.VMEM((SLOTS * 8, 128), F32),
        pltpu.VMEM((ROWS, D_DEP), BF),
        pltpu.VMEM((ROWS, D_DEP), BF),
        pltpu.SemaphoreType.DMA((SEQ + 2,)),
    ]


def exchange(array, axis):
    return lax.all_to_all(array, axis, split_axis=0, concat_axis=0, tiled=True)


def moved(array, axis, size, shift):
    return lax.ppermute(array, axis, [(i, (i + shift) % size) for i in range(size)])


def shards(
    queries,
    keys,
    values,
    text_grad,
    active,
    target,
    codes,
    depth_cot,
    w_in,
    norm_gain,
    w_qkv,
    w_out,
):
    seq = ("x", "core")
    owner = ("y", "z")
    mine = jnp.concatenate([w_in, w_qkv, w_out]).reshape(1, 8, D_DEP)
    along_z = exchange(jnp.broadcast_to(mine, (16, 8, D_DEP)), "z").reshape(128, D_DEP)
    along_y = [along_z] + [moved(along_z, "y", 4, shift) for shift in SHIFTS[1:]]
    own_in, own_rest = call(
        weight_kernel,
        (jax.ShapeDtypeStruct((256, D_DEP), BF), jax.ShapeDtypeStruct((128, 2 * D_DEP), BF)),
        "sort_weights",
        scratch_shapes=[pltpu.VMEM((512, D_DEP), BF)],
    )(*along_y)
    rest = [own_rest] + [moved(own_rest, "x", 4, shift) for shift in SHIFTS[1:]]
    rest += [moved(piece, "core", 2, 1) for piece in rest]

    packed = call(pack_kernel, jax.ShapeDtypeStruct((SEQ, FRAMES, 4 * COLS), BF), "pack_heads")(
        queries[0], keys[0], values[0], text_grad[0]
    )
    packed = exchange(packed, seq).reshape(LENGTH, 4 * COLS)
    parts = call(
        forward_kernel,
        jax.ShapeDtypeStruct((LENGTH, D_DEP), BF),
        "attention_forward",
    )(packed, own_in)
    parts = exchange(parts.reshape(SEQ, FRAMES, D_DEP), seq)
    narrow = jax.ShapeDtypeStruct((SLOTS * 8, 128), BF)
    sent = call(
        send_kernel, narrow, "send_rows", scratch_shapes=[pltpu.VMEM((SLOTS * 8, 128), F32)]
    )(parts, target, active)
    slots = exchange(sent.reshape(OWNERS, 16, 128), owner).reshape(SLOTS * 8, 128)
    vmem = pl.BlockSpec(memory_space=pltpu.VMEM)
    anywhere = pl.BlockSpec(memory_space=pl.ANY)
    grads = call(
        depth_kernel,
        narrow,
        "depth_layer",
        in_specs=[vmem, anywhere, anywhere, vmem] + [anywhere] * SEQ,
        out_specs=vmem,
        scratch_shapes=depth_scratch(),
        vmem=58,
    )(
        slots,
        codes.reshape(ROWS, D_DEP),
        depth_cot.reshape(ROWS, D_DEP),
        norm_gain.reshape(1, D_DEP),
        *rest,
    )
    late_in, unused = lax.optimization_barrier((own_in, grads))
    near_in = moved(late_in, "core", 2, 1)
    returned = exchange(grads.reshape(OWNERS, 16, 128), owner).reshape(SLOTS * 8, 128)
    rows = call(
        return_kernel,
        jax.ShapeDtypeStruct((4, FRAMES, D_DEP), BF),
        "return_rows",
        scratch_shapes=[pltpu.VMEM((SLOTS * 8, 128), F32)],
    )(returned, target, active)
    rows = exchange(rows, "x").reshape(4 * FRAMES, D_DEP)
    half = jax.ShapeDtypeStruct((4 * FRAMES, COLS), BF)
    own_carried, near_carried = call(carry_kernel, (half, half), "context_grads")(
        rows, own_in, near_in
    )
    grads = call(
        backward_kernel,
        jax.ShapeDtypeStruct((LENGTH, 3 * COLS), BF),
        "attention_backward",
        scratch_shapes=[pltpu.VMEM((LENGTH, COLS), BF)],
    )(packed, own_carried, moved(near_carried, "core", 2, 1))
    grads = exchange(grads.reshape(SEQ, FRAMES, 3 * COLS), seq)
    shape = jax.ShapeDtypeStruct((FRAMES, D_CTX), BF)
    query_grad, key_grad, value_grad = call(unpack_kernel, (shape, shape, shape), "unpack_grads")(grads)
    return query_grad[None], key_grad[None], value_grad[None]


def solution(mesh):
    split = Mesh(mesh.devices.reshape(4, 2, 4, 16), ("x", "core", "y", "z"))
    rows = P(("y", "z"), ("x", "core"), None)
    frames = P(("y", "z"), ("x", "core"))
    code_rows = P(("y", "z"), ("x", "core"), None, None)
    flat = P(("x", "core", "y", "z"))
    in_specs = (
        rows,
        rows,
        rows,
        rows,
        frames,
        frames,
        code_rows,
        code_rows,
        flat,
        P(),
        flat,
        flat,
    )
    return jax.shard_map(
        shards, mesh=split, in_specs=in_specs, out_specs=(rows, rows, rows), check_vma=False
    )
```

time: 207 us -> 191 us (0.923)
  waiting for transfers between devices: 36.4 us -> 51.7 us
  blocking collectives: 29.8 us -> 15 us
  Pallas kernels: 29.5 us -> 22.7 us
  starting transfers between devices: 102 us -> 95.3 us
  local copies, waits for them, and re-layouts: 6.32 us -> 3.85 us
    all_to_all x2 -> x1, blocking collectives: 29.8 us -> 15 us  [exchange(): return lax.all_to_all(array, axis, split_axis=0, concat_axis=0, tiled=True)]
    all_to_all x5 -> x6, waiting for transfers between devices: 25.6 us -> 39.4 us  [exchange(): return lax.all_to_all(array, axis, split_axis=0, concat_axis=0, tiled=True)]
    ppermute x17 -> x12, starting transfers between devices: 49.4 us -> 41.4 us  [moved(): lax.ppermute(array, axis, [(i, (i + shift) % size) for i in range(size)])]
    pallas_call x5 -> x6, Pallas kernels: 23.2 us -> 16.4 us  [the longest x1 11.5 us: shards(): call(depth_kernel, narrow, 'depth_layer', in_specs=[vmem, anywhere, anywh...]
    reshape x4 -> x0, local copies, waits for them, and re-layouts: 3.7 us -> none  [the longest x1 1.05 us: shards(): exchange(sent.reshape(OWNERS, CAP, D_DEP), owner).reshape(SLOTS, D_DEP)]
    ppermute x17 -> x12, waiting for transfers between devices: 10.8 us -> 12.3 us  [moved(): lax.ppermute(array, axis, [(i, (i + shift) % size) for i in range(size)])]
    all_to_all x5 -> x6, starting transfers between devices: 52.7 us -> 54 us  [exchange(): return lax.all_to_all(array, axis, split_axis=0, concat_axis=0, tiled=True)]
  transfers between devices with their start and end apart: 22 -> 18, of which waited for: 7 -> 11; matrix products, arithmetic and copies ran while one was open for 2% -> 0% of each run, Pallas kernels for 10% -> 2%
where the time goes in v3:
time: 191 us; the launch traced here: 190 us
  starting transfers between devices  95.3 us (50%)
  waiting for transfers between devices  51.7 us (27%)
  Pallas kernels  22.7 us (12%)
  blocking collectives  15 us (8%)
  local copies, waits for them, and re-layouts  3.85 us (2%)
    all_to_all x6, starting transfers between devices, exchange(): return lax.all_to_all(array, axis, split_axis=0, concat_axis=0, tiled=True)  54 us
    ppermute x12, starting transfers between devices, moved(): lax.ppermute(array, axis, [(i, (i + shift) % size) for i in range(size)])  41.4 us
    all_to_all x6, waiting for transfers between devices, exchange(): return lax.all_to_all(array, axis, split_axis=0, concat_axis=0, tiled=True)  39.4 us
    all_to_all x1, blocking collectives, exchange(): return lax.all_to_all(array, axis, split_axis=0, concat_axis=0, tiled=True)  15 us
    ppermute x12, waiting for transfers between devices, moved(): lax.ppermute(array, axis, [(i, (i + shift) % size) for i in range(size)])  12.3 us
    pallas_call x1, Pallas kernels, shards(): call(depth_kernel, narrow, 'depth_layer', in_specs=[vmem, anywhere, anywh...  11.5 us
  transfers between devices with their start and end apart: 18, of which 11 were waited for; matrix products, arithmetic and copies ran while one was open for 0% of the time, Pallas kernels for 2%

profile of v3, /device:TPU:1, one launch (start us, length us, event | category | flops | bytes accessed | tf_op | source)
XLA Modules:
  0.0 190.2 jit_solution(11285676590473601018)
XLA Ops:
  2.1 15.9 %all-to-all-start.1 = ((bf16[16,8,1024]{2,1,0:T(8,128)(2,1)}), bf16[16,8,1024]{2,1,0:T(8,128)(2,1)S(1)}, u32[]{:S(2)}, u32[]{:S(2)}) async-start(bf16[16,8,1024]{2,1,0:T(8,128)(2,1)} %broadcast_in_dim.17), calls=%async_computation.1 | async-start | bytes 524288 | tf_op jit(solution)/shard_map/all_to_all | solution.py:344
  20.1 11.1 %all-to-all-done.1 = bf16[16,8,1024]{2,1,0:T(8,128)(2,1)S(1)} async-done(((bf16[16,8,1024]{2,1,0:T(8,128)(2,1)}), bf16[16,8,1024]{2,1,0:T(8,128)(2,1)S(1)}, u32[]{:S(2)}, u32[]{:S(2)}) %all-to-all-start.1) | async-done | bytes 262176 | tf_op jit(solution)/shard_map/all_to_all | solution.py:344
  31.1 10.5 %all-to-all-start = ((bf16[8,64,1024]{2,1,0:T(8,128)(2,1)}), bf16[8,64,1024]{2,1,0:T(8,128)(2,1)S(1)}, u32[]{:S(2)}, u32[]{:S(2)}) async-start(bf16[8,64,1024]{2,1,0:T(8,128)(2,1)} %pack_heads.1), calls=%async_computation | async-start | bytes 2097152 | tf_op jit(solution)/shard_map/all_to_all | solution.py:344
  41.6 3.2 %collective-permute-start = (bf16[128,1024]{1,0:T(8,128)(2,1)S(1)}, bf16[128,1024]{1,0:T(8,128)(2,1)S(1)}, u32[]{:S(2)}, u32[]{:S(2)}) collective-permute-start(bf16[128,1024]{1,0:T(8,128)(2,1)S(1)} %bitcast.23), channel_id=1, source_target_pairs={{0,16},{16,32},{32,48},{48,0},{1,17},{17,33},{33,49},{49,1},{2,18}... | collective-permute-start | bytes 786440 | tf_op jit(solution)/shard_map/ppermute | solution.py:348
  44.8 3.4 %collective-permute-start.1 = (bf16[128,1024]{1,0:T(8,128)(2,1)S(1)}, bf16[128,1024]{1,0:T(8,128)(2,1)S(1)}, u32[]{:S(2)}, u32[]{:S(2)}) collective-permute-start(bf16[128,1024]{1,0:T(8,128)(2,1)S(1)} %bitcast.24), channel_id=1, source_target_pairs={{0,48},{16,0},{32,16},{48,32},{1,49},{17,1},{33,17},{49,33},{2,50}... | collective-permute-start | bytes 786440 | tf_op jit(solution)/shard_map/ppermute | solution.py:348
  48.2 3.5 %collective-permute-start.2 = (bf16[128,1024]{1,0:T(8,128)(2,1)S(1)}, bf16[128,1024]{1,0:T(8,128)(2,1)S(1)}, u32[]{:S(2)}, u32[]{:S(2)}) collective-permute-start(bf16[128,1024]{1,0:T(8,128)(2,1)S(1)} %bitcast.25), channel_id=1, source_target_pairs={{0,32},{16,48},{32,0},{48,16},{1,33},{17,49},{33,1},{49,17},{2,34}... | collective-permute-start | bytes 786440 | tf_op jit(solution)/shard_map/ppermute | solution.py:348
  54.3 4.6 %collective-permute-done.2.refs_3_ = bf16[128,1024]{1,0:T(8,128)(2,1)S(1)} collective-permute-done((bf16[128,1024]{1,0:T(8,128)(2,1)S(1)}, bf16[128,1024]{1,0:T(8,128)(2,1)S(1)}, u32[]{:S(2)}, u32[]{:S(2)}) %collective-permute-start.2) | collective-permute-done | bytes 262176 | tf_op jit(solution)/shard_map/ppermute | solution.py:348
  60.1 3.0 %attention_forward.1 = bf16[512,1024]{1,0:T(8,128)(2,1)} custom-call(bf16[512,1024]{1,0:T(8,128)(2,1)S(1)} %bitcast.18, bf16[256,1024]{1,0:T(8,128)(2,1)S(1)} %get-tuple-element.13.w_in_ref.own_in_ref), custom_call_target="tpu_custom_call" | custom-call | tf_op jit(solution)/shard_map/attention_forward/pallas_call | solution.py:383
  63.1 5.8 %all-to-all-start.2 = ((bf16[8,64,1024]{2,1,0:T(8,128)(2,1)}), bf16[8,64,1024]{2,1,0:T(8,128)(2,1)S(1)}, u32[]{:S(2)}, u32[]{:S(2)}) async-start(bf16[8,64,1024]{2,1,0:T(8,128)(2,1)} %bitcast.6), calls=%async_computation.2 | async-start | bytes 2097152 | tf_op jit(solution)/shard_map/all_to_all | solution.py:344
  68.9 3.4 %collective-permute-start.3 = (bf16[128,2048]{1,0:T(8,128)(2,1)S(1)}, bf16[128,2048]{1,0:T(8,128)(2,1)}, u32[]{:S(2)}, u32[]{:S(2)}) collective-permute-start(bf16[128,2048]{1,0:T(8,128)(2,1)S(1)} %get-tuple-element.12.refs_0_), channel_id=1, source_target_pairs={{0,128},{128,256},{256,384},{384,0},{1,129},{129,257},{257,385},{3... | collective-permute-start | bytes 1572872 | tf_op jit(solution)/shard_map/ppermute | solution.py:348
  72.3 3.2 %collective-permute-start.4 = (bf16[128,2048]{1,0:T(8,128)(2,1)S(1)}, bf16[128,2048]{1,0:T(8,128)(2,1)}, u32[]{:S(2)}, u32[]{:S(2)}) collective-permute-start(bf16[128,2048]{1,0:T(8,128)(2,1)S(1)} %get-tuple-element.12.refs_0_), channel_id=1, source_target_pairs={{0,384},{128,0},{256,128},{384,256},{1,385},{129,1},{257,129},{385... | collective-permute-start | bytes 1572872 | tf_op jit(solution)/shard_map/ppermute | solution.py:348
  75.5 3.6 %collective-permute-start.5 = (bf16[128,2048]{1,0:T(8,128)(2,1)S(1)}, bf16[128,2048]{1,0:T(8,128)(2,1)}, u32[]{:S(2)}, u32[]{:S(2)}) collective-permute-start(bf16[128,2048]{1,0:T(8,128)(2,1)S(1)} %get-tuple-element.12.refs_0_), channel_id=1, source_target_pairs={{0,256},{128,384},{256,0},{384,128},{1,257},{129,385},{257,1},{385... | collective-permute-start | bytes 1572872 | tf_op jit(solution)/shard_map/ppermute | solution.py:348
  79.1 4.9 %all-to-all-done.2.parts_ref = bf16[8,64,1024]{2,1,0:T(8,128)(2,1)S(1)} async-done(((bf16[8,64,1024]{2,1,0:T(8,128)(2,1)}), bf16[8,64,1024]{2,1,0:T(8,128)(2,1)S(1)}, u32[]{:S(2)}, u32[]{:S(2)}) %all-to-all-start.2) | async-done | bytes 1048608 | tf_op jit(solution)/shard_map/all_to_all | solution.py:344
  85.2 9.7 %all-to-all-start.3 = ((bf16[64,16,128]{2,1,0:T(8,128)(2,1)}), bf16[64,16,128]{2,1,0:T(8,128)(2,1)S(1)}, u32[]{:S(2)}, u32[]{:S(2)}) async-start(bf16[64,16,128]{2,1,0:T(8,128)(2,1)} %bitcast.7), calls=%async_computation.3 | async-start | bytes 524288 | tf_op jit(solution)/shard_map/all_to_all | solution.py:344
  94.8 3.5 %collective-permute-start.6 = (bf16[128,2048]{1,0:T(8,128)(2,1)S(1)}, bf16[128,2048]{1,0:T(8,128)(2,1)S(1)}, u32[]{:S(2)}, u32[]{:S(2)}) collective-permute-start(bf16[128,2048]{1,0:T(8,128)(2,1)S(1)} %get-tuple-element.12.refs_0_), channel_id=1, source_target_pairs={{0,64},{64,0},{1,65},{65,1},{2,66},{66,2},{3,67},{67,3},{4,68},{68... | collective-permute-start | bytes 1572872 | tf_op jit(solution)/shard_map/ppermute | solution.py:348
  102.8 3.9 %collective-permute-done.5.refs_3_ = bf16[128,2048]{1,0:T(8,128)(2,1)} collective-permute-done((bf16[128,2048]{1,0:T(8,128)(2,1)S(1)}, bf16[128,2048]{1,0:T(8,128)(2,1)}, u32[]{:S(2)}, u32[]{:S(2)}) %collective-permute-start.5) | collective-permute-done | bytes 524320 | tf_op jit(solution)/shard_map/ppermute | solution.py:348
  113.8 11.5 %depth_layer.1 = bf16[1024,128]{1,0:T(8,128)(2,1)} custom-call(bf16[1024,128]{1,0:T(8,128)(2,1)} %bitcast.31, bf16[472,1024]{1,0:T(8,128)(2,1)} %bitcast.33, bf16[472,1024]{1,0:T(8,128)(2,1)} %bitcast.34, bf16[1,1024]{1,0:T(2,128)(2,1)} %reshape.51.gain_ref, bf16[128,2048]{1,0:T(8,128)(2,1)} %copy-done, bf16[128,2048]{1,0:T(8,128)(2,1)} %collective-permute-done.3.refs_1_, ...), custom_call_target="tpu_custom_call" | custom-call | tf_op jit(solution)/shard_map/depth_layer/pallas_call | solution.py:396
  125.3 8.7 %all-to-all-start.4 = ((bf16[64,16,128]{2,1,0:T(8,128)(2,1)}), bf16[64,16,128]{2,1,0:T(8,128)(2,1)S(1)}, u32[]{:S(2)}, u32[]{:S(2)}) async-start(bf16[64,16,128]{2,1,0:T(8,128)(2,1)} %bitcast.32), calls=%async_computation.4 | async-start | bytes 524288 | tf_op jit(solution)/shard_map/all_to_all | solution.py:344
  134.0 3.4 %collective-permute-start.10 = (bf16[256,1024]{1,0:T(8,128)(2,1)S(1)}, bf16[256,1024]{1,0:T(8,128)(2,1)S(1)}, u32[]{:S(2)}, u32[]{:S(2)}) collective-permute-start(bf16[256,1024]{1,0:T(8,128)(2,1)S(1)} %get-tuple-element.13.w_in_ref.own_in_ref), channel_id=1, source_target_pairs={{0,64},{64,0},{1,65},{65,1},{2,66},{66,2},{3,67},{67,3},{4,68},{68... | collective-permute-start | bytes 1572872 | tf_op jit(solution)/shard_map/ppermute | solution.py:348
  137.4 14.7 %all-to-all-done.4 = bf16[64,16,128]{2,1,0:T(8,128)(2,1)S(1)} async-done(((bf16[64,16,128]{2,1,0:T(8,128)(2,1)}), bf16[64,16,128]{2,1,0:T(8,128)(2,1)S(1)}, u32[]{:S(2)}, u32[]{:S(2)}) %all-to-all-start.4) | async-done | bytes 262176 | tf_op jit(solution)/shard_map/all_to_all | solution.py:344
  153.2 3.5 %all-to-all-start.5 = ((bf16[4,64,1024]{2,1,0:T(8,128)(2,1)}), bf16[4,64,1024]{2,1,0:T(8,128)(2,1)S(1)}, u32[]{:S(2)}, u32[]{:S(2)}) async-start(bf16[4,64,1024]{2,1,0:T(8,128)(2,1)} %return_rows.1), calls=%async_computation.5 | async-start | bytes 1048576 | tf_op jit(solution)/shard_map/all_to_all | solution.py:344
  156.7 6.9 %all-to-all-done.5 = bf16[4,64,1024]{2,1,0:T(8,128)(2,1)S(1)} async-done(((bf16[4,64,1024]{2,1,0:T(8,128)(2,1)}), bf16[4,64,1024]{2,1,0:T(8,128)(2,1)S(1)}, u32[]{:S(2)}, u32[]{:S(2)}) %all-to-all-start.5) | async-done | bytes 524320 | tf_op jit(solution)/shard_map/all_to_all | solution.py:344
  164.1 6.9 %collective-permute-start.11 = (bf16[256,256]{1,0:T(8,128)(2,1)S(1)}, bf16[256,256]{1,0:T(8,128)(2,1)S(1)}, u32[]{:S(2)}, u32[]{:S(2)}) collective-permute-start(bf16[256,256]{1,0:T(8,128)(2,1)S(1)} %get-tuple-element.15), channel_id=1, source_target_pairs={{0,64},{64,0},{1,65},{65,1},{2,66},{66,2},{3,67},{67,3},{4,68},{68... | collective-permute-start | bytes 393224 | tf_op jit(solution)/shard_map/ppermute | solution.py:348
  174.3 15.0 %all_to_all.35.packed_ref = bf16[8,64,768]{2,1,0:T(8,128)(2,1)S(1)} all-to-all(bf16[8,64,768]{2,1,0:T(8,128)(2,1)S(1)} %bitcast.20), channel_id=1, replica_groups=mesh['x'=4,'core'=2,'y'=4,'z'=16] {'x','core'}, dimensions={0} | all-to-all | bytes 1572864 | tf_op jit(solution)/shard_map/all_to_all | solution.py:344
  (50 shorter events, 25.6 us)
Async XLA Ops:
  1.4 16.6 %copy-start.3 = (bf16[1,64,2048]{2,1,0:T(8,128)(2,1)S(1)}, bf16[1,64,2048]{2,1,0:T(8,128)(2,1)}, u32[]{:S(2)}) copy-start(bf16[1,64,2048]{2,1,0:T(8,128)(2,1)} %param.14) | copy-start | bytes 786436
  2.1 15.9 %copy-start.1 = (bf16[1,64,2048]{2,1,0:T(8,128)(2,1)S(1)}, bf16[1,64,2048]{2,1,0:T(8,128)(2,1)}, u32[]{:S(2)}) copy-start(bf16[1,64,2048]{2,1,0:T(8,128)(2,1)} %param.12) | copy-start | bytes 786436
  2.1 15.9 %copy-start.2 = (bf16[1,64,2048]{2,1,0:T(8,128)(2,1)S(1)}, bf16[1,64,2048]{2,1,0:T(8,128)(2,1)}, u32[]{:S(2)}) copy-start(bf16[1,64,2048]{2,1,0:T(8,128)(2,1)} %param.13) | copy-start | bytes 786436
  2.1 29.0 %all-to-all-start.1 = ((bf16[16,8,1024]{2,1,0:T(8,128)(2,1)}), bf16[16,8,1024]{2,1,0:T(8,128)(2,1)S(1)}, u32[]{:S(2)}, u32[]{:S(2)}) async-start(bf16[16,8,1024]{2,1,0:T(8,128)(2,1)} %broadcast_in_dim.17), calls=%async_computation.1 | async-start | bytes 524288 | tf_op jit(solution)/shard_map/all_to_all | solution.py:344
  31.1 29.0 %all-to-all-start = ((bf16[8,64,1024]{2,1,0:T(8,128)(2,1)}), bf16[8,64,1024]{2,1,0:T(8,128)(2,1)S(1)}, u32[]{:S(2)}, u32[]{:S(2)}) async-start(bf16[8,64,1024]{2,1,0:T(8,128)(2,1)} %pack_heads.1), calls=%async_computation | async-start | bytes 2097152 | tf_op jit(solution)/shard_map/all_to_all | solution.py:344
  41.6 11.2 %collective-permute-start = (bf16[128,1024]{1,0:T(8,128)(2,1)S(1)}, bf16[128,1024]{1,0:T(8,128)(2,1)S(1)}, u32[]{:S(2)}, u32[]{:S(2)}) collective-permute-start(bf16[128,1024]{1,0:T(8,128)(2,1)S(1)} %bitcast.23), channel_id=1, source_target_pairs={{0,16},{16,32},{32,48},{48,0},{1,17},{17,33},{33,49},{49,1},{2,18}... | collective-permute-start | bytes 786440 | tf_op jit(solution)/shard_map/ppermute | solution.py:348
  44.8 9.5 %collective-permute-start.1 = (bf16[128,1024]{1,0:T(8,128)(2,1)S(1)}, bf16[128,1024]{1,0:T(8,128)(2,1)S(1)}, u32[]{:S(2)}, u32[]{:S(2)}) collective-permute-start(bf16[128,1024]{1,0:T(8,128)(2,1)S(1)} %bitcast.24), channel_id=1, source_target_pairs={{0,48},{16,0},{32,16},{48,32},{1,49},{17,1},{33,17},{49,33},{2,50}... | collective-permute-start | bytes 786440 | tf_op jit(solution)/shard_map/ppermute | solution.py:348
  48.2 10.8 %collective-permute-start.2 = (bf16[128,1024]{1,0:T(8,128)(2,1)S(1)}, bf16[128,1024]{1,0:T(8,128)(2,1)S(1)}, u32[]{:S(2)}, u32[]{:S(2)}) collective-permute-start(bf16[128,1024]{1,0:T(8,128)(2,1)S(1)} %bitcast.25), channel_id=1, source_target_pairs={{0,32},{16,48},{32,0},{48,16},{1,33},{17,49},{33,1},{49,17},{2,34}... | collective-permute-start | bytes 786440 | tf_op jit(solution)/shard_map/ppermute | solution.py:348
  60.1 34.7 %copy-start = (bf16[128,2048]{1,0:T(8,128)(2,1)}, bf16[128,2048]{1,0:T(8,128)(2,1)S(1)}, u32[]{:S(2)}) copy-start(bf16[128,2048]{1,0:T(8,128)(2,1)S(1)} %get-tuple-element.12.refs_0_) | copy-start | bytes 1572868
  63.1 20.9 %all-to-all-start.2 = ((bf16[8,64,1024]{2,1,0:T(8,128)(2,1)}), bf16[8,64,1024]{2,1,0:T(8,128)(2,1)S(1)}, u32[]{:S(2)}, u32[]{:S(2)}) async-start(bf16[8,64,1024]{2,1,0:T(8,128)(2,1)} %bitcast.6), calls=%async_computation.2 | async-start | bytes 2097152 | tf_op jit(solution)/shard_map/all_to_all | solution.py:344
  68.9 15.2 %copy-start.6 = (s32[1,64]{1,0:T(1,128)S(1)}, s32[1,64]{1,0:T(1,128)}, u32[]{:S(2)}) copy-start(s32[1,64]{1,0:T(1,128)} %active_ref.3) | copy-start | bytes 772
  68.9 29.5 %collective-permute-start.3 = (bf16[128,2048]{1,0:T(8,128)(2,1)S(1)}, bf16[128,2048]{1,0:T(8,128)(2,1)}, u32[]{:S(2)}, u32[]{:S(2)}) collective-permute-start(bf16[128,2048]{1,0:T(8,128)(2,1)S(1)} %get-tuple-element.12.refs_0_), channel_id=1, source_target_pairs={{0,128},{128,256},{256,384},{384,0},{1,129},{129,257},{257,385},{3... | collective-permute-start | bytes 1572872 | tf_op jit(solution)/shard_map/ppermute | solution.py:348
  72.3 28.0 %collective-permute-start.4 = (bf16[128,2048]{1,0:T(8,128)(2,1)S(1)}, bf16[128,2048]{1,0:T(8,128)(2,1)}, u32[]{:S(2)}, u32[]{:S(2)}) collective-permute-start(bf16[128,2048]{1,0:T(8,128)(2,1)S(1)} %get-tuple-element.12.refs_0_), channel_id=1, source_target_pairs={{0,384},{128,0},{256,128},{384,256},{1,385},{129,1},{257,129},{385... | collective-permute-start | bytes 1572872 | tf_op jit(solution)/shard_map/ppermute | solution.py:348
  75.5 31.1 %collective-permute-start.5 = (bf16[128,2048]{1,0:T(8,128)(2,1)S(1)}, bf16[128,2048]{1,0:T(8,128)(2,1)}, u32[]{:S(2)}, u32[]{:S(2)}) collective-permute-start(bf16[128,2048]{1,0:T(8,128)(2,1)S(1)} %get-tuple-element.12.refs_0_), channel_id=1, source_target_pairs={{0,256},{128,384},{256,0},{384,128},{1,257},{129,385},{257,1},{385... | collective-permute-start | bytes 1572872 | tf_op jit(solution)/shard_map/ppermute | solution.py:348
  85.2 24.4 %copy-start.11 = (bf16[1024]{0:T(1024)(128)(2,1)S(1)}, bf16[1024]{0:T(1024)(128)(2,1)}, u32[]{:S(2)}) copy-start(bf16[1024]{0:T(1024)(128)(2,1)} %param.21) | copy-start | bytes 6148
  85.2 27.9 %all-to-all-start.3 = ((bf16[64,16,128]{2,1,0:T(8,128)(2,1)}), bf16[64,16,128]{2,1,0:T(8,128)(2,1)S(1)}, u32[]{:S(2)}, u32[]{:S(2)}) async-start(bf16[64,16,128]{2,1,0:T(8,128)(2,1)} %bitcast.7), calls=%async_computation.3 | async-start | bytes 524288 | tf_op jit(solution)/shard_map/all_to_all | solution.py:344
  94.8 15.4 %collective-permute-start.6 = (bf16[128,2048]{1,0:T(8,128)(2,1)S(1)}, bf16[128,2048]{1,0:T(8,128)(2,1)S(1)}, u32[]{:S(2)}, u32[]{:S(2)}) collective-permute-start(bf16[128,2048]{1,0:T(8,128)(2,1)S(1)} %get-tuple-element.12.refs_0_), channel_id=1, source_target_pairs={{0,64},{64,0},{1,65},{65,1},{2,66},{66,2},{3,67},{67,3},{4,68},{68... | collective-permute-start | bytes 1572872 | tf_op jit(solution)/shard_map/ppermute | solution.py:348
  98.4 11.8 %collective-permute-start.7 = (bf16[128,2048]{1,0:T(8,128)(2,1)}, bf16[128,2048]{1,0:T(8,128)(2,1)S(1)}, u32[]{:S(2)}, u32[]{:S(2)}) collective-permute-start(bf16[128,2048]{1,0:T(8,128)(2,1)} %collective-permute-done.3.refs_1_), channel_id=1, source_target_pairs={{0,64},{64,0},{1,65},{65,1},{2,66},{66,2},{3,67},{67,3},{4,68},{68... | collective-permute-start | bytes 1572872 | tf_op jit(solution)/shard_map/ppermute | solution.py:348
  100.3 9.9 %collective-permute-start.8 = (bf16[128,2048]{1,0:T(8,128)(2,1)}, bf16[128,2048]{1,0:T(8,128)(2,1)S(1)}, u32[]{:S(2)}, u32[]{:S(2)}) collective-permute-start(bf16[128,2048]{1,0:T(8,128)(2,1)} %collective-permute-done.4.refs_2_), channel_id=1, source_target_pairs={{0,64},{64,0},{1,65},{65,1},{2,66},{66,2},{3,67},{67,3},{4,68},{68... | collective-permute-start | bytes 1572872 | tf_op jit(solution)/shard_map/ppermute | solution.py:348
  106.6 4.6 %collective-permute-start.9 = (bf16[128,2048]{1,0:T(8,128)(2,1)}, bf16[128,2048]{1,0:T(8,128)(2,1)}, u32[]{:S(2)}, u32[]{:S(2)}) collective-permute-start(bf16[128,2048]{1,0:T(8,128)(2,1)} %collective-permute-done.5.refs_3_), channel_id=1, source_target_pairs={{0,64},{64,0},{1,65},{65,1},{2,66},{66,2},{3,67},{67,3},{4,68},{68... | collective-permute-start | bytes 1572872 | tf_op jit(solution)/shard_map/ppermute | solution.py:348
  125.3 26.8 %all-to-all-start.4 = ((bf16[64,16,128]{2,1,0:T(8,128)(2,1)}), bf16[64,16,128]{2,1,0:T(8,128)(2,1)S(1)}, u32[]{:S(2)}, u32[]{:S(2)}) async-start(bf16[64,16,128]{2,1,0:T(8,128)(2,1)} %bitcast.32), calls=%async_computation.4 | async-start | bytes 524288 | tf_op jit(solution)/shard_map/all_to_all | solution.py:344
  134.0 22.7 %collective-permute-start.10 = (bf16[256,1024]{1,0:T(8,128)(2,1)S(1)}, bf16[256,1024]{1,0:T(8,128)(2,1)S(1)}, u32[]{:S(2)}, u32[]{:S(2)}) collective-permute-start(bf16[256,1024]{1,0:T(8,128)(2,1)S(1)} %get-tuple-element.13.w_in_ref.own_in_ref), channel_id=1, source_target_pairs={{0,64},{64,0},{1,65},{65,1},{2,66},{66,2},{3,67},{67,3},{4,68},{68... | collective-permute-start | bytes 1572872 | tf_op jit(solution)/shard_map/ppermute | solution.py:348
  153.2 10.4 %all-to-all-start.5 = ((bf16[4,64,1024]{2,1,0:T(8,128)(2,1)}), bf16[4,64,1024]{2,1,0:T(8,128)(2,1)S(1)}, u32[]{:S(2)}, u32[]{:S(2)}) async-start(bf16[4,64,1024]{2,1,0:T(8,128)(2,1)} %return_rows.1), calls=%async_computation.5 | async-start | bytes 1048576 | tf_op jit(solution)/shard_map/all_to_all | solution.py:344
  164.1 7.9 %collective-permute-start.11 = (bf16[256,256]{1,0:T(8,128)(2,1)S(1)}, bf16[256,256]{1,0:T(8,128)(2,1)S(1)}, u32[]{:S(2)}, u32[]{:S(2)}) collective-permute-start(bf16[256,256]{1,0:T(8,128)(2,1)S(1)} %get-tuple-element.15), channel_id=1, source_target_pairs={{0,64},{64,0},{1,65},{65,1},{2,66},{66,2},{3,67},{67,3},{4,68},{68... | collective-permute-start | bytes 393224 | tf_op jit(solution)/shard_map/ppermute | solution.py:348
  (6 other events, 23.4 us)

commit v4 on v3

--- a/solution.py
+++ b/solution.py
@@ -86,13 +86,17 @@
         rest_ref[:, place * 512 : (place + 1) * 512] = new.astype(BF)
 
 
+def seq_index():
+    return lax.axis_index("x") * 2 + lax.axis_index("core")
+
+
 def pack_kernel(*refs):
-    ins, out_ref = refs[:4], refs[4]
-    for part in range(SEQ):
+    ins, outs = refs[:4], refs[4:]
+    here = seq_index()
+    for shift, out_ref in enumerate(outs):
+        start = pl.multiple_of(((here + shift) & 7) * COLS, COLS)
         for place, ref in enumerate(ins):
-            out_ref[part, :, place * COLS : (place + 1) * COLS] = ref[
-                :, part * COLS : (part + 1) * COLS
-            ]
+            out_ref[:, place * COLS : (place + 1) * COLS] = ref[:, pl.ds(start, COLS)]
 
 
 def unpack_kernel(packed_ref, first_ref, second_ref, third_ref):
@@ -116,14 +120,19 @@
     return query, key, value, weights
 
 
-def forward_kernel(packed_ref, w_in_ref, out_ref):
-    total = None
+def forward_kernel(*refs):
+    pieces, packed_ref, context_ref = refs[:SEQ], refs[SEQ], refs[SEQ + 1]
+    here = seq_index()
+    for shift, piece in enumerate(pieces):
+        start = pl.multiple_of(((here + SEQ - shift) & 7) * FRAMES, FRAMES)
+        packed_ref[pl.ds(start, FRAMES), :] = piece[...]
     for head in range(2):
         unused_q, unused_k, value, weights = head_weights(packed_ref, head)
-        context = dot(weights.astype(BF), value).astype(BF)
-        part = dot(context, w_in_ref[head * HEAD : (head + 1) * HEAD, :])
-        total = part if total is None else total + part
-    out_ref[...] = total.astype(BF)
+        context_ref[:, head * HEAD : (head + 1) * HEAD] = dot(weights.astype(BF), value).astype(BF)
+
+
+def enter_kernel(context_ref, w_in_ref, out_ref):
+    out_ref[...] = dot(context_ref[...], w_in_ref[...]).astype(BF)
 
 
 def backward_kernel(packed_ref, own_ref, near_ref, out_ref, grad_s):
@@ -376,15 +385,22 @@
     rest = [own_rest] + [moved(own_rest, "x", 4, shift) for shift in SHIFTS[1:]]
     rest += [moved(piece, "core", 2, 1) for piece in rest]
 
-    packed = call(pack_kernel, jax.ShapeDtypeStruct((SEQ, FRAMES, 4 * COLS), BF), "pack_heads")(
+    block = jax.ShapeDtypeStruct((FRAMES, 4 * COLS), BF)
+    blocks = call(pack_kernel, [block] * SEQ, "pack_heads")(
         queries[0], keys[0], values[0], text_grad[0]
     )
-    packed = exchange(packed, seq).reshape(LENGTH, 4 * COLS)
-    parts = call(
+    blocks = [blocks[0]] + [moved(blocks[k], seq, SEQ, k) for k in range(1, SEQ)]
+    packed, context = call(
         forward_kernel,
-        jax.ShapeDtypeStruct((LENGTH, D_DEP), BF),
+        (
+            jax.ShapeDtypeStruct((LENGTH, 4 * COLS), BF),
+            jax.ShapeDtypeStruct((LENGTH, COLS), BF),
+        ),
         "attention_forward",
-    )(packed, own_in)
+    )(*blocks)
+    parts = call(enter_kernel, jax.ShapeDtypeStruct((LENGTH, D_DEP), BF), "enter_depth")(
+        context, own_in
+    )
     parts = exchange(parts.reshape(SEQ, FRAMES, D_DEP), seq)
     narrow = jax.ShapeDtypeStruct((SLOTS * 8, 128), BF)
     sent = call(

time: 191 us -> 188 us (0.984)
  waiting for transfers between devices: 51.7 us -> 36.3 us
  starting transfers between devices: 95.3 us -> 108 us
    ppermute x12 -> x19, starting transfers between devices: 41.4 us -> 64.3 us  [moved(): lax.ppermute(array, axis, [(i, (i + shift) % size) for i in range(size)])]
    all_to_all x6 -> x5, waiting for transfers between devices: 39.4 us -> 29 us  [exchange(): return lax.all_to_all(array, axis, split_axis=0, concat_axis=0, tiled=True)]
    all_to_all x6 -> x5, starting transfers between devices: 54 us -> 43.7 us  [exchange(): return lax.all_to_all(array, axis, split_axis=0, concat_axis=0, tiled=True)]
    ppermute x12 -> x19, waiting for transfers between devices: 12.3 us -> 7.33 us  [moved(): lax.ppermute(array, axis, [(i, (i + shift) % size) for i in range(size)])]
    pallas_call x2 -> x3, Pallas kernels: 4.09 us -> 2.93 us  [the longest x1 1.44 us: shards(): call(enter_kernel, jax.ShapeDtypeStruct((LENGTH, D_DEP), BF), 'enter_depth')]
  transfers between devices with their start and end apart: 18 -> 24, of which waited for: 11 -> 7; matrix products, arithmetic and copies ran while one was open for 0% -> 0% of each run, Pallas kernels for 2% -> 2%
where the time goes in v4:
time: 188 us; the launch traced here: 187 us
  starting transfers between devices  108 us (57%)
  waiting for transfers between devices  36.3 us (19%)
  Pallas kernels  21.5 us (11%)
  blocking collectives  15 us (8%)
  local copies, waits for them, and re-layouts  4.63 us (2%)
    ppermute x19, starting transfers between devices, moved(): lax.ppermute(array, axis, [(i, (i + shift) % size) for i in range(size)])  64.3 us
    all_to_all x5, starting transfers between devices, exchange(): return lax.all_to_all(array, axis, split_axis=0, concat_axis=0, tiled=True)  43.7 us
    all_to_all x5, waiting for transfers between devices, exchange(): return lax.all_to_all(array, axis, split_axis=0, concat_axis=0, tiled=True)  29 us
    all_to_all x1, blocking collectives, exchange(): return lax.all_to_all(array, axis, split_axis=0, concat_axis=0, tiled=True)  15 us
    pallas_call x1, Pallas kernels, shards(): call(depth_kernel, narrow, 'depth_layer', in_specs=[vmem, anywhere, anywh...  11.5 us
    ppermute x19, waiting for transfers between devices, moved(): lax.ppermute(array, axis, [(i, (i + shift) % size) for i in range(size)])  7.33 us
  transfers between devices with their start and end apart: 24, of which 7 were waited for; matrix products, arithmetic and copies ran while one was open for 0% of the time, Pallas kernels for 2%

profile of v4, /device:TPU:1, one launch (start us, length us, event | category | flops | bytes accessed | tf_op | source)
XLA Modules:
  0.0 187.2 jit_solution(3745762734344242577)
XLA Ops:
  2.1 15.9 %all-to-all-start = ((bf16[16,8,1024]{2,1,0:T(8,128)(2,1)}), bf16[16,8,1024]{2,1,0:T(8,128)(2,1)S(1)}, u32[]{:S(2)}, u32[]{:S(2)}) async-start(bf16[16,8,1024]{2,1,0:T(8,128)(2,1)} %broadcast_in_dim.17), calls=%async_computation | async-start | bytes 524288 | tf_op jit(solution)/shard_map/all_to_all | solution.py:353
  21.2 3.1 %collective-permute-start.1 = (bf16[64,1024]{1,0:T(8,128)(2,1)S(1)}, bf16[64,1024]{1,0:T(8,128)(2,1)S(1)}, u32[]{:S(2)}, u32[]{:S(2)}) collective-permute-start(bf16[64,1024]{1,0:T(8,128)(2,1)S(1)} %get-tuple-element.23), channel_id=1, source_target_pairs={{0,128},{64,192},{128,256},{192,320},{256,384},{320,448},{384,0},{... | collective-permute-start | bytes 393224 | tf_op jit(solution)/shard_map/ppermute | solution.py:357
  24.3 3.5 %collective-permute-start.2 = (bf16[64,1024]{1,0:T(8,128)(2,1)S(1)}, bf16[64,1024]{1,0:T(8,128)(2,1)S(1)}, u32[]{:S(2)}, u32[]{:S(2)}) collective-permute-start(bf16[64,1024]{1,0:T(8,128)(2,1)S(1)} %get-tuple-element.24), channel_id=1, source_target_pairs={{0,192},{64,256},{128,320},{192,384},{256,448},{320,0},{384,64},{4... | collective-permute-start | bytes 393224 | tf_op jit(solution)/shard_map/ppermute | solution.py:357
  30.2 3.9 %collective-permute-start.4 = (bf16[64,1024]{1,0:T(8,128)(2,1)S(1)}, bf16[64,1024]{1,0:T(8,128)(2,1)S(1)}, u32[]{:S(2)}, u32[]{:S(2)}) collective-permute-start(bf16[64,1024]{1,0:T(8,128)(2,1)S(1)} %get-tuple-element.26), channel_id=1, source_target_pairs={{0,320},{64,384},{128,448},{192,0},{256,64},{320,128},{384,192},{4... | collective-permute-start | bytes 393224 | tf_op jit(solution)/shard_map/ppermute | solution.py:357
  34.2 3.2 %collective-permute-start.7 = (bf16[128,1024]{1,0:T(8,128)(2,1)S(1)}, bf16[128,1024]{1,0:T(8,128)(2,1)S(1)}, u32[]{:S(2)}, u32[]{:S(2)}) collective-permute-start(bf16[128,1024]{1,0:T(8,128)(2,1)S(1)} %bitcast.20), channel_id=1, source_target_pairs={{0,16},{16,32},{32,48},{48,0},{1,17},{17,33},{33,49},{49,1},{2,18}... | collective-permute-start | bytes 786440 | tf_op jit(solution)/shard_map/ppermute | solution.py:357
  37.4 3.4 %collective-permute-start.8 = (bf16[128,1024]{1,0:T(8,128)(2,1)S(1)}, bf16[128,1024]{1,0:T(8,128)(2,1)S(1)}, u32[]{:S(2)}, u32[]{:S(2)}) collective-permute-start(bf16[128,1024]{1,0:T(8,128)(2,1)S(1)} %bitcast.21), channel_id=1, source_target_pairs={{0,48},{16,0},{32,16},{48,32},{1,49},{17,1},{33,17},{49,33},{2,50}... | collective-permute-start | bytes 786440 | tf_op jit(solution)/shard_map/ppermute | solution.py:357
  40.8 3.5 %collective-permute-start.9 = (bf16[128,1024]{1,0:T(8,128)(2,1)S(1)}, bf16[128,1024]{1,0:T(8,128)(2,1)S(1)}, u32[]{:S(2)}, u32[]{:S(2)}) collective-permute-start(bf16[128,1024]{1,0:T(8,128)(2,1)S(1)} %bitcast.22), channel_id=1, source_target_pairs={{0,32},{16,48},{32,0},{48,16},{1,33},{17,49},{33,1},{49,17},{2,34}... | collective-permute-start | bytes 786440 | tf_op jit(solution)/shard_map/ppermute | solution.py:357
  46.9 6.1 %collective-permute-start.6 = (bf16[64,1024]{1,0:T(8,128)(2,1)S(1)}, bf16[64,1024]{1,0:T(8,128)(2,1)S(1)}, u32[]{:S(2)}, u32[]{:S(2)}) collective-permute-start(bf16[64,1024]{1,0:T(8,128)(2,1)S(1)} %get-tuple-element.28), channel_id=1, source_target_pairs={{0,448},{64,0},{128,64},{192,128},{256,192},{320,256},{384,320},{4... | collective-permute-start | bytes 393224 | tf_op jit(solution)/shard_map/ppermute | solution.py:357
  59.9 5.4 %all-to-all-start.1 = ((bf16[8,64,1024]{2,1,0:T(8,128)(2,1)}), bf16[8,64,1024]{2,1,0:T(8,128)(2,1)S(1)}, u32[]{:S(2)}, u32[]{:S(2)}) async-start(bf16[8,64,1024]{2,1,0:T(8,128)(2,1)} %bitcast.5), calls=%async_computation.1 | async-start | bytes 2097152 | tf_op jit(solution)/shard_map/all_to_all | solution.py:353
  65.2 3.4 %collective-permute-start.10 = (bf16[128,2048]{1,0:T(8,128)(2,1)S(1)}, bf16[128,2048]{1,0:T(8,128)(2,1)}, u32[]{:S(2)}, u32[]{:S(2)}) collective-permute-start(bf16[128,2048]{1,0:T(8,128)(2,1)S(1)} %get-tuple-element.32.refs_0_), channel_id=1, source_target_pairs={{0,128},{128,256},{256,384},{384,0},{1,129},{129,257},{257,385},{3... | collective-permute-start | bytes 1572872 | tf_op jit(solution)/shard_map/ppermute | solution.py:357
  68.7 3.2 %collective-permute-start.11 = (bf16[128,2048]{1,0:T(8,128)(2,1)S(1)}, bf16[128,2048]{1,0:T(8,128)(2,1)}, u32[]{:S(2)}, u32[]{:S(2)}) collective-permute-start(bf16[128,2048]{1,0:T(8,128)(2,1)S(1)} %get-tuple-element.32.refs_0_), channel_id=1, source_target_pairs={{0,384},{128,0},{256,128},{384,256},{1,385},{129,1},{257,129},{385... | collective-permute-start | bytes 1572872 | tf_op jit(solution)/shard_map/ppermute | solution.py:357
  71.9 3.6 %collective-permute-start.12 = (bf16[128,2048]{1,0:T(8,128)(2,1)S(1)}, bf16[128,2048]{1,0:T(8,128)(2,1)}, u32[]{:S(2)}, u32[]{:S(2)}) collective-permute-start(bf16[128,2048]{1,0:T(8,128)(2,1)S(1)} %get-tuple-element.32.refs_0_), channel_id=1, source_target_pairs={{0,256},{128,384},{256,0},{384,128},{1,257},{129,385},{257,1},{385... | collective-permute-start | bytes 1572872 | tf_op jit(solution)/shard_map/ppermute | solution.py:357
  75.5 4.9 %all-to-all-done.1.parts_ref = bf16[8,64,1024]{2,1,0:T(8,128)(2,1)S(1)} async-done(((bf16[8,64,1024]{2,1,0:T(8,128)(2,1)}), bf16[8,64,1024]{2,1,0:T(8,128)(2,1)S(1)}, u32[]{:S(2)}, u32[]{:S(2)}) %all-to-all-start.1) | async-done | bytes 1048608 | tf_op jit(solution)/shard_map/all_to_all | solution.py:353
  81.5 10.1 %all-to-all-start.2 = ((bf16[64,16,128]{2,1,0:T(8,128)(2,1)}), bf16[64,16,128]{2,1,0:T(8,128)(2,1)S(1)}, u32[]{:S(2)}, u32[]{:S(2)}) async-start(bf16[64,16,128]{2,1,0:T(8,128)(2,1)} %bitcast.6), calls=%async_computation.2 | async-start | bytes 524288 | tf_op jit(solution)/shard_map/all_to_all | solution.py:353
  91.6 3.5 %collective-permute-start.13 = (bf16[128,2048]{1,0:T(8,128)(2,1)S(1)}, bf16[128,2048]{1,0:T(8,128)(2,1)S(1)}, u32[]{:S(2)}, u32[]{:S(2)}) collective-permute-start(bf16[128,2048]{1,0:T(8,128)(2,1)S(1)} %get-tuple-element.32.refs_0_), channel_id=1, source_target_pairs={{0,64},{64,0},{1,65},{65,1},{2,66},{66,2},{3,67},{67,3},{4,68},{68... | collective-permute-start | bytes 1572872 | tf_op jit(solution)/shard_map/ppermute | solution.py:357
  99.5 3.4 %collective-permute-done.12.refs_3_ = bf16[128,2048]{1,0:T(8,128)(2,1)} collective-permute-done((bf16[128,2048]{1,0:T(8,128)(2,1)S(1)}, bf16[128,2048]{1,0:T(8,128)(2,1)}, u32[]{:S(2)}, u32[]{:S(2)}) %collective-permute-start.12) | collective-permute-done | bytes 524320 | tf_op jit(solution)/shard_map/ppermute | solution.py:357
  110.5 11.5 %depth_layer.1 = bf16[1024,128]{1,0:T(8,128)(2,1)} custom-call(bf16[1024,128]{1,0:T(8,128)(2,1)} %bitcast.28, bf16[472,1024]{1,0:T(8,128)(2,1)} %bitcast.30, bf16[472,1024]{1,0:T(8,128)(2,1)} %bitcast.31, bf16[1,1024]{1,0:T(2,128)(2,1)} %reshape.47.gain_ref, bf16[128,2048]{1,0:T(8,128)(2,1)} %copy-done, bf16[128,2048]{1,0:T(8,128)(2,1)} %collective-permute-done.10.refs_1_, ...), custom_call_target="tpu_custom_call" | custom-call | tf_op jit(solution)/shard_map/depth_layer/pallas_call | solution.py:412
  122.1 8.9 %all-to-all-start.3 = ((bf16[64,16,128]{2,1,0:T(8,128)(2,1)}), bf16[64,16,128]{2,1,0:T(8,128)(2,1)S(1)}, u32[]{:S(2)}, u32[]{:S(2)}) async-start(bf16[64,16,128]{2,1,0:T(8,128)(2,1)} %bitcast.29), calls=%async_computation.3 | async-start | bytes 524288 | tf_op jit(solution)/shard_map/all_to_all | solution.py:353
  131.0 3.1 %collective-permute-start.17 = (bf16[256,1024]{1,0:T(8,128)(2,1)S(1)}, bf16[256,1024]{1,0:T(8,128)(2,1)S(1)}, u32[]{:S(2)}, u32[]{:S(2)}) collective-permute-start(bf16[256,1024]{1,0:T(8,128)(2,1)S(1)} %get-tuple-element.33.w_in_ref.own_in_ref), channel_id=1, source_target_pairs={{0,64},{64,0},{1,65},{65,1},{2,66},{66,2},{3,67},{67,3},{4,68},{68... | collective-permute-start | bytes 1572872 | tf_op jit(solution)/shard_map/ppermute | solution.py:357
  134.1 15.5 %all-to-all-done.3 = bf16[64,16,128]{2,1,0:T(8,128)(2,1)S(1)} async-done(((bf16[64,16,128]{2,1,0:T(8,128)(2,1)}), bf16[64,16,128]{2,1,0:T(8,128)(2,1)S(1)}, u32[]{:S(2)}, u32[]{:S(2)}) %all-to-all-start.3) | async-done | bytes 262176 | tf_op jit(solution)/shard_map/all_to_all | solution.py:353
  150.8 3.5 %all-to-all-start.4 = ((bf16[4,64,1024]{2,1,0:T(8,128)(2,1)}), bf16[4,64,1024]{2,1,0:T(8,128)(2,1)S(1)}, u32[]{:S(2)}, u32[]{:S(2)}) async-start(bf16[4,64,1024]{2,1,0:T(8,128)(2,1)} %return_rows.1), calls=%async_computation.4 | async-start | bytes 1048576 | tf_op jit(solution)/shard_map/all_to_all | solution.py:353
  154.2 6.9 %all-to-all-done.4 = bf16[4,64,1024]{2,1,0:T(8,128)(2,1)S(1)} async-done(((bf16[4,64,1024]{2,1,0:T(8,128)(2,1)}), bf16[4,64,1024]{2,1,0:T(8,128)(2,1)S(1)}, u32[]{:S(2)}, u32[]{:S(2)}) %all-to-all-start.4) | async-done | bytes 524320 | tf_op jit(solution)/shard_map/all_to_all | solution.py:353
  161.6 6.4 %collective-permute-start.18 = (bf16[256,256]{1,0:T(8,128)(2,1)S(1)}, bf16[256,256]{1,0:T(8,128)(2,1)S(1)}, u32[]{:S(2)}, u32[]{:S(2)}) collective-permute-start(bf16[256,256]{1,0:T(8,128)(2,1)S(1)} %get-tuple-element.35), channel_id=1, source_target_pairs={{0,64},{64,0},{1,65},{65,1},{2,66},{66,2},{3,67},{67,3},{4,68},{68... | collective-permute-start | bytes 393224 | tf_op jit(solution)/shard_map/ppermute | solution.py:357
  171.3 15.0 %all_to_all.30.packed_ref = bf16[8,64,768]{2,1,0:T(8,128)(2,1)S(1)} all-to-all(bf16[8,64,768]{2,1,0:T(8,128)(2,1)S(1)} %bitcast.17), channel_id=1, replica_groups=mesh['x'=4,'core'=2,'y'=4,'z'=16] {'x','core'}, dimensions={0} | all-to-all | bytes 1572864 | tf_op jit(solution)/shard_map/all_to_all | solution.py:353
  (63 shorter events, 35.3 us)
Async XLA Ops:
  2.1 32.0 %all-to-all-start = ((bf16[16,8,1024]{2,1,0:T(8,128)(2,1)}), bf16[16,8,1024]{2,1,0:T(8,128)(2,1)S(1)}, u32[]{:S(2)}, u32[]{:S(2)}) async-start(bf16[16,8,1024]{2,1,0:T(8,128)(2,1)} %broadcast_in_dim.17), calls=%async_computation | async-start | bytes 524288 | tf_op jit(solution)/shard_map/all_to_all | solution.py:353
  19.1 15.0 %collective-permute-start = (bf16[64,1024]{1,0:T(8,128)(2,1)S(1)}, bf16[64,1024]{1,0:T(8,128)(2,1)S(1)}, u32[]{:S(2)}, u32[]{:S(2)}) collective-permute-start(bf16[64,1024]{1,0:T(8,128)(2,1)S(1)} %get-tuple-element.22), channel_id=1, source_target_pairs={{0,64},{64,128},{128,192},{192,256},{256,320},{320,384},{384,448},... | collective-permute-start | bytes 393224 | tf_op jit(solution)/shard_map/ppermute | solution.py:357
  21.2 16.2 %collective-permute-start.1 = (bf16[64,1024]{1,0:T(8,128)(2,1)S(1)}, bf16[64,1024]{1,0:T(8,128)(2,1)S(1)}, u32[]{:S(2)}, u32[]{:S(2)}) collective-permute-start(bf16[64,1024]{1,0:T(8,128)(2,1)S(1)} %get-tuple-element.23), channel_id=1, source_target_pairs={{0,128},{64,192},{128,256},{192,320},{256,384},{320,448},{384,0},{... | collective-permute-start | bytes 393224 | tf_op jit(solution)/shard_map/ppermute | solution.py:357
  24.3 16.4 %collective-permute-start.2 = (bf16[64,1024]{1,0:T(8,128)(2,1)S(1)}, bf16[64,1024]{1,0:T(8,128)(2,1)S(1)}, u32[]{:S(2)}, u32[]{:S(2)}) collective-permute-start(bf16[64,1024]{1,0:T(8,128)(2,1)S(1)} %get-tuple-element.24), channel_id=1, source_target_pairs={{0,192},{64,256},{128,320},{192,384},{256,448},{320,0},{384,64},{4... | collective-permute-start | bytes 393224 | tf_op jit(solution)/shard_map/ppermute | solution.py:357
  27.8 16.5 %collective-permute-start.3 = (bf16[64,1024]{1,0:T(8,128)(2,1)S(1)}, bf16[64,1024]{1,0:T(8,128)(2,1)S(1)}, u32[]{:S(2)}, u32[]{:S(2)}) collective-permute-start(bf16[64,1024]{1,0:T(8,128)(2,1)S(1)} %get-tuple-element.25), channel_id=1, source_target_pairs={{0,256},{64,320},{128,384},{192,448},{256,0},{320,64},{384,128},{4... | collective-permute-start | bytes 393224 | tf_op jit(solution)/shard_map/ppermute | solution.py:357
  30.2 16.7 %collective-permute-start.4 = (bf16[64,1024]{1,0:T(8,128)(2,1)S(1)}, bf16[64,1024]{1,0:T(8,128)(2,1)S(1)}, u32[]{:S(2)}, u32[]{:S(2)}) collective-permute-start(bf16[64,1024]{1,0:T(8,128)(2,1)S(1)} %get-tuple-element.26), channel_id=1, source_target_pairs={{0,320},{64,384},{128,448},{192,0},{256,64},{320,128},{384,192},{4... | collective-permute-start | bytes 393224 | tf_op jit(solution)/shard_map/ppermute | solution.py:357
  34.2 23.1 %collective-permute-start.7 = (bf16[128,1024]{1,0:T(8,128)(2,1)S(1)}, bf16[128,1024]{1,0:T(8,128)(2,1)S(1)}, u32[]{:S(2)}, u32[]{:S(2)}) collective-permute-start(bf16[128,1024]{1,0:T(8,128)(2,1)S(1)} %bitcast.20), channel_id=1, source_target_pairs={{0,16},{16,32},{32,48},{48,0},{1,17},{17,33},{33,49},{49,1},{2,18}... | collective-permute-start | bytes 786440 | tf_op jit(solution)/shard_map/ppermute | solution.py:357
  37.4 19.9 %collective-permute-start.8 = (bf16[128,1024]{1,0:T(8,128)(2,1)S(1)}, bf16[128,1024]{1,0:T(8,128)(2,1)S(1)}, u32[]{:S(2)}, u32[]{:S(2)}) collective-permute-start(bf16[128,1024]{1,0:T(8,128)(2,1)S(1)} %bitcast.21), channel_id=1, source_target_pairs={{0,48},{16,0},{32,16},{48,32},{1,49},{17,1},{33,17},{49,33},{2,50}... | collective-permute-start | bytes 786440 | tf_op jit(solution)/shard_map/ppermute | solution.py:357
  40.8 16.5 %collective-permute-start.9 = (bf16[128,1024]{1,0:T(8,128)(2,1)S(1)}, bf16[128,1024]{1,0:T(8,128)(2,1)S(1)}, u32[]{:S(2)}, u32[]{:S(2)}) collective-permute-start(bf16[128,1024]{1,0:T(8,128)(2,1)S(1)} %bitcast.22), channel_id=1, source_target_pairs={{0,32},{16,48},{32,0},{48,16},{1,33},{17,49},{33,1},{49,17},{2,34}... | collective-permute-start | bytes 786440 | tf_op jit(solution)/shard_map/ppermute | solution.py:357
  44.3 8.7 %collective-permute-start.5 = (bf16[64,1024]{1,0:T(8,128)(2,1)S(1)}, bf16[64,1024]{1,0:T(8,128)(2,1)S(1)}, u32[]{:S(2)}, u32[]{:S(2)}) collective-permute-start(bf16[64,1024]{1,0:T(8,128)(2,1)S(1)} %get-tuple-element.27), channel_id=1, source_target_pairs={{0,384},{64,448},{128,0},{192,64},{256,128},{320,192},{384,256},{4... | collective-permute-start | bytes 393224 | tf_op jit(solution)/shard_map/ppermute | solution.py:357
  46.9 9.0 %collective-permute-start.6 = (bf16[64,1024]{1,0:T(8,128)(2,1)S(1)}, bf16[64,1024]{1,0:T(8,128)(2,1)S(1)}, u32[]{:S(2)}, u32[]{:S(2)}) collective-permute-start(bf16[64,1024]{1,0:T(8,128)(2,1)S(1)} %get-tuple-element.28), channel_id=1, source_target_pairs={{0,448},{64,0},{128,64},{192,128},{256,192},{320,256},{384,320},{4... | collective-permute-start | bytes 393224 | tf_op jit(solution)/shard_map/ppermute | solution.py:357
  59.9 20.5 %all-to-all-start.1 = ((bf16[8,64,1024]{2,1,0:T(8,128)(2,1)}), bf16[8,64,1024]{2,1,0:T(8,128)(2,1)S(1)}, u32[]{:S(2)}, u32[]{:S(2)}) async-start(bf16[8,64,1024]{2,1,0:T(8,128)(2,1)} %bitcast.5), calls=%async_computation.1 | async-start | bytes 2097152 | tf_op jit(solution)/shard_map/all_to_all | solution.py:353
  65.2 29.9 %collective-permute-start.10 = (bf16[128,2048]{1,0:T(8,128)(2,1)S(1)}, bf16[128,2048]{1,0:T(8,128)(2,1)}, u32[]{:S(2)}, u32[]{:S(2)}) collective-permute-start(bf16[128,2048]{1,0:T(8,128)(2,1)S(1)} %get-tuple-element.32.refs_0_), channel_id=1, source_target_pairs={{0,128},{128,256},{256,384},{384,0},{1,129},{129,257},{257,385},{3... | collective-permute-start | bytes 1572872 | tf_op jit(solution)/shard_map/ppermute | solution.py:357
  68.7 28.4 %collective-permute-start.11 = (bf16[128,2048]{1,0:T(8,128)(2,1)S(1)}, bf16[128,2048]{1,0:T(8,128)(2,1)}, u32[]{:S(2)}, u32[]{:S(2)}) collective-permute-start(bf16[128,2048]{1,0:T(8,128)(2,1)S(1)} %get-tuple-element.32.refs_0_), channel_id=1, source_target_pairs={{0,384},{128,0},{256,128},{384,256},{1,385},{129,1},{257,129},{385... | collective-permute-start | bytes 1572872 | tf_op jit(solution)/shard_map/ppermute | solution.py:357
  71.9 31.1 %collective-permute-start.12 = (bf16[128,2048]{1,0:T(8,128)(2,1)S(1)}, bf16[128,2048]{1,0:T(8,128)(2,1)}, u32[]{:S(2)}, u32[]{:S(2)}) collective-permute-start(bf16[128,2048]{1,0:T(8,128)(2,1)S(1)} %get-tuple-element.32.refs_0_), channel_id=1, source_target_pairs={{0,256},{128,384},{256,0},{384,128},{1,257},{129,385},{257,1},{385... | collective-permute-start | bytes 1572872 | tf_op jit(solution)/shard_map/ppermute | solution.py:357
  81.5 28.4 %all-to-all-start.2 = ((bf16[64,16,128]{2,1,0:T(8,128)(2,1)}), bf16[64,16,128]{2,1,0:T(8,128)(2,1)S(1)}, u32[]{:S(2)}, u32[]{:S(2)}) async-start(bf16[64,16,128]{2,1,0:T(8,128)(2,1)} %bitcast.6), calls=%async_computation.2 | async-start | bytes 524288 | tf_op jit(solution)/shard_map/all_to_all | solution.py:353
  91.6 14.9 %collective-permute-start.13 = (bf16[128,2048]{1,0:T(8,128)(2,1)S(1)}, bf16[128,2048]{1,0:T(8,128)(2,1)S(1)}, u32[]{:S(2)}, u32[]{:S(2)}) collective-permute-start(bf16[128,2048]{1,0:T(8,128)(2,1)S(1)} %get-tuple-element.32.refs_0_), channel_id=1, source_target_pairs={{0,64},{64,0},{1,65},{65,1},{2,66},{66,2},{3,67},{67,3},{4,68},{68... | collective-permute-start | bytes 1572872 | tf_op jit(solution)/shard_map/ppermute | solution.py:357
  95.1 11.4 %collective-permute-start.14 = (bf16[128,2048]{1,0:T(8,128)(2,1)}, bf16[128,2048]{1,0:T(8,128)(2,1)S(1)}, u32[]{:S(2)}, u32[]{:S(2)}) collective-permute-start(bf16[128,2048]{1,0:T(8,128)(2,1)} %collective-permute-done.10.refs_1_), channel_id=1, source_target_pairs={{0,64},{64,0},{1,65},{65,1},{2,66},{66,2},{3,67},{67,3},{4,68},{68... | collective-permute-start | bytes 1572872 | tf_op jit(solution)/shard_map/ppermute | solution.py:357
  97.1 9.5 %collective-permute-start.15 = (bf16[128,2048]{1,0:T(8,128)(2,1)}, bf16[128,2048]{1,0:T(8,128)(2,1)S(1)}, u32[]{:S(2)}, u32[]{:S(2)}) collective-permute-start(bf16[128,2048]{1,0:T(8,128)(2,1)} %collective-permute-done.11.refs_2_), channel_id=1, source_target_pairs={{0,64},{64,0},{1,65},{65,1},{2,66},{66,2},{3,67},{67,3},{4,68},{68... | collective-permute-start | bytes 1572872 | tf_op jit(solution)/shard_map/ppermute | solution.py:357
  102.9 5.2 %collective-permute-start.16 = (bf16[128,2048]{1,0:T(8,128)(2,1)}, bf16[128,2048]{1,0:T(8,128)(2,1)}, u32[]{:S(2)}, u32[]{:S(2)}) collective-permute-start(bf16[128,2048]{1,0:T(8,128)(2,1)} %collective-permute-done.12.refs_3_), channel_id=1, source_target_pairs={{0,64},{64,0},{1,65},{65,1},{2,66},{66,2},{3,67},{67,3},{4,68},{68... | collective-permute-start | bytes 1572872 | tf_op jit(solution)/shard_map/ppermute | solution.py:357
  122.1 27.6 %all-to-all-start.3 = ((bf16[64,16,128]{2,1,0:T(8,128)(2,1)}), bf16[64,16,128]{2,1,0:T(8,128)(2,1)S(1)}, u32[]{:S(2)}, u32[]{:S(2)}) async-start(bf16[64,16,128]{2,1,0:T(8,128)(2,1)} %bitcast.29), calls=%async_computation.3 | async-start | bytes 524288 | tf_op jit(solution)/shard_map/all_to_all | solution.py:353
  131.0 23.3 %collective-permute-start.17 = (bf16[256,1024]{1,0:T(8,128)(2,1)S(1)}, bf16[256,1024]{1,0:T(8,128)(2,1)S(1)}, u32[]{:S(2)}, u32[]{:S(2)}) collective-permute-start(bf16[256,1024]{1,0:T(8,128)(2,1)S(1)} %get-tuple-element.33.w_in_ref.own_in_ref), channel_id=1, source_target_pairs={{0,64},{64,0},{1,65},{65,1},{2,66},{66,2},{3,67},{67,3},{4,68},{68... | collective-permute-start | bytes 1572872 | tf_op jit(solution)/shard_map/ppermute | solution.py:357
  150.8 10.4 %all-to-all-start.4 = ((bf16[4,64,1024]{2,1,0:T(8,128)(2,1)}), bf16[4,64,1024]{2,1,0:T(8,128)(2,1)S(1)}, u32[]{:S(2)}, u32[]{:S(2)}) async-start(bf16[4,64,1024]{2,1,0:T(8,128)(2,1)} %return_rows.1), calls=%async_computation.4 | async-start | bytes 1048576 | tf_op jit(solution)/shard_map/all_to_all | solution.py:353
  161.6 7.3 %collective-permute-start.18 = (bf16[256,256]{1,0:T(8,128)(2,1)S(1)}, bf16[256,256]{1,0:T(8,128)(2,1)S(1)}, u32[]{:S(2)}, u32[]{:S(2)}) collective-permute-start(bf16[256,256]{1,0:T(8,128)(2,1)S(1)} %get-tuple-element.35), channel_id=1, source_target_pairs={{0,64},{64,0},{1,65},{65,1},{2,66},{66,2},{3,67},{67,3},{4,68},{68... | collective-permute-start | bytes 393224 | tf_op jit(solution)/shard_map/ppermute | solution.py:357
  (12 other events, 143.0 us)

commit v5 on v4

--- a/solution.py
+++ b/solution.py
@@ -57,8 +57,8 @@
     )
 
 
-def weight_kernel(*refs):
-    pieces, in_ref, rest_ref, gathered_ref = refs[:4], refs[4], refs[5], refs[6]
+def enter_kernel(*refs):
+    pieces, (context_ref, in_ref, rest_ref, out_ref, gathered_ref) = refs[:4], refs[4:]
     here = lax.axis_index("y")
     for shift, piece in zip(SHIFTS, pieces):
         start = pl.multiple_of(((here + 4 - shift) & 3) * 128, 128)
@@ -68,7 +68,9 @@
         return (iota((rows, 512), 1) == source).astype(F32).astype(BF)
 
     row = iota((256, 512), 0)
-    in_ref[...] = dot(picked(256, ((row >> 2) << 3) + (row & 3)), gathered_ref[...]).astype(BF)
+    w_in = dot(picked(256, ((row >> 2) << 3) + (row & 3)), gathered_ref[...]).astype(BF)
+    in_ref[...] = w_in
+    out_ref[...] = dot(context_ref[...], w_in).astype(BF)
     row = iota((128, 512), 0)
     base = (row >> 1) << 3
     even = (row & 1) == 0
@@ -129,10 +131,6 @@
     for head in range(2):
         unused_q, unused_k, value, weights = head_weights(packed_ref, head)
         context_ref[:, head * HEAD : (head + 1) * HEAD] = dot(weights.astype(BF), value).astype(BF)
-
-
-def enter_kernel(context_ref, w_in_ref, out_ref):
-    out_ref[...] = dot(context_ref[...], w_in_ref[...]).astype(BF)
 
 
 def backward_kernel(packed_ref, own_ref, near_ref, out_ref, grad_s):
@@ -261,7 +259,7 @@
     hidden_s[...] = hidden
     copies[1].wait()
     cot_s[...] = jnp.concatenate([given_s[...].astype(F32), spare], axis=0)
-    gain = gain_ref[...].astype(F32)
+    gain = jnp.concatenate([gain_ref[c : c + 1, :].astype(F32) for c in range(8)], axis=1)
     scale = lax.rsqrt(jnp.sum(hidden * hidden, axis=1, keepdims=True) * (1.0 / D_DEP) + 1e-05)
     normed = (hidden * scale * gain).astype(BF)
     for copy in copies[2:]:
@@ -376,15 +374,6 @@
     mine = jnp.concatenate([w_in, w_qkv, w_out]).reshape(1, 8, D_DEP)
     along_z = exchange(jnp.broadcast_to(mine, (16, 8, D_DEP)), "z").reshape(128, D_DEP)
     along_y = [along_z] + [moved(along_z, "y", 4, shift) for shift in SHIFTS[1:]]
-    own_in, own_rest = call(
-        weight_kernel,
-        (jax.ShapeDtypeStruct((256, D_DEP), BF), jax.ShapeDtypeStruct((128, 2 * D_DEP), BF)),
-        "sort_weights",
-        scratch_shapes=[pltpu.VMEM((512, D_DEP), BF)],
-    )(*along_y)
-    rest = [own_rest] + [moved(own_rest, "x", 4, shift) for shift in SHIFTS[1:]]
-    rest += [moved(piece, "core", 2, 1) for piece in rest]
-
     block = jax.ShapeDtypeStruct((FRAMES, 4 * COLS), BF)
     blocks = call(pack_kernel, [block] * SEQ, "pack_heads")(
         queries[0], keys[0], values[0], text_grad[0]
@@ -398,10 +387,20 @@
         ),
         "attention_forward",
     )(*blocks)
-    parts = call(enter_kernel, jax.ShapeDtypeStruct((LENGTH, D_DEP), BF), "enter_depth")(
-        context, own_in
-    )
+    own_in, own_rest, parts = call(
+        enter_kernel,
+        (
+            jax.ShapeDtypeStruct((COLS, D_DEP), BF),
+            jax.ShapeDtypeStruct((128, 2 * D_DEP), BF),
+            jax.ShapeDtypeStruct((LENGTH, D_DEP), BF),
+        ),
+        "enter_depth",
+        scratch_shapes=[pltpu.VMEM((512, D_DEP), BF)],
+    )(*along_y, context)
+    far_rest = [moved(own_rest, "x", 4, shift) for shift in SHIFTS[1:]]
     parts = exchange(parts.reshape(SEQ, FRAMES, D_DEP), seq)
+    parts, near_rest = lax.optimization_barrier((parts, moved(own_rest, "core", 2, 1)))
+    rest = [own_rest, *far_rest, near_rest] + [moved(piece, "core", 2, 1) for piece in far_rest]
     narrow = jax.ShapeDtypeStruct((SLOTS * 8, 128), BF)
     sent = call(
         send_kernel, narrow, "send_rows", scratch_shapes=[pltpu.VMEM((SLOTS * 8, 128), F32)]
@@ -421,7 +420,7 @@
         slots,
         codes.reshape(ROWS, D_DEP),
         depth_cot.reshape(ROWS, D_DEP),
-        norm_gain.reshape(1, D_DEP),
+        norm_gain.reshape(8, 128),
         *rest,
     )
     late_in, unused = lax.optimization_barrier((own_in, grads))

time: 188 us -> 186 us (0.989)
    all_to_all x5, waiting for transfers between devices: 29 us -> 25.4 us  [exchange(): return lax.all_to_all(array, axis, split_axis=0, concat_axis=0, tiled=True)]
    ppermute x19, waiting for transfers between devices: 7.33 us -> 10.6 us  [moved(): lax.ppermute(array, axis, [(i, (i + shift) % size) for i in range(size)])]
  transfers between devices with their start and end apart: 24 -> 24, of which waited for: 7 -> 9; matrix products, arithmetic and copies ran while one was open for 0% -> 0% of each run, Pallas kernels for 2% -> 2%
where the time goes in v5:
time: 186 us; the launch traced here: 185 us
  starting transfers between devices  108 us (58%)
  waiting for transfers between devices  36.1 us (19%)
  Pallas kernels  20.8 us (11%)
  blocking collectives  15 us (8%)
  local copies, waits for them, and re-layouts  3.26 us (2%)
    ppermute x19, starting transfers between devices, moved(): lax.ppermute(array, axis, [(i, (i + shift) % size) for i in range(size)])  65.8 us
    all_to_all x5, starting transfers between devices, exchange(): return lax.all_to_all(array, axis, split_axis=0, concat_axis=0, tiled=True)  42.6 us
    all_to_all x5, waiting for transfers between devices, exchange(): return lax.all_to_all(array, axis, split_axis=0, concat_axis=0, tiled=True)  25.4 us
    all_to_all x1, blocking collectives, exchange(): return lax.all_to_all(array, axis, split_axis=0, concat_axis=0, tiled=True)  15 us
    pallas_call x1, Pallas kernels, shards(): call(depth_kernel, narrow, 'depth_layer', in_specs=[vmem, anywhere, anywh...  11.5 us
    ppermute x19, waiting for transfers between devices, moved(): lax.ppermute(array, axis, [(i, (i + shift) % size) for i in range(size)])  10.6 us
  transfers between devices with their start and end apart: 24, of which 9 were waited for; matrix products, arithmetic and copies ran while one was open for 0% of the time, Pallas kernels for 2%

profile of v5, /device:TPU:1, one launch (start us, length us, event | category | flops | bytes accessed | tf_op | source)
XLA Modules:
  0.0 185.3 jit_solution(14334516422835788141)
XLA Ops:
  2.1 15.9 %all-to-all-start = ((bf16[16,8,1024]{2,1,0:T(8,128)(2,1)}), bf16[16,8,1024]{2,1,0:T(8,128)(2,1)S(1)}, u32[]{:S(2)}, u32[]{:S(2)}) async-start(bf16[16,8,1024]{2,1,0:T(8,128)(2,1)} %broadcast_in_dim.17), calls=%async_computation | async-start | bytes 524288 | tf_op jit(solution)/shard_map/all_to_all | solution.py:351
  21.2 3.1 %collective-permute-start.1 = (bf16[64,1024]{1,0:T(8,128)(2,1)S(1)}, bf16[64,1024]{1,0:T(8,128)(2,1)S(1)}, u32[]{:S(2)}, u32[]{:S(2)}) collective-permute-start(bf16[64,1024]{1,0:T(8,128)(2,1)S(1)} %get-tuple-element.26), channel_id=1, source_target_pairs={{0,128},{64,192},{128,256},{192,320},{256,384},{320,448},{384,0},{... | collective-permute-start | bytes 393224 | tf_op jit(solution)/shard_map/ppermute | solution.py:355
  24.3 3.5 %collective-permute-start.2 = (bf16[64,1024]{1,0:T(8,128)(2,1)S(1)}, bf16[64,1024]{1,0:T(8,128)(2,1)S(1)}, u32[]{:S(2)}, u32[]{:S(2)}) collective-permute-start(bf16[64,1024]{1,0:T(8,128)(2,1)S(1)} %get-tuple-element.27), channel_id=1, source_target_pairs={{0,192},{64,256},{128,320},{192,384},{256,448},{320,0},{384,64},{4... | collective-permute-start | bytes 393224 | tf_op jit(solution)/shard_map/ppermute | solution.py:355
  30.2 3.9 %collective-permute-start.4 = (bf16[64,1024]{1,0:T(8,128)(2,1)S(1)}, bf16[64,1024]{1,0:T(8,128)(2,1)S(1)}, u32[]{:S(2)}, u32[]{:S(2)}) collective-permute-start(bf16[64,1024]{1,0:T(8,128)(2,1)S(1)} %get-tuple-element.29), channel_id=1, source_target_pairs={{0,320},{64,384},{128,448},{192,0},{256,64},{320,128},{384,192},{4... | collective-permute-start | bytes 393224 | tf_op jit(solution)/shard_map/ppermute | solution.py:355
  34.2 3.2 %collective-permute-start.7 = (bf16[128,1024]{1,0:T(8,128)(2,1)S(1)}, bf16[128,1024]{1,0:T(8,128)(2,1)S(1)}, u32[]{:S(2)}, u32[]{:S(2)}) collective-permute-start(bf16[128,1024]{1,0:T(8,128)(2,1)S(1)} %bitcast.20), channel_id=1, source_target_pairs={{0,16},{16,32},{32,48},{48,0},{1,17},{17,33},{33,49},{49,1},{2,18}... | collective-permute-start | bytes 786440 | tf_op jit(solution)/shard_map/ppermute | solution.py:355
  37.4 3.4 %collective-permute-start.8 = (bf16[128,1024]{1,0:T(8,128)(2,1)S(1)}, bf16[128,1024]{1,0:T(8,128)(2,1)S(1)}, u32[]{:S(2)}, u32[]{:S(2)}) collective-permute-start(bf16[128,1024]{1,0:T(8,128)(2,1)S(1)} %bitcast.21), channel_id=1, source_target_pairs={{0,48},{16,0},{32,16},{48,32},{1,49},{17,1},{33,17},{49,33},{2,50}... | collective-permute-start | bytes 786440 | tf_op jit(solution)/shard_map/ppermute | solution.py:355
  40.8 3.5 %collective-permute-start.9 = (bf16[128,1024]{1,0:T(8,128)(2,1)S(1)}, bf16[128,1024]{1,0:T(8,128)(2,1)S(1)}, u32[]{:S(2)}, u32[]{:S(2)}) collective-permute-start(bf16[128,1024]{1,0:T(8,128)(2,1)S(1)} %bitcast.22), channel_id=1, source_target_pairs={{0,32},{16,48},{32,0},{48,16},{1,33},{17,49},{33,1},{49,17},{2,34}... | collective-permute-start | bytes 786440 | tf_op jit(solution)/shard_map/ppermute | solution.py:355
  46.9 6.1 %collective-permute-start.6 = (bf16[64,1024]{1,0:T(8,128)(2,1)S(1)}, bf16[64,1024]{1,0:T(8,128)(2,1)S(1)}, u32[]{:S(2)}, u32[]{:S(2)}) collective-permute-start(bf16[64,1024]{1,0:T(8,128)(2,1)S(1)} %get-tuple-element.31), channel_id=1, source_target_pairs={{0,448},{64,0},{128,64},{192,128},{256,192},{320,256},{384,320},{4... | collective-permute-start | bytes 393224 | tf_op jit(solution)/shard_map/ppermute | solution.py:355
  59.1 5.4 %all-to-all-start.1 = ((bf16[8,64,1024]{2,1,0:T(8,128)(2,1)}), bf16[8,64,1024]{2,1,0:T(8,128)(2,1)S(1)}, u32[]{:S(2)}, u32[]{:S(2)}) async-start(bf16[8,64,1024]{2,1,0:T(8,128)(2,1)} %bitcast.5), calls=%async_computation.1 | async-start | bytes 2097152 | tf_op jit(solution)/shard_map/all_to_all | solution.py:351
  66.5 3.6 %collective-permute-start.11 = (bf16[128,2048]{1,0:T(8,128)(2,1)S(1)}, bf16[128,2048]{1,0:T(8,128)(2,1)}, u32[]{:S(2)}, u32[]{:S(2)}) collective-permute-start(bf16[128,2048]{1,0:T(8,128)(2,1)S(1)} %get-tuple-element.35.refs_0_), channel_id=1, source_target_pairs={{0,128},{128,256},{256,384},{384,0},{1,129},{129,257},{257,385},{3... | collective-permute-start | bytes 1572872 | tf_op jit(solution)/shard_map/ppermute | solution.py:355
  70.2 3.1 %collective-permute-start.12 = (bf16[128,2048]{1,0:T(8,128)(2,1)S(1)}, bf16[128,2048]{1,0:T(8,128)(2,1)}, u32[]{:S(2)}, u32[]{:S(2)}) collective-permute-start(bf16[128,2048]{1,0:T(8,128)(2,1)S(1)} %get-tuple-element.35.refs_0_), channel_id=1, source_target_pairs={{0,384},{128,0},{256,128},{384,256},{1,385},{129,1},{257,129},{385... | collective-permute-start | bytes 1572872 | tf_op jit(solution)/shard_map/ppermute | solution.py:355
  73.3 3.7 %collective-permute-start.13 = (bf16[128,2048]{1,0:T(8,128)(2,1)S(1)}, bf16[128,2048]{1,0:T(8,128)(2,1)}, u32[]{:S(2)}, u32[]{:S(2)}) collective-permute-start(bf16[128,2048]{1,0:T(8,128)(2,1)S(1)} %get-tuple-element.35.refs_0_), channel_id=1, source_target_pairs={{0,256},{128,384},{256,0},{384,128},{1,257},{129,385},{257,1},{385... | collective-permute-start | bytes 1572872 | tf_op jit(solution)/shard_map/ppermute | solution.py:355
  80.7 10.0 %all-to-all-start.2 = ((bf16[64,16,128]{2,1,0:T(8,128)(2,1)}), bf16[64,16,128]{2,1,0:T(8,128)(2,1)S(1)}, u32[]{:S(2)}, u32[]{:S(2)}) async-start(bf16[64,16,128]{2,1,0:T(8,128)(2,1)} %bitcast.6), calls=%async_computation.2 | async-start | bytes 524288 | tf_op jit(solution)/shard_map/all_to_all | solution.py:351
  90.7 3.5 %collective-permute-start.14 = (bf16[128,2048]{1,0:T(8,128)(2,1)}, bf16[128,2048]{1,0:T(8,128)(2,1)S(1)}, u32[]{:S(2)}, u32[]{:S(2)}) collective-permute-start(bf16[128,2048]{1,0:T(8,128)(2,1)} %collective-permute-done.11.refs_1_), channel_id=1, source_target_pairs={{0,64},{64,0},{1,65},{65,1},{2,66},{66,2},{3,67},{67,3},{4,68},{68... | collective-permute-start | bytes 1572872 | tf_op jit(solution)/shard_map/ppermute | solution.py:355
  96.2 6.0 %collective-permute-done.13.refs_3_ = bf16[128,2048]{1,0:T(8,128)(2,1)} collective-permute-done((bf16[128,2048]{1,0:T(8,128)(2,1)S(1)}, bf16[128,2048]{1,0:T(8,128)(2,1)}, u32[]{:S(2)}, u32[]{:S(2)}) %collective-permute-start.13) | collective-permute-done | bytes 524320 | tf_op jit(solution)/shard_map/ppermute | solution.py:355
  102.2 2.9 %collective-permute-start.16 = (bf16[128,2048]{1,0:T(8,128)(2,1)}, bf16[128,2048]{1,0:T(8,128)(2,1)S(1)}, u32[]{:S(2)}, u32[]{:S(2)}) collective-permute-start(bf16[128,2048]{1,0:T(8,128)(2,1)} %collective-permute-done.13.refs_3_), channel_id=1, source_target_pairs={{0,64},{64,0},{1,65},{65,1},{2,66},{66,2},{3,67},{67,3},{4,68},{68... | collective-permute-start | bytes 1572872 | tf_op jit(solution)/shard_map/ppermute | solution.py:355
  109.6 11.5 %depth_layer.1 = bf16[1024,128]{1,0:T(8,128)(2,1)} custom-call(bf16[1024,128]{1,0:T(8,128)(2,1)} %bitcast.29, bf16[472,1024]{1,0:T(8,128)(2,1)} %bitcast.31, bf16[472,1024]{1,0:T(8,128)(2,1)} %bitcast.32, bf16[8,128]{1,0:T(8,128)(2,1)} %bitcast.33, bf16[128,2048]{1,0:T(8,128)(2,1)} %copy-done, bf16[128,2048]{1,0:T(8,128)(2,1)} %collective-permute-done.11.refs_1_, ...), custom_call_target="tpu_custom_call" | custom-call | tf_op jit(solution)/shard_map/depth_layer/pallas_call | solution.py:411
  121.2 7.9 %all-to-all-start.3 = ((bf16[64,16,128]{2,1,0:T(8,128)(2,1)}), bf16[64,16,128]{2,1,0:T(8,128)(2,1)S(1)}, u32[]{:S(2)}, u32[]{:S(2)}) async-start(bf16[64,16,128]{2,1,0:T(8,128)(2,1)} %bitcast.30), calls=%async_computation.3 | async-start | bytes 524288 | tf_op jit(solution)/shard_map/all_to_all | solution.py:351
  129.1 4.1 %collective-permute-start.17 = (bf16[256,1024]{1,0:T(8,128)(2,1)S(1)}, bf16[256,1024]{1,0:T(8,128)(2,1)S(1)}, u32[]{:S(2)}, u32[]{:S(2)}) collective-permute-start(bf16[256,1024]{1,0:T(8,128)(2,1)S(1)} %get-tuple-element.39.own_in_ref), channel_id=1, source_target_pairs={{0,64},{64,0},{1,65},{65,1},{2,66},{66,2},{3,67},{67,3},{4,68},{68... | collective-permute-start | bytes 1572872 | tf_op jit(solution)/shard_map/ppermute | solution.py:355
  133.2 13.7 %all-to-all-done.3 = bf16[64,16,128]{2,1,0:T(8,128)(2,1)S(1)} async-done(((bf16[64,16,128]{2,1,0:T(8,128)(2,1)}), bf16[64,16,128]{2,1,0:T(8,128)(2,1)S(1)}, u32[]{:S(2)}, u32[]{:S(2)}) %all-to-all-start.3) | async-done | bytes 262176 | tf_op jit(solution)/shard_map/all_to_all | solution.py:351
  148.0 3.5 %all-to-all-start.4 = ((bf16[4,64,1024]{2,1,0:T(8,128)(2,1)}), bf16[4,64,1024]{2,1,0:T(8,128)(2,1)S(1)}, u32[]{:S(2)}, u32[]{:S(2)}) async-start(bf16[4,64,1024]{2,1,0:T(8,128)(2,1)} %return_rows.1), calls=%async_computation.4 | async-start | bytes 1048576 | tf_op jit(solution)/shard_map/all_to_all | solution.py:351
  151.5 6.9 %all-to-all-done.4 = bf16[4,64,1024]{2,1,0:T(8,128)(2,1)S(1)} async-done(((bf16[4,64,1024]{2,1,0:T(8,128)(2,1)}), bf16[4,64,1024]{2,1,0:T(8,128)(2,1)S(1)}, u32[]{:S(2)}, u32[]{:S(2)}) %all-to-all-start.4) | async-done | bytes 524320 | tf_op jit(solution)/shard_map/all_to_all | solution.py:351
  158.9 7.1 %collective-permute-start.18 = (bf16[256,256]{1,0:T(8,128)(2,1)S(1)}, bf16[256,256]{1,0:T(8,128)(2,1)S(1)}, u32[]{:S(2)}, u32[]{:S(2)}) collective-permute-start(bf16[256,256]{1,0:T(8,128)(2,1)S(1)} %get-tuple-element.41), channel_id=1, source_target_pairs={{0,64},{64,0},{1,65},{65,1},{2,66},{66,2},{3,67},{67,3},{4,68},{68... | collective-permute-start | bytes 393224 | tf_op jit(solution)/shard_map/ppermute | solution.py:355
  169.3 15.0 %all_to_all.30.packed_ref = bf16[8,64,768]{2,1,0:T(8,128)(2,1)S(1)} all-to-all(bf16[8,64,768]{2,1,0:T(8,128)(2,1)S(1)} %bitcast.18), channel_id=1, replica_groups=mesh['x'=4,'core'=2,'y'=4,'z'=16] {'x','core'}, dimensions={0} | all-to-all | bytes 1572864 | tf_op jit(solution)/shard_map/all_to_all | solution.py:351
  (59 shorter events, 33.8 us)
Async XLA Ops:
  2.1 32.0 %all-to-all-start = ((bf16[16,8,1024]{2,1,0:T(8,128)(2,1)}), bf16[16,8,1024]{2,1,0:T(8,128)(2,1)S(1)}, u32[]{:S(2)}, u32[]{:S(2)}) async-start(bf16[16,8,1024]{2,1,0:T(8,128)(2,1)} %broadcast_in_dim.17), calls=%async_computation | async-start | bytes 524288 | tf_op jit(solution)/shard_map/all_to_all | solution.py:351
  19.1 15.0 %collective-permute-start = (bf16[64,1024]{1,0:T(8,128)(2,1)S(1)}, bf16[64,1024]{1,0:T(8,128)(2,1)S(1)}, u32[]{:S(2)}, u32[]{:S(2)}) collective-permute-start(bf16[64,1024]{1,0:T(8,128)(2,1)S(1)} %get-tuple-element.25), channel_id=1, source_target_pairs={{0,64},{64,128},{128,192},{192,256},{256,320},{320,384},{384,448},... | collective-permute-start | bytes 393224 | tf_op jit(solution)/shard_map/ppermute | solution.py:355
  21.2 16.2 %collective-permute-start.1 = (bf16[64,1024]{1,0:T(8,128)(2,1)S(1)}, bf16[64,1024]{1,0:T(8,128)(2,1)S(1)}, u32[]{:S(2)}, u32[]{:S(2)}) collective-permute-start(bf16[64,1024]{1,0:T(8,128)(2,1)S(1)} %get-tuple-element.26), channel_id=1, source_target_pairs={{0,128},{64,192},{128,256},{192,320},{256,384},{320,448},{384,0},{... | collective-permute-start | bytes 393224 | tf_op jit(solution)/shard_map/ppermute | solution.py:355
  24.3 16.4 %collective-permute-start.2 = (bf16[64,1024]{1,0:T(8,128)(2,1)S(1)}, bf16[64,1024]{1,0:T(8,128)(2,1)S(1)}, u32[]{:S(2)}, u32[]{:S(2)}) collective-permute-start(bf16[64,1024]{1,0:T(8,128)(2,1)S(1)} %get-tuple-element.27), channel_id=1, source_target_pairs={{0,192},{64,256},{128,320},{192,384},{256,448},{320,0},{384,64},{4... | collective-permute-start | bytes 393224 | tf_op jit(solution)/shard_map/ppermute | solution.py:355
  27.8 16.5 %collective-permute-start.3 = (bf16[64,1024]{1,0:T(8,128)(2,1)S(1)}, bf16[64,1024]{1,0:T(8,128)(2,1)S(1)}, u32[]{:S(2)}, u32[]{:S(2)}) collective-permute-start(bf16[64,1024]{1,0:T(8,128)(2,1)S(1)} %get-tuple-element.28), channel_id=1, source_target_pairs={{0,256},{64,320},{128,384},{192,448},{256,0},{320,64},{384,128},{4... | collective-permute-start | bytes 393224 | tf_op jit(solution)/shard_map/ppermute | solution.py:355
  30.2 16.7 %collective-permute-start.4 = (bf16[64,1024]{1,0:T(8,128)(2,1)S(1)}, bf16[64,1024]{1,0:T(8,128)(2,1)S(1)}, u32[]{:S(2)}, u32[]{:S(2)}) collective-permute-start(bf16[64,1024]{1,0:T(8,128)(2,1)S(1)} %get-tuple-element.29), channel_id=1, source_target_pairs={{0,320},{64,384},{128,448},{192,0},{256,64},{320,128},{384,192},{4... | collective-permute-start | bytes 393224 | tf_op jit(solution)/shard_map/ppermute | solution.py:355
  34.2 23.1 %collective-permute-start.7 = (bf16[128,1024]{1,0:T(8,128)(2,1)S(1)}, bf16[128,1024]{1,0:T(8,128)(2,1)S(1)}, u32[]{:S(2)}, u32[]{:S(2)}) collective-permute-start(bf16[128,1024]{1,0:T(8,128)(2,1)S(1)} %bitcast.20), channel_id=1, source_target_pairs={{0,16},{16,32},{32,48},{48,0},{1,17},{17,33},{33,49},{49,1},{2,18}... | collective-permute-start | bytes 786440 | tf_op jit(solution)/shard_map/ppermute | solution.py:355
  37.4 19.9 %collective-permute-start.8 = (bf16[128,1024]{1,0:T(8,128)(2,1)S(1)}, bf16[128,1024]{1,0:T(8,128)(2,1)S(1)}, u32[]{:S(2)}, u32[]{:S(2)}) collective-permute-start(bf16[128,1024]{1,0:T(8,128)(2,1)S(1)} %bitcast.21), channel_id=1, source_target_pairs={{0,48},{16,0},{32,16},{48,32},{1,49},{17,1},{33,17},{49,33},{2,50}... | collective-permute-start | bytes 786440 | tf_op jit(solution)/shard_map/ppermute | solution.py:355
  40.8 16.5 %collective-permute-start.9 = (bf16[128,1024]{1,0:T(8,128)(2,1)S(1)}, bf16[128,1024]{1,0:T(8,128)(2,1)S(1)}, u32[]{:S(2)}, u32[]{:S(2)}) collective-permute-start(bf16[128,1024]{1,0:T(8,128)(2,1)S(1)} %bitcast.22), channel_id=1, source_target_pairs={{0,32},{16,48},{32,0},{48,16},{1,33},{17,49},{33,1},{49,17},{2,34}... | collective-permute-start | bytes 786440 | tf_op jit(solution)/shard_map/ppermute | solution.py:355
  44.3 8.7 %collective-permute-start.5 = (bf16[64,1024]{1,0:T(8,128)(2,1)S(1)}, bf16[64,1024]{1,0:T(8,128)(2,1)S(1)}, u32[]{:S(2)}, u32[]{:S(2)}) collective-permute-start(bf16[64,1024]{1,0:T(8,128)(2,1)S(1)} %get-tuple-element.30), channel_id=1, source_target_pairs={{0,384},{64,448},{128,0},{192,64},{256,128},{320,192},{384,256},{4... | collective-permute-start | bytes 393224 | tf_op jit(solution)/shard_map/ppermute | solution.py:355
  46.9 9.0 %collective-permute-start.6 = (bf16[64,1024]{1,0:T(8,128)(2,1)S(1)}, bf16[64,1024]{1,0:T(8,128)(2,1)S(1)}, u32[]{:S(2)}, u32[]{:S(2)}) collective-permute-start(bf16[64,1024]{1,0:T(8,128)(2,1)S(1)} %get-tuple-element.31), channel_id=1, source_target_pairs={{0,448},{64,0},{128,64},{192,128},{256,192},{320,256},{384,320},{4... | collective-permute-start | bytes 393224 | tf_op jit(solution)/shard_map/ppermute | solution.py:355
  59.1 20.5 %all-to-all-start.1 = ((bf16[8,64,1024]{2,1,0:T(8,128)(2,1)}), bf16[8,64,1024]{2,1,0:T(8,128)(2,1)S(1)}, u32[]{:S(2)}, u32[]{:S(2)}) async-start(bf16[8,64,1024]{2,1,0:T(8,128)(2,1)} %bitcast.5), calls=%async_computation.1 | async-start | bytes 2097152 | tf_op jit(solution)/shard_map/all_to_all | solution.py:351
  64.5 12.5 %collective-permute-start.10 = (bf16[128,2048]{1,0:T(8,128)(2,1)S(1)}, bf16[128,2048]{1,0:T(8,128)(2,1)}, u32[]{:S(2)}, u32[]{:S(2)}) collective-permute-start(bf16[128,2048]{1,0:T(8,128)(2,1)S(1)} %get-tuple-element.35.refs_0_), channel_id=1, source_target_pairs={{0,64},{64,0},{1,65},{65,1},{2,66},{66,2},{3,67},{67,3},{4,68},{68... | collective-permute-start | bytes 1572872 | tf_op jit(solution)/shard_map/ppermute | solution.py:355
  66.5 24.2 %collective-permute-start.11 = (bf16[128,2048]{1,0:T(8,128)(2,1)S(1)}, bf16[128,2048]{1,0:T(8,128)(2,1)}, u32[]{:S(2)}, u32[]{:S(2)}) collective-permute-start(bf16[128,2048]{1,0:T(8,128)(2,1)S(1)} %get-tuple-element.35.refs_0_), channel_id=1, source_target_pairs={{0,128},{128,256},{256,384},{384,0},{1,129},{129,257},{257,385},{3... | collective-permute-start | bytes 1572872 | tf_op jit(solution)/shard_map/ppermute | solution.py:355
  70.2 24.1 %collective-permute-start.12 = (bf16[128,2048]{1,0:T(8,128)(2,1)S(1)}, bf16[128,2048]{1,0:T(8,128)(2,1)}, u32[]{:S(2)}, u32[]{:S(2)}) collective-permute-start(bf16[128,2048]{1,0:T(8,128)(2,1)S(1)} %get-tuple-element.35.refs_0_), channel_id=1, source_target_pairs={{0,384},{128,0},{256,128},{384,256},{1,385},{129,1},{257,129},{385... | collective-permute-start | bytes 1572872 | tf_op jit(solution)/shard_map/ppermute | solution.py:355
  73.3 28.9 %collective-permute-start.13 = (bf16[128,2048]{1,0:T(8,128)(2,1)S(1)}, bf16[128,2048]{1,0:T(8,128)(2,1)}, u32[]{:S(2)}, u32[]{:S(2)}) collective-permute-start(bf16[128,2048]{1,0:T(8,128)(2,1)S(1)} %get-tuple-element.35.refs_0_), channel_id=1, source_target_pairs={{0,256},{128,384},{256,0},{384,128},{1,257},{129,385},{257,1},{385... | collective-permute-start | bytes 1572872 | tf_op jit(solution)/shard_map/ppermute | solution.py:355
  80.7 28.2 %all-to-all-start.2 = ((bf16[64,16,128]{2,1,0:T(8,128)(2,1)}), bf16[64,16,128]{2,1,0:T(8,128)(2,1)S(1)}, u32[]{:S(2)}, u32[]{:S(2)}) async-start(bf16[64,16,128]{2,1,0:T(8,128)(2,1)} %bitcast.6), calls=%async_computation.2 | async-start | bytes 524288 | tf_op jit(solution)/shard_map/all_to_all | solution.py:351
  90.7 14.4 %collective-permute-start.14 = (bf16[128,2048]{1,0:T(8,128)(2,1)}, bf16[128,2048]{1,0:T(8,128)(2,1)S(1)}, u32[]{:S(2)}, u32[]{:S(2)}) collective-permute-start(bf16[128,2048]{1,0:T(8,128)(2,1)} %collective-permute-done.11.refs_1_), channel_id=1, source_target_pairs={{0,64},{64,0},{1,65},{65,1},{2,66},{66,2},{3,67},{67,3},{4,68},{68... | collective-permute-start | bytes 1572872 | tf_op jit(solution)/shard_map/ppermute | solution.py:355
  94.2 10.9 %collective-permute-start.15 = (bf16[128,2048]{1,0:T(8,128)(2,1)}, bf16[128,2048]{1,0:T(8,128)(2,1)S(1)}, u32[]{:S(2)}, u32[]{:S(2)}) collective-permute-start(bf16[128,2048]{1,0:T(8,128)(2,1)} %collective-permute-done.12.refs_2_), channel_id=1, source_target_pairs={{0,64},{64,0},{1,65},{65,1},{2,66},{66,2},{3,67},{67,3},{4,68},{68... | collective-permute-start | bytes 1572872 | tf_op jit(solution)/shard_map/ppermute | solution.py:355
  102.2 4.5 %collective-permute-start.16 = (bf16[128,2048]{1,0:T(8,128)(2,1)}, bf16[128,2048]{1,0:T(8,128)(2,1)S(1)}, u32[]{:S(2)}, u32[]{:S(2)}) collective-permute-start(bf16[128,2048]{1,0:T(8,128)(2,1)} %collective-permute-done.13.refs_3_), channel_id=1, source_target_pairs={{0,64},{64,0},{1,65},{65,1},{2,66},{66,2},{3,67},{67,3},{4,68},{68... | collective-permute-start | bytes 1572872 | tf_op jit(solution)/shard_map/ppermute | solution.py:355
  121.2 25.7 %all-to-all-start.3 = ((bf16[64,16,128]{2,1,0:T(8,128)(2,1)}), bf16[64,16,128]{2,1,0:T(8,128)(2,1)S(1)}, u32[]{:S(2)}, u32[]{:S(2)}) async-start(bf16[64,16,128]{2,1,0:T(8,128)(2,1)} %bitcast.30), calls=%async_computation.3 | async-start | bytes 524288 | tf_op jit(solution)/shard_map/all_to_all | solution.py:351
  129.1 22.4 %collective-permute-start.17 = (bf16[256,1024]{1,0:T(8,128)(2,1)S(1)}, bf16[256,1024]{1,0:T(8,128)(2,1)S(1)}, u32[]{:S(2)}, u32[]{:S(2)}) collective-permute-start(bf16[256,1024]{1,0:T(8,128)(2,1)S(1)} %get-tuple-element.39.own_in_ref), channel_id=1, source_target_pairs={{0,64},{64,0},{1,65},{65,1},{2,66},{66,2},{3,67},{67,3},{4,68},{68... | collective-permute-start | bytes 1572872 | tf_op jit(solution)/shard_map/ppermute | solution.py:355
  148.0 10.4 %all-to-all-start.4 = ((bf16[4,64,1024]{2,1,0:T(8,128)(2,1)}), bf16[4,64,1024]{2,1,0:T(8,128)(2,1)S(1)}, u32[]{:S(2)}, u32[]{:S(2)}) async-start(bf16[4,64,1024]{2,1,0:T(8,128)(2,1)} %return_rows.1), calls=%async_computation.4 | async-start | bytes 1048576 | tf_op jit(solution)/shard_map/all_to_all | solution.py:351
  158.9 8.1 %collective-permute-start.18 = (bf16[256,256]{1,0:T(8,128)(2,1)S(1)}, bf16[256,256]{1,0:T(8,128)(2,1)S(1)}, u32[]{:S(2)}, u32[]{:S(2)}) collective-permute-start(bf16[256,256]{1,0:T(8,128)(2,1)S(1)} %get-tuple-element.41), channel_id=1, source_target_pairs={{0,64},{64,0},{1,65},{65,1},{2,66},{66,2},{3,67},{67,3},{4,68},{68... | collective-permute-start | bytes 393224 | tf_op jit(solution)/shard_map/ppermute | solution.py:355
  (11 other events, 101.5 us)

commit v6 on v5

--- a/solution.py
+++ b/solution.py
@@ -226,14 +226,9 @@
         projected_s,
         grads_s,
         narrow_s,
-        codes_s,
-        given_s,
         sems,
     ) = refs
-    copies = [
-        pltpu.make_async_copy(codes_ref, codes_s, sems.at[0]),
-        pltpu.make_async_copy(cot_ref, given_s, sems.at[1]),
-    ]
+    copies = []
     for part, piece in zip(parts_held(), pieces):
         goal = weights_s.at[pl.ds(pl.multiple_of(part * 128, 128), 128), :]
         copies.append(pltpu.make_async_copy(piece, goal, sems.at[len(copies)]))
@@ -252,17 +247,15 @@
         (live_row > 0.5) & (rank_row == (iota((PADDED, SLOTS), 0) >> 3).astype(F32))
     ).astype(F32)
     spare = jnp.zeros((PADDED - ROWS, D_DEP), F32)
-    copies[0].wait()
     hidden = dot(spread.astype(BF), slots) + jnp.concatenate(
-        [codes_s[...].astype(F32), spare], axis=0
+        [codes_ref[...].astype(F32), spare], axis=0
     )
     hidden_s[...] = hidden
-    copies[1].wait()
-    cot_s[...] = jnp.concatenate([given_s[...].astype(F32), spare], axis=0)
+    cot_s[...] = jnp.concatenate([cot_ref[...].astype(F32), spare], axis=0)
     gain = jnp.concatenate([gain_ref[c : c + 1, :].astype(F32) for c in range(8)], axis=1)
     scale = lax.rsqrt(jnp.sum(hidden * hidden, axis=1, keepdims=True) * (1.0 / D_DEP) + 1e-05)
     normed = (hidden * scale * gain).astype(BF)
-    for copy in copies[2:]:
+    for copy in copies:
         copy.wait()
     width = DHEADS * DHEAD
     w_out = weights_s[:, 3 * width :].reshape(SEQ, 2, DHEAD, width)
@@ -341,9 +334,7 @@
         pltpu.VMEM((PADDED, 3 * width), BF),
         pltpu.VMEM((PADDED, 3 * width), BF),
         pltpu.VMEM((SLOTS * 8, 128), F32),
-        pltpu.VMEM((ROWS, D_DEP), BF),
-        pltpu.VMEM((ROWS, D_DEP), BF),
-        pltpu.SemaphoreType.DMA((SEQ + 2,)),
+        pltpu.SemaphoreType.DMA((SEQ,)),
     ]
 
 
@@ -412,7 +403,7 @@
         depth_kernel,
         narrow,
         "depth_layer",
-        in_specs=[vmem, anywhere, anywhere, vmem] + [anywhere] * SEQ,
+        in_specs=[vmem] * 4 + [anywhere] * SEQ,
         out_specs=vmem,
         scratch_shapes=depth_scratch(),
         vmem=58,

time: 186 us -> 186 us (level)
  no operation moved by 1% of the time
where the time goes in v6:
time: 186 us; the launch traced here: 185 us
  starting transfers between devices  108 us (58%)
  waiting for transfers between devices  36.1 us (19%)
  Pallas kernels  20.8 us (11%)
  blocking collectives  15 us (8%)
  local copies, waits for them, and re-layouts  3.26 us (2%)
    ppermute x19, starting transfers between devices, moved(): lax.ppermute(array, axis, [(i, (i + shift) % size) for i in range(size)])  65.8 us
    all_to_all x5, starting transfers between devices, exchange(): return lax.all_to_all(array, axis, split_axis=0, concat_axis=0, tiled=True)  42.6 us
    all_to_all x5, waiting for transfers between devices, exchange(): return lax.all_to_all(array, axis, split_axis=0, concat_axis=0, tiled=True)  25.4 us
    all_to_all x1, blocking collectives, exchange(): return lax.all_to_all(array, axis, split_axis=0, concat_axis=0, tiled=True)  15 us
    pallas_call x1, Pallas kernels, shards(): call(depth_kernel, narrow, 'depth_layer', in_specs=[vmem] * 4 + [anywhere...  11.5 us
    ppermute x19, waiting for transfers between devices, moved(): lax.ppermute(array, axis, [(i, (i + shift) % size) for i in range(size)])  10.6 us
  transfers between devices with their start and end apart: 24, of which 9 were waited for; matrix products, arithmetic and copies ran while one was open for 0% of the time, Pallas kernels for 2%

profile of v6, /device:TPU:1, one launch (start us, length us, event | category | flops | bytes accessed | tf_op | source)
XLA Modules:
  0.0 185.3 jit_solution(11334810801950589241)
XLA Ops:
  2.1 15.9 %all-to-all-start = ((bf16[16,8,1024]{2,1,0:T(8,128)(2,1)}), bf16[16,8,1024]{2,1,0:T(8,128)(2,1)S(1)}, u32[]{:S(2)}, u32[]{:S(2)}) async-start(bf16[16,8,1024]{2,1,0:T(8,128)(2,1)} %broadcast_in_dim.17), calls=%async_computation | async-start | bytes 524288 | tf_op jit(solution)/shard_map/all_to_all | solution.py:342
  21.2 3.1 %collective-permute-start.1 = (bf16[64,1024]{1,0:T(8,128)(2,1)S(1)}, bf16[64,1024]{1,0:T(8,128)(2,1)S(1)}, u32[]{:S(2)}, u32[]{:S(2)}) collective-permute-start(bf16[64,1024]{1,0:T(8,128)(2,1)S(1)} %get-tuple-element.26), channel_id=1, source_target_pairs={{0,128},{64,192},{128,256},{192,320},{256,384},{320,448},{384,0},{... | collective-permute-start | bytes 393224 | tf_op jit(solution)/shard_map/ppermute | solution.py:346
  24.3 3.5 %collective-permute-start.2 = (bf16[64,1024]{1,0:T(8,128)(2,1)S(1)}, bf16[64,1024]{1,0:T(8,128)(2,1)S(1)}, u32[]{:S(2)}, u32[]{:S(2)}) collective-permute-start(bf16[64,1024]{1,0:T(8,128)(2,1)S(1)} %get-tuple-element.27), channel_id=1, source_target_pairs={{0,192},{64,256},{128,320},{192,384},{256,448},{320,0},{384,64},{4... | collective-permute-start | bytes 393224 | tf_op jit(solution)/shard_map/ppermute | solution.py:346
  30.2 3.9 %collective-permute-start.4 = (bf16[64,1024]{1,0:T(8,128)(2,1)S(1)}, bf16[64,1024]{1,0:T(8,128)(2,1)S(1)}, u32[]{:S(2)}, u32[]{:S(2)}) collective-permute-start(bf16[64,1024]{1,0:T(8,128)(2,1)S(1)} %get-tuple-element.29), channel_id=1, source_target_pairs={{0,320},{64,384},{128,448},{192,0},{256,64},{320,128},{384,192},{4... | collective-permute-start | bytes 393224 | tf_op jit(solution)/shard_map/ppermute | solution.py:346
  34.2 3.2 %collective-permute-start.7 = (bf16[128,1024]{1,0:T(8,128)(2,1)S(1)}, bf16[128,1024]{1,0:T(8,128)(2,1)S(1)}, u32[]{:S(2)}, u32[]{:S(2)}) collective-permute-start(bf16[128,1024]{1,0:T(8,128)(2,1)S(1)} %bitcast.20), channel_id=1, source_target_pairs={{0,16},{16,32},{32,48},{48,0},{1,17},{17,33},{33,49},{49,1},{2,18}... | collective-permute-start | bytes 786440 | tf_op jit(solution)/shard_map/ppermute | solution.py:346
  37.4 3.4 %collective-permute-start.8 = (bf16[128,1024]{1,0:T(8,128)(2,1)S(1)}, bf16[128,1024]{1,0:T(8,128)(2,1)S(1)}, u32[]{:S(2)}, u32[]{:S(2)}) collective-permute-start(bf16[128,1024]{1,0:T(8,128)(2,1)S(1)} %bitcast.21), channel_id=1, source_target_pairs={{0,48},{16,0},{32,16},{48,32},{1,49},{17,1},{33,17},{49,33},{2,50}... | collective-permute-start | bytes 786440 | tf_op jit(solution)/shard_map/ppermute | solution.py:346
  40.8 3.5 %collective-permute-start.9 = (bf16[128,1024]{1,0:T(8,128)(2,1)S(1)}, bf16[128,1024]{1,0:T(8,128)(2,1)S(1)}, u32[]{:S(2)}, u32[]{:S(2)}) collective-permute-start(bf16[128,1024]{1,0:T(8,128)(2,1)S(1)} %bitcast.22), channel_id=1, source_target_pairs={{0,32},{16,48},{32,0},{48,16},{1,33},{17,49},{33,1},{49,17},{2,34}... | collective-permute-start | bytes 786440 | tf_op jit(solution)/shard_map/ppermute | solution.py:346
  46.9 6.1 %collective-permute-start.6 = (bf16[64,1024]{1,0:T(8,128)(2,1)S(1)}, bf16[64,1024]{1,0:T(8,128)(2,1)S(1)}, u32[]{:S(2)}, u32[]{:S(2)}) collective-permute-start(bf16[64,1024]{1,0:T(8,128)(2,1)S(1)} %get-tuple-element.31), channel_id=1, source_target_pairs={{0,448},{64,0},{128,64},{192,128},{256,192},{320,256},{384,320},{4... | collective-permute-start | bytes 393224 | tf_op jit(solution)/shard_map/ppermute | solution.py:346
  59.1 5.4 %all-to-all-start.1 = ((bf16[8,64,1024]{2,1,0:T(8,128)(2,1)}), bf16[8,64,1024]{2,1,0:T(8,128)(2,1)S(1)}, u32[]{:S(2)}, u32[]{:S(2)}) async-start(bf16[8,64,1024]{2,1,0:T(8,128)(2,1)} %bitcast.5), calls=%async_computation.1 | async-start | bytes 2097152 | tf_op jit(solution)/shard_map/all_to_all | solution.py:342
  66.5 3.6 %collective-permute-start.11 = (bf16[128,2048]{1,0:T(8,128)(2,1)S(1)}, bf16[128,2048]{1,0:T(8,128)(2,1)}, u32[]{:S(2)}, u32[]{:S(2)}) collective-permute-start(bf16[128,2048]{1,0:T(8,128)(2,1)S(1)} %get-tuple-element.35.refs_0_), channel_id=1, source_target_pairs={{0,128},{128,256},{256,384},{384,0},{1,129},{129,257},{257,385},{3... | collective-permute-start | bytes 1572872 | tf_op jit(solution)/shard_map/ppermute | solution.py:346
  70.2 3.1 %collective-permute-start.12 = (bf16[128,2048]{1,0:T(8,128)(2,1)S(1)}, bf16[128,2048]{1,0:T(8,128)(2,1)}, u32[]{:S(2)}, u32[]{:S(2)}) collective-permute-start(bf16[128,2048]{1,0:T(8,128)(2,1)S(1)} %get-tuple-element.35.refs_0_), channel_id=1, source_target_pairs={{0,384},{128,0},{256,128},{384,256},{1,385},{129,1},{257,129},{385... | collective-permute-start | bytes 1572872 | tf_op jit(solution)/shard_map/ppermute | solution.py:346
  73.3 3.7 %collective-permute-start.13 = (bf16[128,2048]{1,0:T(8,128)(2,1)S(1)}, bf16[128,2048]{1,0:T(8,128)(2,1)}, u32[]{:S(2)}, u32[]{:S(2)}) collective-permute-start(bf16[128,2048]{1,0:T(8,128)(2,1)S(1)} %get-tuple-element.35.refs_0_), channel_id=1, source_target_pairs={{0,256},{128,384},{256,0},{384,128},{1,257},{129,385},{257,1},{385... | collective-permute-start | bytes 1572872 | tf_op jit(solution)/shard_map/ppermute | solution.py:346
  80.7 10.0 %all-to-all-start.2 = ((bf16[64,16,128]{2,1,0:T(8,128)(2,1)}), bf16[64,16,128]{2,1,0:T(8,128)(2,1)S(1)}, u32[]{:S(2)}, u32[]{:S(2)}) async-start(bf16[64,16,128]{2,1,0:T(8,128)(2,1)} %bitcast.6), calls=%async_computation.2 | async-start | bytes 524288 | tf_op jit(solution)/shard_map/all_to_all | solution.py:342
  90.7 3.5 %collective-permute-start.14 = (bf16[128,2048]{1,0:T(8,128)(2,1)}, bf16[128,2048]{1,0:T(8,128)(2,1)S(1)}, u32[]{:S(2)}, u32[]{:S(2)}) collective-permute-start(bf16[128,2048]{1,0:T(8,128)(2,1)} %collective-permute-done.11.refs_1_), channel_id=1, source_target_pairs={{0,64},{64,0},{1,65},{65,1},{2,66},{66,2},{3,67},{67,3},{4,68},{68... | collective-permute-start | bytes 1572872 | tf_op jit(solution)/shard_map/ppermute | solution.py:346
  96.2 6.0 %collective-permute-done.13.refs_3_ = bf16[128,2048]{1,0:T(8,128)(2,1)} collective-permute-done((bf16[128,2048]{1,0:T(8,128)(2,1)S(1)}, bf16[128,2048]{1,0:T(8,128)(2,1)}, u32[]{:S(2)}, u32[]{:S(2)}) %collective-permute-start.13) | collective-permute-done | bytes 524320 | tf_op jit(solution)/shard_map/ppermute | solution.py:346
  102.2 2.9 %collective-permute-start.16 = (bf16[128,2048]{1,0:T(8,128)(2,1)}, bf16[128,2048]{1,0:T(8,128)(2,1)S(1)}, u32[]{:S(2)}, u32[]{:S(2)}) collective-permute-start(bf16[128,2048]{1,0:T(8,128)(2,1)} %collective-permute-done.13.refs_3_), channel_id=1, source_target_pairs={{0,64},{64,0},{1,65},{65,1},{2,66},{66,2},{3,67},{67,3},{4,68},{68... | collective-permute-start | bytes 1572872 | tf_op jit(solution)/shard_map/ppermute | solution.py:346
  109.6 11.5 %depth_layer.1 = bf16[1024,128]{1,0:T(8,128)(2,1)} custom-call(bf16[1024,128]{1,0:T(8,128)(2,1)} %bitcast.29, bf16[472,1024]{1,0:T(8,128)(2,1)} %bitcast.31, bf16[472,1024]{1,0:T(8,128)(2,1)} %bitcast.32, bf16[8,128]{1,0:T(8,128)(2,1)} %bitcast.33, bf16[128,2048]{1,0:T(8,128)(2,1)} %copy-done, bf16[128,2048]{1,0:T(8,128)(2,1)} %collective-permute-done.11.refs_1_, ...), custom_call_target="tpu_custom_call" | custom-call | tf_op jit(solution)/shard_map/depth_layer/pallas_call | solution.py:402
  121.2 7.9 %all-to-all-start.3 = ((bf16[64,16,128]{2,1,0:T(8,128)(2,1)}), bf16[64,16,128]{2,1,0:T(8,128)(2,1)S(1)}, u32[]{:S(2)}, u32[]{:S(2)}) async-start(bf16[64,16,128]{2,1,0:T(8,128)(2,1)} %bitcast.30), calls=%async_computation.3 | async-start | bytes 524288 | tf_op jit(solution)/shard_map/all_to_all | solution.py:342
  129.1 4.1 %collective-permute-start.17 = (bf16[256,1024]{1,0:T(8,128)(2,1)S(1)}, bf16[256,1024]{1,0:T(8,128)(2,1)S(1)}, u32[]{:S(2)}, u32[]{:S(2)}) collective-permute-start(bf16[256,1024]{1,0:T(8,128)(2,1)S(1)} %get-tuple-element.39.own_in_ref), channel_id=1, source_target_pairs={{0,64},{64,0},{1,65},{65,1},{2,66},{66,2},{3,67},{67,3},{4,68},{68... | collective-permute-start | bytes 1572872 | tf_op jit(solution)/shard_map/ppermute | solution.py:346
  133.2 13.7 %all-to-all-done.3 = bf16[64,16,128]{2,1,0:T(8,128)(2,1)S(1)} async-done(((bf16[64,16,128]{2,1,0:T(8,128)(2,1)}), bf16[64,16,128]{2,1,0:T(8,128)(2,1)S(1)}, u32[]{:S(2)}, u32[]{:S(2)}) %all-to-all-start.3) | async-done | bytes 262176 | tf_op jit(solution)/shard_map/all_to_all | solution.py:342
  148.0 3.5 %all-to-all-start.4 = ((bf16[4,64,1024]{2,1,0:T(8,128)(2,1)}), bf16[4,64,1024]{2,1,0:T(8,128)(2,1)S(1)}, u32[]{:S(2)}, u32[]{:S(2)}) async-start(bf16[4,64,1024]{2,1,0:T(8,128)(2,1)} %return_rows.1), calls=%async_computation.4 | async-start | bytes 1048576 | tf_op jit(solution)/shard_map/all_to_all | solution.py:342
  151.5 6.9 %all-to-all-done.4 = bf16[4,64,1024]{2,1,0:T(8,128)(2,1)S(1)} async-done(((bf16[4,64,1024]{2,1,0:T(8,128)(2,1)}), bf16[4,64,1024]{2,1,0:T(8,128)(2,1)S(1)}, u32[]{:S(2)}, u32[]{:S(2)}) %all-to-all-start.4) | async-done | bytes 524320 | tf_op jit(solution)/shard_map/all_to_all | solution.py:342
  158.9 7.1 %collective-permute-start.18 = (bf16[256,256]{1,0:T(8,128)(2,1)S(1)}, bf16[256,256]{1,0:T(8,128)(2,1)S(1)}, u32[]{:S(2)}, u32[]{:S(2)}) collective-permute-start(bf16[256,256]{1,0:T(8,128)(2,1)S(1)} %get-tuple-element.41), channel_id=1, source_target_pairs={{0,64},{64,0},{1,65},{65,1},{2,66},{66,2},{3,67},{67,3},{4,68},{68... | collective-permute-start | bytes 393224 | tf_op jit(solution)/shard_map/ppermute | solution.py:346
  169.3 15.0 %all_to_all.30.packed_ref = bf16[8,64,768]{2,1,0:T(8,128)(2,1)S(1)} all-to-all(bf16[8,64,768]{2,1,0:T(8,128)(2,1)S(1)} %bitcast.18), channel_id=1, replica_groups=mesh['x'=4,'core'=2,'y'=4,'z'=16] {'x','core'}, dimensions={0} | all-to-all | bytes 1572864 | tf_op jit(solution)/shard_map/all_to_all | solution.py:342
  (59 shorter events, 33.8 us)
Async XLA Ops:
  2.1 32.0 %all-to-all-start = ((bf16[16,8,1024]{2,1,0:T(8,128)(2,1)}), bf16[16,8,1024]{2,1,0:T(8,128)(2,1)S(1)}, u32[]{:S(2)}, u32[]{:S(2)}) async-start(bf16[16,8,1024]{2,1,0:T(8,128)(2,1)} %broadcast_in_dim.17), calls=%async_computation | async-start | bytes 524288 | tf_op jit(solution)/shard_map/all_to_all | solution.py:342
  19.1 15.0 %collective-permute-start = (bf16[64,1024]{1,0:T(8,128)(2,1)S(1)}, bf16[64,1024]{1,0:T(8,128)(2,1)S(1)}, u32[]{:S(2)}, u32[]{:S(2)}) collective-permute-start(bf16[64,1024]{1,0:T(8,128)(2,1)S(1)} %get-tuple-element.25), channel_id=1, source_target_pairs={{0,64},{64,128},{128,192},{192,256},{256,320},{320,384},{384,448},... | collective-permute-start | bytes 393224 | tf_op jit(solution)/shard_map/ppermute | solution.py:346
  21.2 16.2 %collective-permute-start.1 = (bf16[64,1024]{1,0:T(8,128)(2,1)S(1)}, bf16[64,1024]{1,0:T(8,128)(2,1)S(1)}, u32[]{:S(2)}, u32[]{:S(2)}) collective-permute-start(bf16[64,1024]{1,0:T(8,128)(2,1)S(1)} %get-tuple-element.26), channel_id=1, source_target_pairs={{0,128},{64,192},{128,256},{192,320},{256,384},{320,448},{384,0},{... | collective-permute-start | bytes 393224 | tf_op jit(solution)/shard_map/ppermute | solution.py:346
  24.3 16.4 %collective-permute-start.2 = (bf16[64,1024]{1,0:T(8,128)(2,1)S(1)}, bf16[64,1024]{1,0:T(8,128)(2,1)S(1)}, u32[]{:S(2)}, u32[]{:S(2)}) collective-permute-start(bf16[64,1024]{1,0:T(8,128)(2,1)S(1)} %get-tuple-element.27), channel_id=1, source_target_pairs={{0,192},{64,256},{128,320},{192,384},{256,448},{320,0},{384,64},{4... | collective-permute-start | bytes 393224 | tf_op jit(solution)/shard_map/ppermute | solution.py:346
  27.8 16.5 %collective-permute-start.3 = (bf16[64,1024]{1,0:T(8,128)(2,1)S(1)}, bf16[64,1024]{1,0:T(8,128)(2,1)S(1)}, u32[]{:S(2)}, u32[]{:S(2)}) collective-permute-start(bf16[64,1024]{1,0:T(8,128)(2,1)S(1)} %get-tuple-element.28), channel_id=1, source_target_pairs={{0,256},{64,320},{128,384},{192,448},{256,0},{320,64},{384,128},{4... | collective-permute-start | bytes 393224 | tf_op jit(solution)/shard_map/ppermute | solution.py:346
  30.2 16.7 %collective-permute-start.4 = (bf16[64,1024]{1,0:T(8,128)(2,1)S(1)}, bf16[64,1024]{1,0:T(8,128)(2,1)S(1)}, u32[]{:S(2)}, u32[]{:S(2)}) collective-permute-start(bf16[64,1024]{1,0:T(8,128)(2,1)S(1)} %get-tuple-element.29), channel_id=1, source_target_pairs={{0,320},{64,384},{128,448},{192,0},{256,64},{320,128},{384,192},{4... | collective-permute-start | bytes 393224 | tf_op jit(solution)/shard_map/ppermute | solution.py:346
  34.2 23.1 %collective-permute-start.7 = (bf16[128,1024]{1,0:T(8,128)(2,1)S(1)}, bf16[128,1024]{1,0:T(8,128)(2,1)S(1)}, u32[]{:S(2)}, u32[]{:S(2)}) collective-permute-start(bf16[128,1024]{1,0:T(8,128)(2,1)S(1)} %bitcast.20), channel_id=1, source_target_pairs={{0,16},{16,32},{32,48},{48,0},{1,17},{17,33},{33,49},{49,1},{2,18}... | collective-permute-start | bytes 786440 | tf_op jit(solution)/shard_map/ppermute | solution.py:346
  37.4 19.9 %collective-permute-start.8 = (bf16[128,1024]{1,0:T(8,128)(2,1)S(1)}, bf16[128,1024]{1,0:T(8,128)(2,1)S(1)}, u32[]{:S(2)}, u32[]{:S(2)}) collective-permute-start(bf16[128,1024]{1,0:T(8,128)(2,1)S(1)} %bitcast.21), channel_id=1, source_target_pairs={{0,48},{16,0},{32,16},{48,32},{1,49},{17,1},{33,17},{49,33},{2,50}... | collective-permute-start | bytes 786440 | tf_op jit(solution)/shard_map/ppermute | solution.py:346
  40.8 16.5 %collective-permute-start.9 = (bf16[128,1024]{1,0:T(8,128)(2,1)S(1)}, bf16[128,1024]{1,0:T(8,128)(2,1)S(1)}, u32[]{:S(2)}, u32[]{:S(2)}) collective-permute-start(bf16[128,1024]{1,0:T(8,128)(2,1)S(1)} %bitcast.22), channel_id=1, source_target_pairs={{0,32},{16,48},{32,0},{48,16},{1,33},{17,49},{33,1},{49,17},{2,34}... | collective-permute-start | bytes 786440 | tf_op jit(solution)/shard_map/ppermute | solution.py:346
  44.3 8.7 %collective-permute-start.5 = (bf16[64,1024]{1,0:T(8,128)(2,1)S(1)}, bf16[64,1024]{1,0:T(8,128)(2,1)S(1)}, u32[]{:S(2)}, u32[]{:S(2)}) collective-permute-start(bf16[64,1024]{1,0:T(8,128)(2,1)S(1)} %get-tuple-element.30), channel_id=1, source_target_pairs={{0,384},{64,448},{128,0},{192,64},{256,128},{320,192},{384,256},{4... | collective-permute-start | bytes 393224 | tf_op jit(solution)/shard_map/ppermute | solution.py:346
  46.9 9.0 %collective-permute-start.6 = (bf16[64,1024]{1,0:T(8,128)(2,1)S(1)}, bf16[64,1024]{1,0:T(8,128)(2,1)S(1)}, u32[]{:S(2)}, u32[]{:S(2)}) collective-permute-start(bf16[64,1024]{1,0:T(8,128)(2,1)S(1)} %get-tuple-element.31), channel_id=1, source_target_pairs={{0,448},{64,0},{128,64},{192,128},{256,192},{320,256},{384,320},{4... | collective-permute-start | bytes 393224 | tf_op jit(solution)/shard_map/ppermute | solution.py:346
  59.1 20.5 %all-to-all-start.1 = ((bf16[8,64,1024]{2,1,0:T(8,128)(2,1)}), bf16[8,64,1024]{2,1,0:T(8,128)(2,1)S(1)}, u32[]{:S(2)}, u32[]{:S(2)}) async-start(bf16[8,64,1024]{2,1,0:T(8,128)(2,1)} %bitcast.5), calls=%async_computation.1 | async-start | bytes 2097152 | tf_op jit(solution)/shard_map/all_to_all | solution.py:342
  64.5 12.5 %collective-permute-start.10 = (bf16[128,2048]{1,0:T(8,128)(2,1)S(1)}, bf16[128,2048]{1,0:T(8,128)(2,1)}, u32[]{:S(2)}, u32[]{:S(2)}) collective-permute-start(bf16[128,2048]{1,0:T(8,128)(2,1)S(1)} %get-tuple-element.35.refs_0_), channel_id=1, source_target_pairs={{0,64},{64,0},{1,65},{65,1},{2,66},{66,2},{3,67},{67,3},{4,68},{68... | collective-permute-start | bytes 1572872 | tf_op jit(solution)/shard_map/ppermute | solution.py:346
  66.5 24.2 %collective-permute-start.11 = (bf16[128,2048]{1,0:T(8,128)(2,1)S(1)}, bf16[128,2048]{1,0:T(8,128)(2,1)}, u32[]{:S(2)}, u32[]{:S(2)}) collective-permute-start(bf16[128,2048]{1,0:T(8,128)(2,1)S(1)} %get-tuple-element.35.refs_0_), channel_id=1, source_target_pairs={{0,128},{128,256},{256,384},{384,0},{1,129},{129,257},{257,385},{3... | collective-permute-start | bytes 1572872 | tf_op jit(solution)/shard_map/ppermute | solution.py:346
  70.2 24.1 %collective-permute-start.12 = (bf16[128,2048]{1,0:T(8,128)(2,1)S(1)}, bf16[128,2048]{1,0:T(8,128)(2,1)}, u32[]{:S(2)}, u32[]{:S(2)}) collective-permute-start(bf16[128,2048]{1,0:T(8,128)(2,1)S(1)} %get-tuple-element.35.refs_0_), channel_id=1, source_target_pairs={{0,384},{128,0},{256,128},{384,256},{1,385},{129,1},{257,129},{385... | collective-permute-start | bytes 1572872 | tf_op jit(solution)/shard_map/ppermute | solution.py:346
  73.3 28.9 %collective-permute-start.13 = (bf16[128,2048]{1,0:T(8,128)(2,1)S(1)}, bf16[128,2048]{1,0:T(8,128)(2,1)}, u32[]{:S(2)}, u32[]{:S(2)}) collective-permute-start(bf16[128,2048]{1,0:T(8,128)(2,1)S(1)} %get-tuple-element.35.refs_0_), channel_id=1, source_target_pairs={{0,256},{128,384},{256,0},{384,128},{1,257},{129,385},{257,1},{385... | collective-permute-start | bytes 1572872 | tf_op jit(solution)/shard_map/ppermute | solution.py:346
  80.7 28.2 %all-to-all-start.2 = ((bf16[64,16,128]{2,1,0:T(8,128)(2,1)}), bf16[64,16,128]{2,1,0:T(8,128)(2,1)S(1)}, u32[]{:S(2)}, u32[]{:S(2)}) async-start(bf16[64,16,128]{2,1,0:T(8,128)(2,1)} %bitcast.6), calls=%async_computation.2 | async-start | bytes 524288 | tf_op jit(solution)/shard_map/all_to_all | solution.py:342
  90.7 14.4 %collective-permute-start.14 = (bf16[128,2048]{1,0:T(8,128)(2,1)}, bf16[128,2048]{1,0:T(8,128)(2,1)S(1)}, u32[]{:S(2)}, u32[]{:S(2)}) collective-permute-start(bf16[128,2048]{1,0:T(8,128)(2,1)} %collective-permute-done.11.refs_1_), channel_id=1, source_target_pairs={{0,64},{64,0},{1,65},{65,1},{2,66},{66,2},{3,67},{67,3},{4,68},{68... | collective-permute-start | bytes 1572872 | tf_op jit(solution)/shard_map/ppermute | solution.py:346
  94.2 10.9 %collective-permute-start.15 = (bf16[128,2048]{1,0:T(8,128)(2,1)}, bf16[128,2048]{1,0:T(8,128)(2,1)S(1)}, u32[]{:S(2)}, u32[]{:S(2)}) collective-permute-start(bf16[128,2048]{1,0:T(8,128)(2,1)} %collective-permute-done.12.refs_2_), channel_id=1, source_target_pairs={{0,64},{64,0},{1,65},{65,1},{2,66},{66,2},{3,67},{67,3},{4,68},{68... | collective-permute-start | bytes 1572872 | tf_op jit(solution)/shard_map/ppermute | solution.py:346
  102.2 4.5 %collective-permute-start.16 = (bf16[128,2048]{1,0:T(8,128)(2,1)}, bf16[128,2048]{1,0:T(8,128)(2,1)S(1)}, u32[]{:S(2)}, u32[]{:S(2)}) collective-permute-start(bf16[128,2048]{1,0:T(8,128)(2,1)} %collective-permute-done.13.refs_3_), channel_id=1, source_target_pairs={{0,64},{64,0},{1,65},{65,1},{2,66},{66,2},{3,67},{67,3},{4,68},{68... | collective-permute-start | bytes 1572872 | tf_op jit(solution)/shard_map/ppermute | solution.py:346
  121.2 25.7 %all-to-all-start.3 = ((bf16[64,16,128]{2,1,0:T(8,128)(2,1)}), bf16[64,16,128]{2,1,0:T(8,128)(2,1)S(1)}, u32[]{:S(2)}, u32[]{:S(2)}) async-start(bf16[64,16,128]{2,1,0:T(8,128)(2,1)} %bitcast.30), calls=%async_computation.3 | async-start | bytes 524288 | tf_op jit(solution)/shard_map/all_to_all | solution.py:342
  129.1 22.4 %collective-permute-start.17 = (bf16[256,1024]{1,0:T(8,128)(2,1)S(1)}, bf16[256,1024]{1,0:T(8,128)(2,1)S(1)}, u32[]{:S(2)}, u32[]{:S(2)}) collective-permute-start(bf16[256,1024]{1,0:T(8,128)(2,1)S(1)} %get-tuple-element.39.own_in_ref), channel_id=1, source_target_pairs={{0,64},{64,0},{1,65},{65,1},{2,66},{66,2},{3,67},{67,3},{4,68},{68... | collective-permute-start | bytes 1572872 | tf_op jit(solution)/shard_map/ppermute | solution.py:346
  148.0 10.4 %all-to-all-start.4 = ((bf16[4,64,1024]{2,1,0:T(8,128)(2,1)}), bf16[4,64,1024]{2,1,0:T(8,128)(2,1)S(1)}, u32[]{:S(2)}, u32[]{:S(2)}) async-start(bf16[4,64,1024]{2,1,0:T(8,128)(2,1)} %return_rows.1), calls=%async_computation.4 | async-start | bytes 1048576 | tf_op jit(solution)/shard_map/all_to_all | solution.py:342
  158.9 8.1 %collective-permute-start.18 = (bf16[256,256]{1,0:T(8,128)(2,1)S(1)}, bf16[256,256]{1,0:T(8,128)(2,1)S(1)}, u32[]{:S(2)}, u32[]{:S(2)}) collective-permute-start(bf16[256,256]{1,0:T(8,128)(2,1)S(1)} %get-tuple-element.41), channel_id=1, source_target_pairs={{0,64},{64,0},{1,65},{65,1},{2,66},{66,2},{3,67},{67,3},{4,68},{68... | collective-permute-start | bytes 393224 | tf_op jit(solution)/shard_map/ppermute | solution.py:346
  (11 other events, 101.5 us)
